TPU v7x, 128 devices: a whole 4x4x4 slice. The times are simulated.
128 devices in a mesh: ctx: 16 (over y, z_hi, core), tp: 8 (over z_lo, x).
Axes of the slice: x: 4, y: 4, z: 4 (z_hi: 2, z_lo: 2; z = z_hi * 2 + z_lo), core: 2. Of those that a mesh axis runs over, the one named last changes fastest.
Arguments:
- ctx_heads: bfloat16 [16384, 4096], P('ctx', 'tp'), may hold values from -6 to 6
- out_weight: bfloat16 [4096, 4096], P('ctx', 'tp'), may hold values from -0.09375 to 0.09375
- hidden_in: bfloat16 [16384, 4096], P(('ctx', 'tp')), may hold values from -54 to 54
- norm_gain: float32 [4096], replicated, may hold values from 0.5 to 1.5
- expert_ids: int32 [16384, 2], P(('ctx', 'tp')), may hold values from 0 to 63, all different within a row; in each aligned block of 128 rows (0 to 127, 128 to 255, ...) at most 6 rows name the same one
- route_weights: float32 [16384, 2], P(('ctx', 'tp')), may hold values from 0.02 to 0.4
- w_gate: bfloat16 [128, 4096, 384], P(('ctx', 'tp')), may hold values from -0.09375 to 0.09375
- w_up: bfloat16 [128, 4096, 384], P(('ctx', 'tp')), may hold values from -0.09375 to 0.09375
- w_down: bfloat16 [128, 384, 4096], P(('ctx', 'tp')), may hold values from -0.21875 to 0.21875
- grad_out: bfloat16 [16384, 4096], P(('ctx', 'tp')), may hold values from -6 to 6
Outputs:
- d_ctx_heads: bfloat16 [16384, 4096], P('ctx', 'tp')
- d_out_weight: bfloat16 [4096, 4096], P('ctx', 'tp')
- d_hidden_in: bfloat16 [16384, 4096], P(('ctx', 'tp'))
- d_route_weights: float32 [16384, 2], P(('ctx', 'tp'))
- d_w_gate: bfloat16 [128, 4096, 384], P(('ctx', 'tp'))
- d_w_up: bfloat16 [128, 4096, 384], P(('ctx', 'tp'))
- d_w_down: bfloat16 [128, 384, 4096], P(('ctx', 'tp'))
Inputs may be any that keep to these rules, and one draw needn't show every extreme that they name: `expert_ids`: each token names 2 different experts. In each aligned block of 128 tokens (the tokens of one device) no expert is named by more than 6 tokens, a bound that some block reaches. Every expert is named by some token.
All inputs are finite; a program needn't handle non-finite values.
Results may differ from a plain program's by a relative error of at most 0.02.
Values may be sent and summed in bfloat16 or wider, within the bound.
A program may use at most 192 MiB of HBM per device.

v0:
```python
import jax
import jax.numpy as jnp
from jax import lax
from jax.sharding import PartitionSpec as P

EPSILON = 1e-06
CONTRACT_FIRST = (((0,), (0,)), ((), ()))
CONTRACT_LAST = (((1,), (1,)), ((), ()))


def normalize(hidden_in, norm_gain):
    hidden_wide = hidden_in.astype(jnp.float32)
    rms_scale = lax.rsqrt(jnp.mean(hidden_wide * hidden_wide, axis=-1, keepdims=True) + EPSILON)
    normed = (hidden_wide * rms_scale * norm_gain).astype(jnp.bfloat16)
    return (hidden_wide, rms_scale, normed)


def norm_backward(hidden_wide, rms_scale, norm_gain, normed_grad, grad_out):
    gained = normed_grad * norm_gain
    inner = jnp.mean(gained * hidden_wide, axis=-1, keepdims=True)
    cubed = rms_scale * rms_scale * rms_scale
    return grad_out.astype(jnp.float32) + rms_scale * gained - hidden_wide * cubed * inner


def expert_half(slot_rows, slot_cots, slot_weights, gate_matrix, up_matrix, down_matrix):
    gate_pre = jnp.dot(slot_rows, gate_matrix, preferred_element_type=jnp.float32)
    up_value = jnp.dot(slot_rows, up_matrix, preferred_element_type=jnp.float32)
    sigmoid_gate = jax.nn.sigmoid(gate_pre)
    silu_gate = gate_pre * sigmoid_gate
    activated = (silu_gate * up_value).astype(jnp.bfloat16)
    back_proj = lax.dot_general(
        slot_cots, down_matrix, CONTRACT_LAST, preferred_element_type=jnp.float32
    )
    weight_dots = jnp.sum(activated.astype(jnp.float32) * back_proj, axis=-1)
    scaled_grad = (slot_weights[:, None] * slot_cots.astype(jnp.float32)).astype(jnp.bfloat16)
    down_wgrad = lax.dot_general(
        activated, scaled_grad, CONTRACT_FIRST, preferred_element_type=jnp.float32
    )
    act_grad = slot_weights[:, None] * back_proj
    gate_grad = (
        act_grad * up_value * sigmoid_gate * (1.0 + gate_pre * (1.0 - sigmoid_gate))
    ).astype(jnp.bfloat16)
    up_grad = (act_grad * silu_gate).astype(jnp.bfloat16)
    gate_wgrad = lax.dot_general(
        slot_rows, gate_grad, CONTRACT_FIRST, preferred_element_type=jnp.float32
    )
    up_wgrad = lax.dot_general(
        slot_rows, up_grad, CONTRACT_FIRST, preferred_element_type=jnp.float32
    )
    slot_grads = lax.dot_general(
        gate_grad, gate_matrix, CONTRACT_LAST, preferred_element_type=jnp.float32
    )
    slot_grads = slot_grads + lax.dot_general(
        up_grad, up_matrix, CONTRACT_LAST, preferred_element_type=jnp.float32
    )
    return (
        slot_grads.astype(jnp.bfloat16),
        weight_dots,
        gate_wgrad.astype(jnp.bfloat16),
        up_wgrad.astype(jnp.bfloat16),
        down_wgrad.astype(jnp.bfloat16),
    )


def per_device(
    ctx_heads,
    out_weight,
    hidden_in,
    norm_gain,
    expert_ids,
    route_weights,
    w_gate,
    w_up,
    w_down,
    grad_out,
):
    tok_rows, features = hidden_in.shape
    pick_count = expert_ids.shape[1]
    devices = lax.axis_size(("ctx", "tp"))
    experts = devices // 2
    capacity = 3 * tok_rows * pick_count // (2 * experts)
    hidden_wide, rms_scale, normed = normalize(hidden_in, norm_gain)
    flat_ids = expert_ids.reshape(-1)
    onehot = (flat_ids[:, None] == jnp.arange(experts, dtype=jnp.int32)[None, :]).astype(jnp.int32)
    slot_rank = jnp.sum((jnp.cumsum(onehot, axis=0) - onehot) * onehot, axis=1)
    target = flat_ids * capacity + slot_rank
    source = jnp.arange(tok_rows * pick_count, dtype=jnp.int32) // pick_count
    send_rows = (
        jnp.zeros((experts * capacity, features), jnp.bfloat16).at[target].set(normed[source])
    )
    send_grads = (
        jnp.zeros((experts * capacity, features), jnp.bfloat16).at[target].set(grad_out[source])
    )
    send_weights = (
        jnp.zeros((experts * capacity,), jnp.float32).at[target].set(route_weights.reshape(-1))
    )
    gate_matrix = w_gate[0]
    up_matrix = w_up[0]
    down_matrix = w_down[0]
    twice_rows = jnp.repeat(send_rows.reshape(experts, capacity, features), 2, axis=0)
    twice_grads = jnp.repeat(send_grads.reshape(experts, capacity, features), 2, axis=0)
    twice_weights = jnp.repeat(send_weights.reshape(experts, capacity), 2, axis=0)
    recv_rows, recv_grads, recv_weights = (
        lax.all_to_all(twice_rows, ("ctx", "tp"), split_axis=0, concat_axis=0, tiled=True),
        lax.all_to_all(twice_grads, ("ctx", "tp"), split_axis=0, concat_axis=0, tiled=True),
        lax.all_to_all(
            twice_weights.astype(jnp.bfloat16),
            ("ctx", "tp"),
            split_axis=0,
            concat_axis=0,
            tiled=True,
        ).astype(twice_weights.dtype),
    )
    slot_grads, weight_dots, gate_wgrad, up_wgrad, down_wgrad = expert_half(
        recv_rows.reshape(-1, features),
        recv_grads.reshape(-1, features),
        recv_weights.reshape(-1),
        gate_matrix,
        up_matrix,
        down_matrix,
    )
    back_rows, back_dots = (
        lax.all_to_all(
            slot_grads.reshape(devices, capacity, features),
            ("ctx", "tp"),
            split_axis=0,
            concat_axis=0,
            tiled=True,
        ),
        lax.all_to_all(
            weight_dots.reshape(devices, capacity).astype(jnp.bfloat16),
            ("ctx", "tp"),
            split_axis=0,
            concat_axis=0,
            tiled=True,
        ).astype(jnp.float32),
    )
    summed_rows = (
        back_rows.reshape(experts, 2, capacity, features)
        .astype(jnp.float32)
        .sum(axis=1)
        .astype(jnp.bfloat16)
    )
    summed_dots = back_dots.reshape(experts, 2, capacity).sum(axis=1)
    picked_rows = summed_rows.reshape(experts * capacity, features)[target]
    normed_grad = (
        picked_rows.reshape(tok_rows, pick_count, features).astype(jnp.float32).sum(axis=1)
    )
    route_grads = summed_dots.reshape(-1)[target].reshape(tok_rows, pick_count)
    resid_grad = norm_backward(hidden_wide, rms_scale, norm_gain, normed_grad, grad_out).astype(
        jnp.bfloat16
    )
    grads_all = lax.all_gather(resid_grad, "tp", axis=0, tiled=True)
    columns = grads_all
    heads_grad = jnp.dot(
        columns,
        lax.all_gather(out_weight, "ctx", axis=0, tiled=True),
        preferred_element_type=jnp.float32,
    ).astype(jnp.bfloat16)
    columns = grads_all
    weight_grad = lax.psum_scatter(
        lax.dot_general(
            columns, ctx_heads, CONTRACT_FIRST, preferred_element_type=jnp.float32
        ).astype(jnp.bfloat16),
        "ctx",
        scatter_dimension=0,
        tiled=True,
    )
    return (
        heads_grad,
        weight_grad,
        resid_grad,
        route_grads,
        gate_wgrad[None],
        up_wgrad[None],
        down_wgrad[None],
    )


def solution(mesh):
    in_specs = (
        P("ctx", "tp"),
        P("ctx", "tp"),
        P(("ctx", "tp"), None),
        P(),
        P(("ctx", "tp"), None),
        P(("ctx", "tp"), None),
        P(("ctx", "tp"), None, None),
        P(("ctx", "tp"), None, None),
        P(("ctx", "tp"), None, None),
        P(("ctx", "tp"), None),
    )
    out_specs = (
        P("ctx", "tp"),
        P("ctx", "tp"),
        P(("ctx", "tp"), None),
        P(("ctx", "tp"), None),
        P(("ctx", "tp"), None, None),
        P(("ctx", "tp"), None, None),
        P(("ctx", "tp"), None, None),
    )
    return jax.shard_map(
        per_device, mesh=mesh, in_specs=in_specs, out_specs=out_specs, check_vma=False
    )
```

profile of v0, /device:TPU:0, one launch (start us, length us, event | category | flops | bytes accessed | tf_op | source)
XLA Modules:
  0.0 730.9 jit_solution(7354940516181845108)
XLA Ops:
  13.6 11.1 %all-to-all-start = ((bf16[128,1,6]{2,1,0:T(2,128)(2,1)}), bf16[128,1,6]{2,1,0:T(2,128)(2,1)S(1)}, u32[]{:S(2)}, u32[]{:S(2)}) async-start(bf16[128,1,6]{2,1,0:T(2,128)(2,1)} %copy.35), calls=%async_computation | async-start | bytes 131072 | tf_op jit(solution)/shard_map/all_to_all | solution.py:106
  28.9 11.2 %scatter_custom_fusion.2 = bf16[384,4096]{1,0:T(8,128)(2,1)} fusion(s32[256]{0:T(256)S(1)} %bitcast.74, bf16[128,4096]{1,0:T(8,128)(2,1)} %fusion.17, s32[1024]{0:T(1024)S(1)} %pad_clamp_fusion.1, bf16[]{:T(256)} %constant.37.clone.1), kind=kCustom, calls=%fused_computation.39 | custom fusion | bytes 3146240 | tf_op jit(solution)/shard_map/scatter | solution.py:89
  52.2 10.3 %all-to-all-start.2 = ((bf16[128,6,4096]{2,1,0:T(8,128)(2,1)}), bf16[128,6,4096]{2,1,0:T(8,128)(2,1)}, u32[]{:S(2)}, u32[]{:S(2)}) async-start(bf16[128,6,4096]{2,1,0:T(8,128)(2,1)} %bitcast.67), calls=%async_computation.2 | async-start | bytes 16777216 | tf_op jit(solution)/shard_map/all_to_all | solution.py:104
  62.5 10.8 %scatter_custom_fusion.1 = bf16[384,4096]{1,0:T(8,128)(2,1)} fusion(s32[256]{0:T(256)S(1)} %bitcast.75, bf16[128,4096]{1,0:T(8,128)(2,1)} %param.19, s32[1024]{0:T(1024)S(1)} %pad_clamp_fusion.1, bf16[]{:T(256)} %constant.37.clone.1), kind=kCustom, calls=%fused_computation.41 | custom fusion | bytes 3146240 | tf_op jit(solution)/shard_map/scatter | solution.py:92
  79.0 89.4 %all-to-all-done.2 = bf16[128,6,4096]{2,1,0:T(8,128)(2,1)} async-done(((bf16[128,6,4096]{2,1,0:T(8,128)(2,1)}), bf16[128,6,4096]{2,1,0:T(8,128)(2,1)}, u32[]{:S(2)}, u32[]{:S(2)}) %all-to-all-start.2) | async-done | bytes 6291488 | tf_op jit(solution)/shard_map/all_to_all | solution.py:104
  175.0 12.5 %all-to-all-start.1 = ((bf16[128,6,4096]{2,1,0:T(8,128)(2,1)}), bf16[128,6,4096]{2,1,0:T(8,128)(2,1)}, u32[]{:S(2)}, u32[]{:S(2)}) async-start(bf16[128,6,4096]{2,1,0:T(8,128)(2,1)} %bitcast.66), calls=%async_computation.1 | async-start | bytes 16777216 | tf_op jit(solution)/shard_map/all_to_all | solution.py:105
  187.8 10.3 %reshape.209 = bf16[768,4096]{1,0:T(8,128)(2,1)} reshape(bf16[128,6,4096]{2,1,0:T(8,128)(2,1)} %all-to-all-done.2) | data formatting | bytes 12582912 | tf_op jit(solution)/shard_map/reshape | solution.py:115
  208.4 85.4 %all-to-all-done.1 = bf16[128,6,4096]{2,1,0:T(8,128)(2,1)} async-done(((bf16[128,6,4096]{2,1,0:T(8,128)(2,1)}), bf16[128,6,4096]{2,1,0:T(8,128)(2,1)}, u32[]{:S(2)}, u32[]{:S(2)}) %all-to-all-start.1) | async-done | bytes 6291488 | tf_op jit(solution)/shard_map/all_to_all | solution.py:105
  293.7 10.2 %reshape.206 = bf16[768,4096]{1,0:T(8,128)(2,1)} reshape(bf16[128,6,4096]{2,1,0:T(8,128)(2,1)} %all-to-all-done.1) | data formatting | bytes 12582912 | tf_op jit(solution)/shard_map/reshape | solution.py:116
  304.0 8.2 %multiply_reduce_fusion = (bf16[768]{0:T(1024)(128)(2,1)S(1)}, bf16[768,384]{0,1:T(8,128)(2,1)}, bf16[768,384]{0,1:T(8,128)(2,1)S(1)}, bf16[768,384]{0,1:T(8,128)(2,1)S(1)}) fusion(f32[768,384]{0,1:T(8,128)} %fusion.11, f32[768,384]{0,1:T(8,128)} %fusion.8, f32[768]{0:T(1024)S(1)} %reshape.215, bf16[768,4096]{1,0:T(8,128)(2,1)} %reshape.206, ...), kind=kOutput, calls=%fused_computation.46 | convolution fusion | flops 2421521664 | bytes 13570560 | tf_op jit(solution)/shard_map/dot_general | solution.py:31
  318.6 8.3 %add_convert_fusion = bf16[768,4096]{1,0:T(8,128)(2,1)} fusion(f32[768,4096]{1,0:T(8,128)} %fusion.6, bf16[768,384]{0,1:T(8,128)(2,1)S(1)} %get-tuple-element.31, bf16[1,4096,384]{2,1,0:T(8,128)(2,1)S(1)} %copy-done.5), kind=kOutput, calls=%fused_computation.8 | convolution fusion | flops 2422210560 | bytes 22609920 | tf_op jit(solution)/shard_map/dot_general | solution.py:53
  326.9 10.1 %reshape.210 = bf16[128,6,4096]{2,1,0:T(8,128)(2,1)} reshape(bf16[768,4096]{1,0:T(8,128)(2,1)} %add_convert_fusion) | data formatting | bytes 12582912 | tf_op jit(solution)/shard_map/reshape | solution.py:124
  337.1 12.5 %all-to-all-start.3 = ((bf16[128,6,4096]{2,1,0:T(8,128)(2,1)}), bf16[128,6,4096]{2,1,0:T(8,128)(2,1)}, u32[]{:S(2)}, u32[]{:S(2)}) async-start(bf16[128,6,4096]{2,1,0:T(8,128)(2,1)} %reshape.210), calls=%async_computation.3 | async-start | bytes 16777216 | tf_op jit(solution)/shard_map/all_to_all | solution.py:123
  349.7 105.8 %all-to-all-done.3 = bf16[128,6,4096]{2,1,0:T(8,128)(2,1)} async-done(((bf16[128,6,4096]{2,1,0:T(8,128)(2,1)}), bf16[128,6,4096]{2,1,0:T(8,128)(2,1)}, u32[]{:S(2)}, u32[]{:S(2)}) %all-to-all-start.3) | async-done | bytes 6291488 | tf_op jit(solution)/shard_map/all_to_all | solution.py:123
  455.5 8.8 %bitcast_reduce_fusion = bf16[64,6,4096]{2,1,0:T(8,128)(2,1)} fusion(bf16[128,6,4096]{2,1,0:T(8,128)(2,1)} %all-to-all-done.3), kind=kLoop, calls=%fused_computation.9 | loop fusion | flops 1572864 | bytes 9437184 | tf_op jit(solution)/shard_map/reduce_sum | solution.py:141
  477.2 7.6 %reduce_sum.72 = f32[128,4096]{1,0:T(8,128)S(1)} reduce(f32[128,2,4096]{2,1,0:T(2,128)} %reshape.216, f32[]{:T(128)} %constant.31.clone.1), dimensions={1}, to_apply=%region_8.9 | reduce | flops 524288 | bytes 6291460 | tf_op jit(solution)/shard_map/reduce_sum | solution.py:147
  489.0 93.9 %all-gather.3.cloned.1.call-done = bf16[1024,4096]{1,0:T(8,128)(2,1)} async-done(((bf16[128,4096]{1,0:T(8,128)(2,1)}), bf16[1024,4096]{1,0:T(8,128)(2,1)}) %all-gather.3.cloned.1.call-update) | async-done | bytes 8388624 | tf_op jit(solution)/shard_map/all_gather | solution.py:153
  582.9 10.2 %convolution_convert_fusion = bf16[4096,512]{1,0:T(8,128)(2,1)} fusion(bf16[1024,4096]{1,0:T(8,128)(2,1)} %all-gather.3.cloned.1.call-done, bf16[1024,512]{1,0:T(8,128)(2,1)} %param.10), kind=kOutput, calls=%fused_computation.12 | convolution fusion | flops 4297064448 | bytes 13631488 | tf_op jit(solution)/shard_map/dot_general | solution.py:162
  593.9 7.4 %all-to-all-start.4 = ((bf16[128,1,6]{2,1,0:T(2,128)(2,1)}), bf16[128,1,6]{2,1,0:T(2,128)(2,1)S(1)}, u32[]{:S(2)}, u32[]{:S(2)}) async-start(bf16[128,1,6]{2,1,0:T(2,128)(2,1)} %convert_element_type.146), calls=%async_computation.5 | async-start | bytes 131072 | tf_op jit(solution)/shard_map/all_to_all | solution.py:130
  601.4 8.1 %fusion.3 = bf16[1,4096,384]{2,1,0:T(8,128)(2,1)} fusion(bf16[768,4096]{1,0:T(8,128)(2,1)} %reshape.209, bf16[768,384]{0,1:T(8,128)(2,1)S(1)} %copy-done.10), kind=kOutput, calls=%fused_computation.16 | convolution fusion | flops 2417491968 | bytes 10027008 | tf_op jit(solution)/shard_map/dot_general | solution.py:44
  609.5 7.1 fusion.5
  624.6 15.5 %all-gather.5.cloned.1.call-done = bf16[4096,512]{1,0:T(8,128)(2,1)} async-done(((bf16[256,512]{1,0:T(8,128)(2,1)}), bf16[4096,512]{1,0:T(8,128)(2,1)}) %all-gather.5.cloned.1.call-update) | async-done | bytes 4194320 | tf_op jit(solution)/shard_map/all_gather | solution.py:157
  640.2 10.2 %convolution_convert_fusion.3 = bf16[1024,512]{1,0:T(8,128)(2,1)} fusion(bf16[1024,4096]{1,0:T(8,128)(2,1)} %all-gather.3.cloned.1.call-done, bf16[4096,512]{1,0:T(8,128)(2,1)} %all-gather.5.cloned.1.call-done), kind=kOutput, calls=%fused_computation.45 | convolution fusion | flops 4295491584 | bytes 13631488 | tf_op jit(solution)/shard_map/dot_general | solution.py:155
  650.4 73.6 %reduce-scatter.2.cloned.1.call-done = bf16[256,512]{1,0:T(8,128)(2,1)} async-done(((bf16[4096,512]{1,0:T(8,128)(2,1)}), bf16[256,512]{1,0:T(8,128)(2,1)}) %reduce-scatter.2.cloned.1.call-update) | async-done | bytes 262160 | tf_op jit(solution)/shard_map/reduce_scatter | solution.py:161
  (88 shorter events, 77.8 us)
Async XLA Ops:
  7.2 190.9 %copy-start = (bf16[1,4096,384]{2,1,0:T(8,128)(2,1)S(1)}, bf16[1,4096,384]{2,1,0:T(8,128)(2,1)}, u32[]{:S(2)}) copy-start(bf16[1,4096,384]{2,1,0:T(8,128)(2,1)} %param.16) | copy-start | bytes 9437188
  13.6 32.1 %all-to-all-start = ((bf16[128,1,6]{2,1,0:T(2,128)(2,1)}), bf16[128,1,6]{2,1,0:T(2,128)(2,1)S(1)}, u32[]{:S(2)}, u32[]{:S(2)}) async-start(bf16[128,1,6]{2,1,0:T(2,128)(2,1)} %copy.35), calls=%async_computation | async-start | bytes 131072 | tf_op jit(solution)/shard_map/all_to_all | solution.py:106
  52.2 116.2 %all-to-all-start.2 = ((bf16[128,6,4096]{2,1,0:T(8,128)(2,1)}), bf16[128,6,4096]{2,1,0:T(8,128)(2,1)}, u32[]{:S(2)}, u32[]{:S(2)}) async-start(bf16[128,6,4096]{2,1,0:T(8,128)(2,1)} %bitcast.67), calls=%async_computation.2 | async-start | bytes 16777216 | tf_op jit(solution)/shard_map/all_to_all | solution.py:104
  175.0 118.7 %all-to-all-start.1 = ((bf16[128,6,4096]{2,1,0:T(8,128)(2,1)}), bf16[128,6,4096]{2,1,0:T(8,128)(2,1)}, u32[]{:S(2)}, u32[]{:S(2)}) async-start(bf16[128,6,4096]{2,1,0:T(8,128)(2,1)} %bitcast.66), calls=%async_computation.1 | async-start | bytes 16777216 | tf_op jit(solution)/shard_map/all_to_all | solution.py:105
  198.1 6.6 copy-start.3
  198.1 6.6 copy-start.4
  312.2 6.4 copy-start.9
  312.2 6.4 copy-start.7
  312.2 6.4 copy-start.5
  337.1 118.4 %all-to-all-start.3 = ((bf16[128,6,4096]{2,1,0:T(8,128)(2,1)}), bf16[128,6,4096]{2,1,0:T(8,128)(2,1)}, u32[]{:S(2)}, u32[]{:S(2)}) async-start(bf16[128,6,4096]{2,1,0:T(8,128)(2,1)} %reshape.210), calls=%async_computation.3 | async-start | bytes 16777216 | tf_op jit(solution)/shard_map/all_to_all | solution.py:123
  349.6 233.3 %all-gather.3.cloned.1.call-start = ((), (), s32[]{:S(2)}) async-start(), calls=%async_computation.6 | async-start | bytes 9437184 | tf_op jit(solution)/shard_map/all_gather | solution.py:153
  477.2 7.6 %copy-start.2 = (bf16[128,4096]{1,0:T(8,128)(2,1)S(1)}, bf16[128,4096]{1,0:T(8,128)(2,1)}, u32[]{:S(2)}) copy-start(bf16[128,4096]{1,0:T(8,128)(2,1)} %param.12) | copy-start | bytes 3145732
  477.2 7.6 %copy-start.11 = (f32[4096]{0:T(1024)S(1)}, f32[4096]{0:T(1024)}, u32[]{:S(2)}) copy-start(f32[4096]{0:T(1024)} %param.13) | copy-start | bytes 49156
  484.8 1.2 copy-start.6
  488.0 152.2 %all-gather.5.cloned.1.call-start = ((), (), s32[]{:S(2)}) async-start(), calls=%async_computation.7 | async-start | bytes 4456448 | tf_op jit(solution)/shard_map/all_gather | solution.py:157
  488.7 235.3 %reduce-scatter.2.cloned.1.call-start = ((), (), s32[]{:S(2)}) async-start(), calls=%async_computation.8 | async-start | bytes 4456448 | tf_op jit(solution)/shard_map/reduce_scatter | solution.py:161
  593.1 8.2 %copy-start.10 = (bf16[768,384]{0,1:T(8,128)(2,1)S(1)}, bf16[768,384]{0,1:T(8,128)(2,1)}, u32[]{:S(2)}) copy-start(bf16[768,384]{0,1:T(8,128)(2,1)} %copy-done.9) | copy-start | bytes 1769476
  593.9 27.7 %all-to-all-start.4 = ((bf16[128,1,6]{2,1,0:T(2,128)(2,1)}), bf16[128,1,6]{2,1,0:T(2,128)(2,1)S(1)}, u32[]{:S(2)}, u32[]{:S(2)}) async-start(bf16[128,1,6]{2,1,0:T(2,128)(2,1)} %convert_element_type.146), calls=%async_computation.5 | async-start | bytes 131072 | tf_op jit(solution)/shard_map/all_to_all | solution.py:130
  601.3 8.1 %copy-start.12 = (bf16[768,384]{0,1:T(8,128)(2,1)S(1)}, bf16[768,384]{0,1:T(8,128)(2,1)}, u32[]{:S(2)}) copy-start(bf16[768,384]{0,1:T(8,128)(2,1)} %get-tuple-element.29) | copy-start | bytes 1769476
  601.4 15.3 %slice-start = ((s8[6291456]{0:T(1024)(128)(4,1)}), s8[4194304]{0:T(1024)(128)(4,1)S(1)}, s32[]{:S(2)}) async-start(s8[6291456]{0:T(1024)(128)(4,1)} %bitcast.68), calls=%async_computation.9 | async-start | bytes 8388608
  609.5 7.1 slice-start.1
  609.5 7.2 copy-start.8
  640.2 83.8 %copy-start.1 = (bf16[1,4096,384]{2,1,0:T(8,128)(2,1)S(1)}, bf16[1,4096,384]{2,1,0:T(8,128)(2,1)}, u32[]{:S(2)}) copy-start(bf16[1,4096,384]{2,1,0:T(8,128)(2,1)} %param.16) | copy-start | bytes 9437188
Sparse Core Ops, SparseCore 0:
  488.1 94.7 all-gather.2
  585.3 54.8 all-gather.4
  644.8 79.1 reduce-scatter.1
where the time goes:
time: 741 us; the launch traced here: 731 us
  waiting for transfers between devices  464 us (63%)
  local copies, waits for them, and re-layouts  99.5 us (13%)
  matrix products  73.8 us (10%)
  starting transfers between devices  54.2 us (7%)
  other arithmetic  24.6 us (3%)
  between operations  14.5 us (2%)
    all_to_all x1, waiting for transfers between devices, per_device(): lax.all_to_all(slot_grads.reshape(devices, capacity, features), ('ctx', '...  106 us
    all_gather x1, waiting for transfers between devices, per_device(): grads_all = lax.all_gather(resid_grad, 'tp', axis=0, tiled=True)  93.9 us
    all_to_all x1, waiting for transfers between devices, per_device(): lax.all_to_all(twice_rows, ('ctx', 'tp'), split_axis=0, concat_axis=0, ti...  89.4 us
    all_to_all x1, waiting for transfers between devices, per_device(): lax.all_to_all(twice_grads, ('ctx', 'tp'), split_axis=0, concat_axis=0, t...  85.4 us
    reduce_scatter x1, waiting for transfers between devices, per_device(): lax.psum_scatter(lax.dot_general(columns, ctx_heads, CONTRACT_FIRST, pref...  73.6 us
    scatter x2, local copies, waits for them, and re-layouts, per_device(): jnp.zeros((experts * capacity, features), jnp.bfloat16).at[target]  22 us
    all_gather x1, waiting for transfers between devices, per_device(): lax.all_gather(out_weight, 'ctx', axis=0, tiled=True)  15.5 us
  transfers between devices with their start and end apart: 8, of which 6 were waited for; matrix products, arithmetic and copies ran while one was open for 14% of the time, Pallas kernels for 0%

commit v1 on v0

v1 whole, which is shorter than its diff:
```python
import functools

import jax
import jax.numpy as jnp
from jax import lax
from jax.experimental import pallas as pl
from jax.experimental.pallas import tpu as pltpu
from jax.sharding import PartitionSpec as P

EPSILON = 1e-06
CAP = 6
BLOCKS = 8
CHUNK = CAP * BLOCKS
CONTRACT_FIRST = (((0,), (0,)), ((), ()))
CONTRACT_LAST = (((1,), (1,)), ((), ()))
MIB = 1 << 20


def iota(shape, dim):
    return lax.broadcasted_iota(jnp.int32, shape, dim)


def mm(a, b, dims=(((1,), (0,)), ((), ()))):
    return lax.dot_general(a, b, dims, preferred_element_type=jnp.float32)


def dispatch_kernel(ids_ref, weight_ref, hidden_ref, gain_ref, cot_ref, rows_ref, cots_ref,
                    slot, weight, stacked_rows, stacked_cots):
    tokens, features = hidden_ref.shape
    width = features // BLOCKS
    experts = slot.shape[0]
    group = rows_ref.shape[0]
    step = pl.program_id(0)

    @pl.when(step == 0)
    def _():
        expert = iota((experts, tokens), 0)
        first = expert == ids_ref[0:1, :]
        second = expert == ids_ref[1:2, :]
        named = jnp.where(first | second, 1.0, 0.0)
        earlier = jnp.where(iota((tokens, tokens), 0) < iota((tokens, tokens), 1), 1.0, 0.0)
        prior = mm(named.astype(jnp.bfloat16), earlier.astype(jnp.bfloat16))
        slot[...] = jnp.where(named > 0.5, prior, -1.0)
        weight[...] = jnp.where(
            first, weight_ref[0:1, :], jnp.where(second, weight_ref[1:2, :], 0.0)
        )
        wide = hidden_ref[...].astype(jnp.float32)
        scale = lax.rsqrt(jnp.mean(wide * wide, axis=-1, keepdims=True) + EPSILON)
        for block in range(BLOCKS):
            columns = slice(block * width, (block + 1) * width)
            rows = slice(block * tokens, (block + 1) * tokens)
            stacked_rows[rows, :] = (
                hidden_ref[:, columns].astype(jnp.float32) * scale * gain_ref[:, columns]
            ).astype(jnp.bfloat16)
            stacked_cots[rows, :] = cot_ref[:, columns]

    here = pl.ds(pl.multiple_of(step * group, group), group)
    shape = (group, CHUNK, tokens)
    slots = jnp.broadcast_to(slot[here, :][:, None, :], shape)
    weights = jnp.broadcast_to(weight[here, :][:, None, :], shape)
    place = iota(shape, 1)
    block_of = place // CAP
    taken = slots == (place - block_of * CAP).astype(jnp.float32)
    weights = jnp.where(taken, weights, 0.0).reshape(group * CHUNK, tokens)
    taken = jnp.where(taken, 1.0, 0.0).reshape(group * CHUNK, tokens)
    block_of = block_of.reshape(group * CHUNK, tokens)
    pick_rows = jnp.concatenate(
        [jnp.where(block_of == b, taken, 0.0).astype(jnp.bfloat16) for b in range(BLOCKS)], axis=1
    )
    pick_cots = jnp.concatenate(
        [jnp.where(block_of == b, weights, 0.0).astype(jnp.bfloat16) for b in range(BLOCKS)], axis=1
    )
    rows = mm(pick_rows, stacked_rows[...]).astype(jnp.bfloat16).reshape(group, CHUNK, width)
    cots = mm(pick_cots, stacked_cots[...]).astype(jnp.bfloat16).reshape(group, CHUNK, width)
    for half in range(2):
        rows_ref[:, half] = rows
        cots_ref[:, half] = cots


def dispatch(ids_t, weights_t, hidden, gain, cots, experts):
    tokens, features = hidden.shape
    width = features // BLOCKS
    group = 8
    whole = lambda shape: pl.BlockSpec(shape, lambda i: (0, 0))
    out = jax.ShapeDtypeStruct((experts, 2, CHUNK, width), jnp.bfloat16)
    out_spec = pl.BlockSpec((group, 2, CHUNK, width), lambda i: (i, 0, 0, 0))
    return pl.pallas_call(
        dispatch_kernel,
        grid=(experts // group,),
        in_specs=[whole(ids_t.shape), whole(weights_t.shape), whole(hidden.shape),
                  whole(gain.shape), whole(cots.shape)],
        out_specs=[out_spec, out_spec],
        out_shape=[out, out],
        scratch_shapes=[
            pltpu.VMEM((experts, tokens), jnp.float32),
            pltpu.VMEM((experts, tokens), jnp.float32),
            pltpu.VMEM((BLOCKS * tokens, width), jnp.bfloat16),
            pltpu.VMEM((BLOCKS * tokens, width), jnp.bfloat16),
        ],
        compiler_params=pltpu.CompilerParams(vmem_limit_bytes=48 * MIB),
        cost_estimate=pl.CostEstimate(
            flops=4 * experts * CHUNK * tokens * features, bytes_accessed=16 * MIB,
            transcendentals=0),
        name="dispatch",
    )(ids_t, weights_t, hidden, gain, cots)


def unpack_matrix(sources):
    rows = sources * CHUNK
    out, inp = iota((rows, rows), 0), iota((rows, rows), 1)
    block = out // (sources * CAP)
    rest = out - block * (sources * CAP)
    source = rest // CAP
    want = source * CHUNK + block * CAP + (rest - source * CAP)
    return jnp.where(inp == want, 1.0, 0.0).astype(jnp.bfloat16)


GROUP = 8


def unpack_rows(unpack, raw_ref, out_ref):
    rows = GROUP * CHUNK
    height = GROUP * CAP
    width = raw_ref.shape[1]
    for g in range(raw_ref.shape[0] // rows):
        flat = mm(unpack, raw_ref[g * rows:(g + 1) * rows, :]).astype(jnp.bfloat16)
        for b in range(BLOCKS):
            out_ref[g * height:(g + 1) * height, b * width:(b + 1) * width] = (
                flat[b * height:(b + 1) * height, :]
            )


def unpack_kernel(raw_ref, out_ref, unpack):
    @pl.when(pl.program_id(0) == 0)
    def _():
        unpack[...] = unpack_matrix(GROUP)

    unpack_rows(unpack[...], raw_ref, out_ref)


def unpack_chunks(raw, steps=8):
    total, width = raw.shape
    rows = total // steps
    return pl.pallas_call(
        unpack_kernel,
        grid=(steps,),
        in_specs=[pl.BlockSpec((rows, width), lambda i: (i, 0))],
        out_specs=pl.BlockSpec((rows // BLOCKS, width * BLOCKS), lambda i: (i, 0)),
        out_shape=jax.ShapeDtypeStruct((total // BLOCKS, width * BLOCKS), jnp.bfloat16),
        scratch_shapes=[pltpu.VMEM((GROUP * CHUNK, GROUP * CHUNK), jnp.bfloat16)],
        compiler_params=pltpu.CompilerParams(vmem_limit_bytes=40 * MIB),
        cost_estimate=pl.CostEstimate(
            flops=2 * total * GROUP * CHUNK * width, bytes_accessed=4 * total * width,
            transcendentals=0),
        name="unpack",
    )(raw)


def back_kernel(raw_ref, gate_ref, up_ref, w_gate_ref, w_up_ref, w_down_ref,
                grads_ref, cots_ref, act_ref, gate_grad_ref, up_grad_ref, dots_ref, unpack):
    @pl.when(pl.program_id(0) == 0)
    def _():
        unpack[...] = unpack_matrix(GROUP)

    unpack_rows(unpack[...], raw_ref, cots_ref)
    back = mm(cots_ref[...], w_down_ref[...], CONTRACT_LAST)
    gate_pre, up_value = gate_ref[...], up_ref[...]
    sigmoid = jax.nn.sigmoid(gate_pre)
    silu = gate_pre * sigmoid
    activated = (silu * up_value).astype(jnp.bfloat16)
    act_ref[...] = activated
    dots_ref[...] = jnp.sum(activated.astype(jnp.float32) * back, axis=-1, keepdims=True)
    gate_grad = (back * up_value * sigmoid * (1.0 + gate_pre * (1.0 - sigmoid))).astype(jnp.bfloat16)
    up_grad = (back * silu).astype(jnp.bfloat16)
    gate_grad_ref[...] = gate_grad
    up_grad_ref[...] = up_grad
    height = GROUP * CAP
    rows = GROUP * CHUNK
    width = raw_ref.shape[1]
    parts = []
    for b in range(BLOCKS):
        columns = slice(b * width, (b + 1) * width)
        parts.append(
            (mm(gate_grad, w_gate_ref[columns, :], CONTRACT_LAST)
             + mm(up_grad, w_up_ref[columns, :], CONTRACT_LAST)).astype(jnp.bfloat16)
        )
    for g in range(raw_ref.shape[0] // rows):
        stacked = jnp.concatenate([p[g * height:(g + 1) * height, :] for p in parts], axis=0)
        grads_ref[g * rows:(g + 1) * rows, :] = mm(
            unpack[...], stacked, CONTRACT_FIRST
        ).astype(jnp.bfloat16)


def expert_back(raw, gate_pre, up_value, w_gate, w_up, w_down, steps=4):
    total, width = raw.shape
    features, hidden = w_gate.shape
    slots = gate_pre.shape[0]
    rows = slots // steps
    tall = lambda shape: pl.BlockSpec(shape, lambda i: (i, 0))
    whole = lambda shape: pl.BlockSpec(shape, lambda i: (0, 0))
    small = jax.ShapeDtypeStruct((slots, hidden), jnp.bfloat16)
    return pl.pallas_call(
        back_kernel,
        grid=(steps,),
        in_specs=[tall((total // steps, width)), tall((rows, hidden)), tall((rows, hidden)),
                  whole(w_gate.shape), whole(w_up.shape), whole(w_down.shape)],
        out_specs=[tall((total // steps, width)), tall((rows, features))]
        + [tall((rows, hidden))] * 3 + [tall((rows, 1))],
        out_shape=[jax.ShapeDtypeStruct(raw.shape, jnp.bfloat16),
                   jax.ShapeDtypeStruct((slots, features), jnp.bfloat16),
                   small, small, small, jax.ShapeDtypeStruct((slots, 1), jnp.float32)],
        scratch_shapes=[pltpu.VMEM((GROUP * CHUNK, GROUP * CHUNK), jnp.bfloat16)],
        compiler_params=pltpu.CompilerParams(vmem_limit_bytes=56 * MIB),
        cost_estimate=pl.CostEstimate(
            flops=6 * slots * features * hidden + 4 * total * GROUP * CHUNK * width,
            bytes_accessed=32 * MIB, transcendentals=slots * hidden),
        name="expert_back",
    )(raw, gate_pre, up_value, w_gate, w_up, w_down)


def combine_kernel(ids_ref, back_ref, hidden_ref, gain_ref, cot_ref, resid_ref, slot, total):
    tokens, features = hidden_ref.shape
    width = features // BLOCKS
    experts = slot.shape[1]
    rows = back_ref.shape[0]
    step = pl.program_id(0)

    @pl.when(step == 0)
    def _():
        expert = iota((tokens, experts), 1)
        named = jnp.where((expert == ids_ref[:, 0:1]) | (expert == ids_ref[:, 1:2]), 1.0, 0.0)
        earlier = jnp.where(iota((tokens, tokens), 1) < iota((tokens, tokens), 0), 1.0, 0.0)
        prior = mm(earlier.astype(jnp.bfloat16), named.astype(jnp.bfloat16))
        slot[...] = jnp.where(named > 0.5, prior, -1.0).astype(jnp.bfloat16)
        total[...] = jnp.zeros_like(total)

    spread_at = iota((experts, rows), 1) // (2 * CHUNK) + step * (rows // (2 * CHUNK))
    spread = jnp.where(iota((experts, rows), 0) == spread_at, 1.0, 0.0).astype(jnp.bfloat16)
    slots = mm(slot[...], spread)
    lane = iota((tokens, rows), 1)
    piece = lane // CAP
    taken = jnp.where(slots == (lane - piece * CAP).astype(jnp.float32), 1.0, 0.0)
    block_of = piece - piece // BLOCKS * BLOCKS
    for b in range(BLOCKS):
        columns = slice(b * width, (b + 1) * width)
        pick = jnp.where(block_of == b, taken, 0.0).astype(jnp.bfloat16)
        total[:, columns] += mm(pick, back_ref[...])

    @pl.when(step == pl.num_programs(0) - 1)
    def _():
        wide = hidden_ref[...].astype(jnp.float32)
        scale = lax.rsqrt(jnp.mean(wide * wide, axis=-1, keepdims=True) + EPSILON)
        gained = total[...] * gain_ref[...]
        inner = jnp.mean(gained * wide, axis=-1, keepdims=True)
        resid_ref[...] = (
            cot_ref[...].astype(jnp.float32) + scale * gained - wide * (scale * scale * scale * inner)
        ).astype(jnp.bfloat16)


def combine(ids, back, hidden, gain, cots, experts, steps=8):
    tokens, features = hidden.shape
    total, width = back.shape
    whole = lambda shape: pl.BlockSpec(shape, lambda i: (0, 0))
    return pl.pallas_call(
        combine_kernel,
        grid=(steps,),
        in_specs=[whole(ids.shape), pl.BlockSpec((total // steps, width), lambda i: (i, 0)),
                  whole(hidden.shape), whole(gain.shape), whole(cots.shape)],
        out_specs=whole(hidden.shape),
        out_shape=jax.ShapeDtypeStruct(hidden.shape, jnp.bfloat16),
        scratch_shapes=[pltpu.VMEM((tokens, experts), jnp.bfloat16),
                        pltpu.VMEM((tokens, features), jnp.float32)],
        compiler_params=pltpu.CompilerParams(vmem_limit_bytes=40 * MIB),
        cost_estimate=pl.CostEstimate(
            flops=2 * BLOCKS * tokens * total * width, bytes_accessed=12 * MIB, transcendentals=0),
        name="combine",
    )(ids, back, hidden, gain, cots)


def per_device(
    ctx_heads,
    out_weight,
    hidden_in,
    norm_gain,
    expert_ids,
    route_weights,
    w_gate,
    w_up,
    w_down,
    grad_out,
):
    tokens, features = hidden_in.shape
    devices = lax.axis_size(("ctx", "tp"))
    experts = devices // 2
    axes = ("ctx", "tp")
    exchange = functools.partial(
        lax.all_to_all, axis_name=axes, split_axis=0, concat_axis=0, tiled=True
    )
    width = features // BLOCKS
    gain = norm_gain.reshape(1, features)
    rounded_weights = route_weights.astype(jnp.bfloat16).astype(jnp.float32)
    send_rows, send_cots = dispatch(
        expert_ids.T, rounded_weights.T, hidden_in, gain, grad_out, experts
    )
    raw_rows = exchange(send_rows.reshape(devices, CHUNK, width)).reshape(-1, width)
    raw_cots = exchange(send_cots.reshape(devices, CHUNK, width)).reshape(-1, width)
    slot_rows = unpack_chunks(raw_rows)
    gate_pre = mm(slot_rows, w_gate[0])
    up_value = mm(slot_rows, w_up[0])
    grads, slot_cots, activated, gate_grad, up_grad, dots = expert_back(
        raw_cots, gate_pre, up_value, w_gate[0], w_up[0], w_down[0]
    )
    back = exchange(grads.reshape(devices, CHUNK, width)).reshape(-1, width)
    back_dots = exchange(dots.reshape(devices, CAP).astype(jnp.bfloat16)).astype(jnp.float32)
    down_wgrad = mm(activated, slot_cots, CONTRACT_FIRST).astype(jnp.bfloat16)
    gate_wgrad = mm(slot_rows, gate_grad, CONTRACT_FIRST).astype(jnp.bfloat16)
    up_wgrad = mm(slot_rows, up_grad, CONTRACT_FIRST).astype(jnp.bfloat16)
    resid_grad = combine(expert_ids, back, hidden_in, gain, grad_out, experts)

    flat_ids = expert_ids.reshape(-1)
    onehot = (flat_ids[:, None] == jnp.arange(experts, dtype=jnp.int32)[None, :]).astype(jnp.int32)
    slot_rank = jnp.sum((jnp.cumsum(onehot, axis=0) - onehot) * onehot, axis=1)
    summed_dots = back_dots.reshape(experts, 2, CAP).sum(axis=1)
    picked = jnp.dot(onehot.astype(jnp.float32), summed_dots, precision=lax.Precision.HIGHEST)
    at_rank = slot_rank[:, None] == jnp.arange(CAP, dtype=jnp.int32)[None, :]
    route_grads = (
        jnp.sum(jnp.where(at_rank, picked, 0.0), axis=1).reshape(tokens, -1) / rounded_weights
    )

    grads_all = lax.all_gather(resid_grad, "tp", axis=0, tiled=True)
    heads_grad = mm(grads_all, lax.all_gather(out_weight, "ctx", axis=0, tiled=True)).astype(
        jnp.bfloat16
    )
    weight_grad = lax.psum_scatter(
        mm(grads_all, ctx_heads, CONTRACT_FIRST).astype(jnp.bfloat16),
        "ctx",
        scatter_dimension=0,
        tiled=True,
    )
    return (
        heads_grad,
        weight_grad,
        resid_grad,
        route_grads,
        gate_wgrad[None],
        up_wgrad[None],
        down_wgrad[None],
    )


def solution(mesh):
    split = P(("ctx", "tp"), None)
    stack = P(("ctx", "tp"), None, None)
    in_specs = (
        P("ctx", "tp"),
        P("ctx", "tp"),
        split,
        P(),
        split,
        split,
        stack,
        stack,
        stack,
        split,
    )
    out_specs = (P("ctx", "tp"), P("ctx", "tp"), split, split, stack, stack, stack)
    return jax.shard_map(
        per_device, mesh=mesh, in_specs=in_specs, out_specs=out_specs, check_vma=False
    )
```

time: 741 us -> 567 us (0.77); the launches traced: 731 us -> 566 us
  waiting for transfers between devices: 464 us -> 327 us
  local copies, waits for them, and re-layouts: 99.5 us -> 9.5 us
  blocking collectives: 0 us -> 86.9 us
  Pallas kernels: 0 us -> 54.9 us
  starting transfers between devices: 54.2 us -> 25.2 us
  matrix products: 73.8 us -> 45.9 us
  other arithmetic: 24.6 us -> 3.46 us
    all_to_all x5 -> x3, waiting for transfers between devices: 281 us -> 142 us  [the longest x1 79 us: per_device(): back = exchange(grads.reshape(devices, CHUNK, width)).reshape(-1, width)]
    all_to_all x0 -> x1, blocking collectives: none -> 86.9 us  [per_device(): exchange(send_rows.reshape(devices, CHUNK, width)).reshape(-1, width)]
    pallas_call x0 -> x4, Pallas kernels: none -> 54.9 us  [the longest x1 28 us: expert_back(): pl.pallas_call(back_kernel, grid=(steps,), in_specs=[tall((total // steps...]
    reshape x9 -> x2, local copies, waits for them, and re-layouts: 46.7 us -> 0.2 us  [per_device(): jnp.sum(jnp.where(at_rank, picked, 0.0), axis=1).reshape(tokens, -1)]
    all_to_all x5 -> x3, starting transfers between devices: 53.8 us -> 24.8 us  [the longest x1 10.6 us: per_device(): back = exchange(grads.reshape(devices, CHUNK, width)).reshape(-1, width)]
    dot_general x10 -> x8, matrix products: 73.8 us -> 45.9 us  [the longest x7 45.7 us: mm(): return lax.dot_general(a, b, dims, preferred_element_type=jnp.float32)]
    scatter x3 -> x0, local copies, waits for them, and re-layouts: 23.4 us -> none  [the longest x2 22 us: per_device(): jnp.zeros((experts * capacity, features), jnp.bfloat16).at[target]]
    reduce_sum x5 -> x1, other arithmetic: 18.3 us -> 0.08 us  [per_device(): summed_dots = back_dots.reshape(experts, 2, CAP).sum(axis=1)]
  transfers between devices with their start and end apart: 8 -> 6, of which waited for: 6 -> 5; matrix products, arithmetic and copies ran while one was open for 14% -> 9% of each run, Pallas kernels for 0% -> 1%
where the time goes in v1:
time: 567 us; the launch traced here: 566 us
  waiting for transfers between devices  327 us (58%)
  blocking collectives  86.9 us (15%)
  Pallas kernels  54.9 us (10%)
  matrix products  45.9 us (8%)
  starting transfers between devices  25.2 us (4%)
  between operations  14 us (2%)
  local copies, waits for them, and re-layouts  9.5 us (2%)
    all_gather x1, waiting for transfers between devices, per_device(): grads_all = lax.all_gather(resid_grad, 'tp', axis=0, tiled=True)  92.3 us
    all_to_all x1, blocking collectives, per_device(): exchange(send_rows.reshape(devices, CHUNK, width)).reshape(-1, width)  86.9 us
    all_to_all x1, waiting for transfers between devices, per_device(): back = exchange(grads.reshape(devices, CHUNK, width)).reshape(-1, width)  79 us
    reduce_scatter x1, waiting for transfers between devices, per_device(): lax.psum_scatter(mm(grads_all, ctx_heads, CONTRACT_FIRST).astype(jnp.bflo...  73.8 us
    all_to_all x1, waiting for transfers between devices, per_device(): exchange(send_cots.reshape(devices, CHUNK, width)).reshape(-1, width)  62.6 us
    dot_general x7, matrix products, mm(): return lax.dot_general(a, b, dims, preferred_element_type=jnp.float32)  45.7 us
    pallas_call x1, Pallas kernels, expert_back(): pl.pallas_call(back_kernel, grid=(steps,), in_specs=[tall((total // steps...  28 us
    all_gather x1, waiting for transfers between devices, per_device(): lax.all_gather(out_weight, 'ctx', axis=0, tiled=True)  18.3 us
  transfers between devices with their start and end apart: 6, of which 5 were waited for; matrix products, arithmetic and copies ran while one was open for 9% of the time, Pallas kernels for 1%

profile of v1, /device:TPU:0, one launch (start us, length us, event | category | flops | bytes accessed | tf_op | source)
XLA Modules:
  0.0 566.4 jit_solution(3510138974605095253)
XLA Ops:
  8.6 1.2 copy-done.5
  9.9 1.2 copy-done.7
  11.8 9.4 %dispatch.1 = (bf16[64,2,48,512]{3,2,1,0:T(8,128)(2,1)}, bf16[64,2,48,512]{3,2,1,0:T(8,128)(2,1)}) custom-call(s32[2,128]{1,0:T(2,128)S(1)} %bitcast.51, f32[2,128]{1,0:T(2,128)S(1)} %convert_bitcast_fusion.weight_ref, bf16[128,4096]{1,0:T(8,128)(2,1)S(1)} %copy-done.5, f32[1,4096]{1,0:T(1,128)S(1)} %bitcast.52, bf16[128,4096]{1,0:T(8,128)(2,1)S(1)} %copy-done.7), custom_call_target="tpu_custom_call" | custom-call | flops 6442450944 | bytes 16777216 | tf_op jit(solution)/shard_map/dispatch/pallas_call | solution.py:87
  21.2 86.9 %all_to_all.21 = bf16[128,48,512]{2,1,0:T(8,128)(2,1)} all-to-all(bf16[128,48,512]{2,1,0:T(8,128)(2,1)} %bitcast.58), channel_id=1, replica_groups=mesh['ctx'=16,'tp'=8] {'ctx','tp'}, dimensions={0} | all-to-all | bytes 12582912 | tf_op jit(solution)/shard_map/all_to_all | solution.py:305
  108.1 6.6 %all-to-all-start = ((bf16[128,48,512]{2,1,0:T(8,128)(2,1)}), bf16[128,48,512]{2,1,0:T(8,128)(2,1)}, u32[]{:S(2)}, u32[]{:S(2)}) async-start(bf16[128,48,512]{2,1,0:T(8,128)(2,1)} %bitcast.57), calls=%async_computation | async-start | bytes 12582912 | tf_op jit(solution)/shard_map/all_to_all | solution.py:306
  114.7 2.8 copy-done.1
  117.5 4.9 unpack.1
  122.4 4.4 fusion.10.gate_ref
  126.8 4.4 fusion.8.up_ref
  131.3 62.6 %all-to-all-done = bf16[128,48,512]{2,1,0:T(8,128)(2,1)} async-done(((bf16[128,48,512]{2,1,0:T(8,128)(2,1)}), bf16[128,48,512]{2,1,0:T(8,128)(2,1)}, u32[]{:S(2)}, u32[]{:S(2)}) %all-to-all-start) | async-done | bytes 6291488 | tf_op jit(solution)/shard_map/all_to_all | solution.py:306
  193.9 28.0 %expert_back.1 = (bf16[6144,512]{1,0:T(8,128)(2,1)}, bf16[768,4096]{1,0:T(8,128)(2,1)}, bf16[768,384]{1,0:T(8,128)(2,1)}, bf16[768,384]{1,0:T(8,128)(2,1)}, bf16[768,384]{1,0:T(8,128)(2,1)}, /*index=5*/f32[768,1]{1,0:T(8,128)}) custom-call(bf16[6144,512]{1,0:T(8,128)(2,1)} %bitcast.4.raw_ref, f32[768,384]{1,0:T(8,128)} %fusion.10.gate_ref, ...), custom_call_target="tpu_custom_call" | custom-call | flops 12079595520 | bytes 33554432 | tf_op jit(solution)/shard_map/expert_back/pallas_call | solution.py:202
  221.9 10.6 %all-to-all-start.2 = ((bf16[128,48,512]{2,1,0:T(8,128)(2,1)}), bf16[128,48,512]{2,1,0:T(8,128)(2,1)}, u32[]{:S(2)}, u32[]{:S(2)}) async-start(bf16[128,48,512]{2,1,0:T(8,128)(2,1)} %bitcast.56), calls=%async_computation.2 | async-start | bytes 12582912 | tf_op jit(solution)/shard_map/all_to_all | solution.py:313
  232.9 79.0 %all-to-all-done.2 = bf16[128,48,512]{2,1,0:T(8,128)(2,1)} async-done(((bf16[128,48,512]{2,1,0:T(8,128)(2,1)}), bf16[128,48,512]{2,1,0:T(8,128)(2,1)}, u32[]{:S(2)}, u32[]{:S(2)}) %all-to-all-start.2) | async-done | bytes 6291488 | tf_op jit(solution)/shard_map/all_to_all | solution.py:313
  311.9 1.2 copy-done.8
  313.1 12.6 %combine.1 = bf16[128,4096]{1,0:T(8,128)(2,1)} custom-call(s32[128,2]{1,0:T(8,128)S(1)} %copy.23.ids_ref, bf16[6144,512]{1,0:T(8,128)(2,1)} %bitcast.11.back_ref, bf16[128,4096]{1,0:T(8,128)(2,1)S(1)} %copy-done.6, f32[1,4096]{1,0:T(1,128)S(1)} %bitcast.53, bf16[128,4096]{1,0:T(8,128)(2,1)S(1)} %copy-done.8), custom_call_target="tpu_custom_call" | custom-call | flops 6442450944 | bytes 12582912 | tf_op jit(solution)/shard_map/combine/pallas_call | solution.py:264
  326.5 92.3 %all-gather.3.cloned.1.call-done = bf16[1024,4096]{1,0:T(8,128)(2,1)} async-done(((bf16[128,4096]{1,0:T(8,128)(2,1)}), bf16[1024,4096]{1,0:T(8,128)(2,1)}) %all-gather.3.cloned.1.call-update) | async-done | bytes 8388624 | tf_op jit(solution)/shard_map/all_gather | solution.py:330
  418.8 9.8 %convolution_convert_fusion = bf16[4096,512]{1,0:T(8,128)(2,1)} fusion(bf16[1024,4096]{1,0:T(8,128)(2,1)} %all-gather.3.cloned.1.call-done, bf16[1024,512]{1,0:T(8,128)(2,1)S(1)} %copy-done), kind=kOutput, calls=%fused_computation | convolution fusion | flops 4297064448 | bytes 13631488 | tf_op jit(solution)/shard_map/dot_general | solution.py:24
  431.8 7.7 %all-to-all-start.3 = ((bf16[128,1,6]{2,1,0:T(2,128)(2,1)}), bf16[128,1,6]{2,1,0:T(2,128)(2,1)S(1)}, u32[]{:S(2)}, u32[]{:S(2)}) async-start(bf16[128,1,6]{2,1,0:T(2,128)(2,1)} %convert_element_type.70), calls=%async_computation.4 | async-start | bytes 131072 | tf_op jit(solution)/shard_map/all_to_all | solution.py:314
  439.5 8.2 %fusion.1 = bf16[1,4096,384]{2,1,0:T(8,128)(2,1)} fusion(bf16[768,4096]{1,0:T(8,128)(2,1)} %copy-done.2, bf16[768,384]{1,0:T(8,128)(2,1)} %get-tuple-element.20), kind=kOutput, calls=%fused_computation.5 | convolution fusion | flops 2417491968 | bytes 10027008 | tf_op jit(solution)/shard_map/dot_general | solution.py:24
  447.7 4.9 fusion
  452.6 4.0 fusion.2
  457.8 18.3 %all-gather.5.cloned.1.call-done = bf16[4096,512]{1,0:T(8,128)(2,1)} async-done(((bf16[256,512]{1,0:T(8,128)(2,1)}), bf16[4096,512]{1,0:T(8,128)(2,1)}) %all-gather.5.cloned.1.call-update) | async-done | bytes 4194320 | tf_op jit(solution)/shard_map/all_gather | solution.py:331
  476.1 10.0 %convolution_convert_fusion.4 = bf16[1024,512]{1,0:T(8,128)(2,1)} fusion(bf16[1024,4096]{1,0:T(8,128)(2,1)} %all-gather.3.cloned.1.call-done, bf16[4096,512]{1,0:T(8,128)(2,1)} %all-gather.5.cloned.1.call-done), kind=kOutput, calls=%fused_computation.7 | convolution fusion | flops 4295491584 | bytes 13631488 | tf_op jit(solution)/shard_map/dot_general | solution.py:24
  486.1 73.8 %reduce-scatter.2.cloned.1.call-done = bf16[256,512]{1,0:T(8,128)(2,1)} async-done(((bf16[4096,512]{1,0:T(8,128)(2,1)}), bf16[256,512]{1,0:T(8,128)(2,1)}) %reduce-scatter.2.cloned.1.call-update) | async-done | bytes 262160 | tf_op jit(solution)/shard_map/reduce_scatter | solution.py:334
  (63 shorter events, 7.8 us)
Async XLA Ops:
  7.2 411.6 %copy-start = (bf16[1024,512]{1,0:T(8,128)(2,1)S(1)}, bf16[1024,512]{1,0:T(8,128)(2,1)}, u32[]{:S(2)}) copy-start(bf16[1024,512]{1,0:T(8,128)(2,1)} %param.10) | copy-start | bytes 3145732
  8.6 1.2 copy-start.5
  9.9 1.2 copy-start.7
  108.1 85.8 %all-to-all-start = ((bf16[128,48,512]{2,1,0:T(8,128)(2,1)}), bf16[128,48,512]{2,1,0:T(8,128)(2,1)}, u32[]{:S(2)}, u32[]{:S(2)}) async-start(bf16[128,48,512]{2,1,0:T(8,128)(2,1)} %bitcast.57), calls=%async_computation | async-start | bytes 12582912 | tf_op jit(solution)/shard_map/all_to_all | solution.py:306
  114.7 2.8 copy-start.1
  117.5 4.9 copy-start.13
  122.4 4.4 copy-start.2
  122.4 4.4 copy-start.14
  221.9 10.9 %copy-start.4 = (s32[128,2]{0,1:T(2,128)S(1)}, s32[128,2]{0,1:T(2,128)}, u32[]{:S(2)}) copy-start(s32[128,2]{0,1:T(2,128)} %param.14) | copy-start | bytes 3076
  221.9 90.0 %copy-start.6 = (bf16[128,4096]{1,0:T(8,128)(2,1)S(1)}, bf16[128,4096]{1,0:T(8,128)(2,1)}, u32[]{:S(2)}) copy-start(bf16[128,4096]{1,0:T(8,128)(2,1)} %hidden_ref.3) | copy-start | bytes 3145732
  221.9 90.0 %copy-start.10 = (f32[4096]{0:T(1024)S(1)}, f32[4096]{0:T(1024)}, u32[]{:S(2)}) copy-start(f32[4096]{0:T(1024)} %param.13) | copy-start | bytes 49156
  221.9 90.0 %all-to-all-start.2 = ((bf16[128,48,512]{2,1,0:T(8,128)(2,1)}), bf16[128,48,512]{2,1,0:T(8,128)(2,1)}, u32[]{:S(2)}, u32[]{:S(2)}) async-start(bf16[128,48,512]{2,1,0:T(8,128)(2,1)} %bitcast.56), calls=%async_computation.2 | async-start | bytes 12582912 | tf_op jit(solution)/shard_map/all_to_all | solution.py:313
  232.5 186.3 %all-gather.3.cloned.1.call-start = ((), (), s32[]{:S(2)}) async-start(), calls=%async_computation.5 | async-start | bytes 9437184 | tf_op jit(solution)/shard_map/all_gather | solution.py:330
  311.9 1.2 copy-start.8
  325.7 150.4 %all-gather.5.cloned.1.call-start = ((), (), s32[]{:S(2)}) async-start(), calls=%async_computation.6 | async-start | bytes 4456448 | tf_op jit(solution)/shard_map/all_gather | solution.py:331
  326.5 233.4 %reduce-scatter.2.cloned.1.call-start = ((), (), s32[]{:S(2)}) async-start(), calls=%async_computation.7 | async-start | bytes 4456448 | tf_op jit(solution)/shard_map/reduce_scatter | solution.py:334
  428.6 19.1 %slice-start = ((s8[6291456]{0:T(1024)(128)(4,1)}), s8[2097152]{0:T(1024)(128)(4,1)S(1)}, s32[]{:S(2)}) async-start(s8[6291456]{0:T(1024)(128)(4,1)} %bitcast.49), calls=%async_computation.8 | async-start | bytes 4194304
  431.8 24.8 %all-to-all-start.3 = ((bf16[128,1,6]{2,1,0:T(2,128)(2,1)}), bf16[128,1,6]{2,1,0:T(2,128)(2,1)S(1)}, u32[]{:S(2)}, u32[]{:S(2)}) async-start(bf16[128,1,6]{2,1,0:T(2,128)(2,1)} %convert_element_type.70), calls=%async_computation.4 | async-start | bytes 131072 | tf_op jit(solution)/shard_map/all_to_all | solution.py:314
  439.5 8.2 %slice-start.1 = ((s8[6291456]{0:T(1024)(128)(4,1)}), s8[4194304]{0:T(1024)(128)(4,1)S(1)}, s32[]{:S(2)}) async-start(s8[6291456]{0:T(1024)(128)(4,1)} %bitcast.49), calls=%async_computation.9 | async-start | bytes 8388608
  439.5 8.2 %copy-start.15 = (bf16[768,384]{1,0:T(8,128)(2,1)S(1)}, bf16[768,384]{1,0:T(8,128)(2,1)}, u32[]{:S(2)}) copy-start(bf16[768,384]{1,0:T(8,128)(2,1)} %get-tuple-element.19) | copy-start | bytes 1769476
  439.5 13.1 %slice-start.2 = ((s8[6291456]{0:T(1024)(128)(4,1)}), s8[4194304]{0:T(1024)(128)(4,1)S(1)}, s32[]{:S(2)}) async-start(s8[6291456]{0:T(1024)(128)(4,1)} %bitcast.54), calls=%async_computation.10 | async-start | bytes 8388608
  447.7 4.9 slice-start.3
  447.7 4.9 copy-start.11
  452.6 4.6 copy-start.12
  (2 other events, 1.4 us)
Sparse Core Ops, SparseCore 0:
  325.8 92.9 all-gather.2
  421.2 54.8 all-gather.4
  480.7 79.1 reduce-scatter.1

commit v2 on v1

--- a/solution.py
+++ b/solution.py
@@ -277,6 +277,193 @@
     )(ids, back, hidden, gain, cots)
 
 
+STEPS = 4
+SAME_L, SAME_R, SAME_T, SAME_B, FAR_C, FAR_L, FAR_R, FAR_T, FAR_B = range(9)
+TO_Z, TO_R, TO_L, PASS_R, PASS_L, EXTRA_A, EXTRA_B, EXTRA_C, EXTRA_D = range(9)
+
+
+def project_kernel(resid_ref, heads_ref, weight_ref, out_heads_ref, out_weight_ref,
+                   pieces, total, partial, from_core, summed, from_y, to_z, from_z,
+                   piece_send, piece_recv, core_send, core_recv, y_send, y_recv, z_send, z_recv):
+    ctx, tp = lax.axis_index("ctx"), lax.axis_index("tp")
+    y, z_hi, core = ctx // 4, (ctx // 2) % 2, ctx % 2
+    z_lo, x = tp // 4, tp % 4
+    right_x, left_x, opposite_x = (x + 1) % 4, (x + 3) % 4, (x + 2) % 4
+    here, there = z_lo * 4, (1 - z_lo) * 4
+    right, left, far = (ctx, here + right_x), (ctx, here + left_x), (ctx, there + x)
+    sibling = (y * 4 + z_hi * 2 + (1 - core), tp)
+    across = (y * 4 + (1 - z_hi) * 2 + core, tp)
+    plane = lambda other: (other * 4 + z_hi * 2 + core, tp)
+    tokens, features = resid_ref.shape
+    chunk = features // STEPS
+    rows = chunk // 4
+    half = tokens // 2
+    group = pieces.shape[1]
+
+    barrier = pltpu.get_barrier_semaphore()
+    peers = [right, left, far, sibling, across] + [plane((y + d) % 4) for d in (1, 2, 3)]
+    for peer in peers:
+        pl.semaphore_signal(barrier, inc=1, device_id=peer, device_id_type=pl.DeviceIdType.MESH)
+    pl.semaphore_wait(barrier, len(peers))
+
+    def remote(src, dst, send, recv, device):
+        return pltpu.make_async_remote_copy(
+            src_ref=src, dst_ref=dst, send_sem=send, recv_sem=recv,
+            device_id=device, device_id_type=pl.DeviceIdType.MESH,
+        )
+
+    whole, top, bottom = pl.ds(0, tokens), pl.ds(0, half), pl.ds(half, half)
+    sent = []
+
+    def send(i, piece, part, kind, lands, device):
+        ref = pieces.at[i, piece, part]
+        copy = remote(ref, ref, piece_send.at[i, kind], piece_recv.at[i, lands], device)
+        copy.start()
+        sent.append(copy)
+
+    def arrive(i, piece, part, lands):
+        ref = pieces.at[i, piece, part]
+        remote(ref, ref, piece_send.at[i, 0], piece_recv.at[i, lands], far).wait_recv()
+
+    def owner(i):
+        return (y + 1 + i) % 4
+
+    def start_own(i):
+        columns = pl.ds(pl.multiple_of(owner(i) * chunk, chunk), chunk)
+        pieces[i, tp] = resid_ref[:, columns]
+        send(i, tp, whole, TO_R, SAME_L, right)
+        send(i, tp, whole, TO_L, SAME_R, left)
+        send(i, tp, whole, TO_Z, FAR_C, far)
+
+    def spread(i):
+        if i % 2 == 0:
+            arrive(i, there + x, whole, FAR_C)
+            send(i, there + x, whole, EXTRA_A, FAR_L, right)
+            send(i, there + x, whole, EXTRA_B, FAR_R, left)
+        arrive(i, here + left_x, whole, SAME_L)
+        send(i, here + left_x, top, PASS_R, SAME_T, right)
+        if i % 2 == 1:
+            send(i, here + left_x, whole, EXTRA_A, FAR_L, far)
+        arrive(i, here + right_x, whole, SAME_R)
+        send(i, here + right_x, bottom, PASS_L, SAME_B, left)
+        if i % 2 == 1:
+            send(i, here + right_x, whole, EXTRA_B, FAR_R, far)
+        if i + 1 < STEPS:
+            start_own(i + 1)
+        if i % 2 == 0:
+            arrive(i, there + left_x, whole, FAR_L)
+            send(i, there + left_x, top, EXTRA_C, FAR_T, right)
+            arrive(i, there + right_x, whole, FAR_R)
+            send(i, there + right_x, bottom, EXTRA_D, FAR_B, left)
+            arrive(i, here + opposite_x, top, SAME_T)
+            arrive(i, here + opposite_x, bottom, SAME_B)
+        else:
+            arrive(i, here + opposite_x, top, SAME_T)
+            send(i, here + opposite_x, top, EXTRA_C, FAR_T, far)
+            arrive(i, here + opposite_x, bottom, SAME_B)
+            send(i, here + opposite_x, bottom, EXTRA_D, FAR_B, far)
+            arrive(i, there + x, whole, FAR_C)
+            arrive(i, there + left_x, whole, FAR_L)
+            arrive(i, there + right_x, whole, FAR_R)
+        arrive(i, there + opposite_x, top, FAR_T)
+        arrive(i, there + opposite_x, bottom, FAR_B)
+
+    def weight_partial(i, whose):
+        def one(zh, carry):
+            first = pl.multiple_of((2 * zh + (core if whose == 0 else 1 - core)) * rows, rows)
+            left_side = pieces[i, :, :, pl.ds(first, rows)].reshape(group * tokens, rows)
+            partial[i, whose, zh] = mm(left_side, heads_ref[...], CONTRACT_FIRST).astype(jnp.bfloat16)
+            return carry
+
+        lax.fori_loop(0, 2, one, 0)
+
+    def heads_partial(i):
+        weight_rows = pl.ds(pl.multiple_of(owner(i) * chunk, chunk), chunk)
+
+        def one(r, carry):
+            tall = pl.ds(pl.multiple_of(r * 2 * tokens, 2 * tokens), 2 * tokens)
+            left_side = pieces[i, pl.ds(2 * r, 2)].reshape(2 * tokens, chunk)
+            value = mm(left_side, weight_ref[weight_rows, :])
+            if i > 0:
+                value = value + total[tall, :]
+            if i < STEPS - 1:
+                total[tall, :] = value
+            else:
+                out_heads_ref[tall, :] = value.astype(jnp.bfloat16)
+            return carry
+
+        lax.fori_loop(0, group // 2, one, 0)
+
+    start_own(0)
+    for i in range(STEPS):
+        spread(i)
+        weight_partial(i, 1)
+        to_core = remote(partial.at[i, 1], from_core.at[i], core_send.at[i], core_recv.at[i], sibling)
+        to_core.start()
+        weight_partial(i, 0)
+        heads_partial(i)
+        to_core.wait()
+        if i < STEPS - 1:
+            summed[i] = (
+                partial[i, 0].astype(jnp.float32) + from_core[i].astype(jnp.float32)
+            ).astype(jnp.bfloat16)
+            copy = remote(summed.at[i], from_y.at[i], y_send.at[i], y_recv.at[i], plane(owner(i)))
+            copy.start()
+            sent.append(copy)
+
+    last = STEPS - 1
+    for i in range(last):
+        remote(summed.at[i], from_y.at[i], y_send.at[i], y_recv.at[i], across).wait_recv()
+
+    def reduced(zh):
+        value = partial[last, 0, zh].astype(jnp.float32) + from_core[last, zh].astype(jnp.float32)
+        for i in range(last):
+            value = value + from_y[i, zh].astype(jnp.float32)
+        return value
+
+    to_z[...] = reduced(1 - z_hi).astype(jnp.bfloat16)
+    copy = remote(to_z, from_z, z_send, z_recv, across)
+    copy.start()
+    own = reduced(z_hi)
+    copy.wait()
+    out_weight_ref[...] = (own + from_z[...].astype(jnp.float32)).astype(jnp.bfloat16)
+    for copy in sent:
+        copy.wait_send()
+
+
+def project(resid, heads, weight, group):
+    tokens, features = resid.shape
+    columns = heads.shape[1]
+    chunk = features // STEPS
+    rows = chunk // 4
+    bf16 = jnp.bfloat16
+    dma = pltpu.SemaphoreType.DMA
+    vmem = pl.BlockSpec(memory_space=pltpu.VMEM)
+    return pl.pallas_call(
+        project_kernel,
+        in_specs=[vmem] * 3,
+        out_specs=[vmem] * 2,
+        out_shape=[jax.ShapeDtypeStruct(heads.shape, bf16), jax.ShapeDtypeStruct((rows, columns), bf16)],
+        scratch_shapes=[
+            pltpu.VMEM((STEPS, group, tokens, chunk), bf16),
+            pltpu.VMEM(heads.shape, jnp.float32),
+            pltpu.VMEM((STEPS, 2, 2, rows, columns), bf16),
+            pltpu.VMEM((STEPS, 2, rows, columns), bf16),
+            pltpu.VMEM((STEPS - 1, 2, rows, columns), bf16),
+            pltpu.VMEM((STEPS - 1, 2, rows, columns), bf16),
+            pltpu.VMEM((rows, columns), bf16),
+            pltpu.VMEM((rows, columns), bf16),
+            dma((STEPS, 9)), dma((STEPS, 9)), dma((STEPS,)), dma((STEPS,)),
+            dma((STEPS - 1,)), dma((STEPS - 1,)), dma, dma,
+        ],
+        compiler_params=pltpu.CompilerParams(
+            collective_id=0, has_side_effects=True, vmem_limit_bytes=48 * MIB),
+        cost_estimate=pl.CostEstimate(
+            flops=4 * group * tokens * features * columns, bytes_accessed=8 * MIB, transcendentals=0),
+        name="project",
+    )(resid, heads, weight)
+
+
 def per_device(
     ctx_heads,
     out_weight,
@@ -305,8 +492,10 @@
     raw_rows = exchange(send_rows.reshape(devices, CHUNK, width)).reshape(-1, width)
     raw_cots = exchange(send_cots.reshape(devices, CHUNK, width)).reshape(-1, width)
     slot_rows = unpack_chunks(raw_rows)
+    full_weight = lax.all_gather(out_weight, "ctx", axis=0, tiled=True)
     gate_pre = mm(slot_rows, w_gate[0])
     up_value = mm(slot_rows, w_up[0])
+    gate_pre, full_weight = lax.optimization_barrier((gate_pre, full_weight))
     grads, slot_cots, activated, gate_grad, up_grad, dots = expert_back(
         raw_cots, gate_pre, up_value, w_gate[0], w_up[0], w_down[0]
     )
@@ -327,16 +516,7 @@
         jnp.sum(jnp.where(at_rank, picked, 0.0), axis=1).reshape(tokens, -1) / rounded_weights
     )
 
-    grads_all = lax.all_gather(resid_grad, "tp", axis=0, tiled=True)
-    heads_grad = mm(grads_all, lax.all_gather(out_weight, "ctx", axis=0, tiled=True)).astype(
-        jnp.bfloat16
-    )
-    weight_grad = lax.psum_scatter(
-        mm(grads_all, ctx_heads, CONTRACT_FIRST).astype(jnp.bfloat16),
-        "ctx",
-        scatter_dimension=0,
-        tiled=True,
-    )
+    heads_grad, weight_grad = project(resid_grad, ctx_heads, full_weight, lax.axis_size("tp"))
     return (
         heads_grad,
         weight_grad,

time: 567 us -> 495 us (0.87)
  Pallas kernels: 54.9 us -> 173 us
  waiting for transfers between devices: 327 us -> 217 us
  blocking collectives: 86.9 us -> 18 us
  matrix products: 45.9 us -> 27.2 us
    pallas_call x0 -> x1, Pallas kernels: none -> 115 us  [project(): pl.pallas_call(project_kernel, in_specs=[vmem] * 3, out_specs=[vmem] * 2,...]
    all_to_all x1, waiting for transfers between devices: 0.01 us -> 80.4 us  [per_device(): exchange(send_rows.reshape(devices, CHUNK, width)).reshape(-1, width)]
    reduce_scatter x1 -> x0, waiting for transfers between devices: 73.8 us -> none  [per_device(): lax.psum_scatter(mm(grads_all, ctx_heads, CONTRACT_FIRST).astype(jnp.bflo...]
    all_to_all x1, blocking collectives: 86.9 us -> 18 us  [per_device(): exchange(dots.reshape(devices, CAP).astype(jnp.bfloat16))]
    all_to_all x1, waiting for transfers between devices: 62.6 us -> 0.01 us  [per_device(): exchange(send_cots.reshape(devices, CHUNK, width)).reshape(-1, width)]
    all_gather x2 -> x1, waiting for transfers between devices: 111 us -> 77.9 us  [per_device(): full_weight = lax.all_gather(out_weight, 'ctx', axis=0, tiled=True)]
    all_to_all x1, waiting for transfers between devices: 79 us -> 58.4 us  [per_device(): back = exchange(grads.reshape(devices, CHUNK, width)).reshape(-1, width)]
    dot_general x7 -> x5, matrix products: 45.7 us -> 26.9 us  [mm(): return lax.dot_general(a, b, dims, preferred_element_type=jnp.float32)]
  transfers between devices with their start and end apart: 6 -> 4, of which waited for: 5 -> 3; matrix products, arithmetic and copies ran while one was open for 9% -> 6% of each run, Pallas kernels for 1% -> 2%
where the time goes in v2:
time: 495 us; the launch traced here: 493 us
  waiting for transfers between devices  217 us (44%)
  Pallas kernels  173 us (35%)
  starting transfers between devices  30.1 us (6%)
  matrix products  27.2 us (5%)
  blocking collectives  18 us (4%)
  between operations  14.2 us (3%)
  local copies, waits for them, and re-layouts  8.97 us (2%)
    pallas_call x1, Pallas kernels, project(): pl.pallas_call(project_kernel, in_specs=[vmem] * 3, out_specs=[vmem] * 2,...  115 us
    all_to_all x1, waiting for transfers between devices, per_device(): exchange(send_rows.reshape(devices, CHUNK, width)).reshape(-1, width)  80.4 us
    all_gather x1, waiting for transfers between devices, per_device(): full_weight = lax.all_gather(out_weight, 'ctx', axis=0, tiled=True)  77.9 us
    all_to_all x1, waiting for transfers between devices, per_device(): back = exchange(grads.reshape(devices, CHUNK, width)).reshape(-1, width)  58.4 us
    pallas_call x1, Pallas kernels, expert_back(): pl.pallas_call(back_kernel, grid=(steps,), in_specs=[tall((total // steps...  28 us
    dot_general x5, matrix products, mm(): return lax.dot_general(a, b, dims, preferred_element_type=jnp.float32)  26.9 us
    all_to_all x1, blocking collectives, per_device(): exchange(dots.reshape(devices, CAP).astype(jnp.bfloat16))  18 us
    pallas_call x1, Pallas kernels, combine(): pl.pallas_call(combine_kernel, grid=(steps,), in_specs=[whole(ids.shape),...  12.7 us
  transfers between devices with their start and end apart: 4, of which 3 were waited for; matrix products, arithmetic and copies ran while one was open for 6% of the time, Pallas kernels for 2%

profile of v2, /device:TPU:0, one launch (start us, length us, event | category | flops | bytes accessed | tf_op | source)
XLA Modules:
  0.0 492.7 jit_solution(9278916325399956343)
XLA Ops:
  8.5 1.2 copy-done.3
  9.8 1.2 copy-done.5
  11.0 0.7 copy-done.8
  11.7 9.4 %dispatch.1 = (bf16[64,2,48,512]{3,2,1,0:T(8,128)(2,1)}, bf16[64,2,48,512]{3,2,1,0:T(8,128)(2,1)}) custom-call(s32[2,128]{1,0:T(2,128)S(1)} %bitcast.46, f32[2,128]{1,0:T(2,128)S(1)} %convert_bitcast_fusion.weight_ref, bf16[128,4096]{1,0:T(8,128)(2,1)S(1)} %copy-done.3, f32[1,4096]{1,0:T(1,128)S(1)} %bitcast.47, bf16[128,4096]{1,0:T(8,128)(2,1)S(1)} %copy-done.5), custom_call_target="tpu_custom_call" | custom-call | flops 6442450944 | bytes 16777216 | tf_op jit(solution)/shard_map/dispatch/pallas_call | solution.py:87
  21.1 11.6 %all-to-all-start.1 = ((bf16[128,48,512]{2,1,0:T(8,128)(2,1)}), bf16[128,48,512]{2,1,0:T(8,128)(2,1)}, u32[]{:S(2)}, u32[]{:S(2)}) async-start(bf16[128,48,512]{2,1,0:T(8,128)(2,1)} %bitcast.51), calls=%async_computation.1 | async-start | bytes 12582912 | tf_op jit(solution)/shard_map/all_to_all | solution.py:492
  33.5 80.4 %all-to-all-done.1 = bf16[128,48,512]{2,1,0:T(8,128)(2,1)} async-done(((bf16[128,48,512]{2,1,0:T(8,128)(2,1)}), bf16[128,48,512]{2,1,0:T(8,128)(2,1)}, u32[]{:S(2)}, u32[]{:S(2)}) %all-to-all-start.1) | async-done | bytes 6291488 | tf_op jit(solution)/shard_map/all_to_all | solution.py:492
  113.8 12.3 %all-to-all-start = ((bf16[128,48,512]{2,1,0:T(8,128)(2,1)}), bf16[128,48,512]{2,1,0:T(8,128)(2,1)}, u32[]{:S(2)}, u32[]{:S(2)}) async-start(bf16[128,48,512]{2,1,0:T(8,128)(2,1)} %bitcast.50), calls=%async_computation | async-start | bytes 12582912 | tf_op jit(solution)/shard_map/all_to_all | solution.py:493
  126.2 8.0 %unpack.1 = bf16[768,4096]{1,0:T(8,128)(2,1)S(1)} custom-call(bf16[6144,512]{1,0:T(8,128)(2,1)} %bitcast.6.raw_ref), custom_call_target="tpu_custom_call" | custom-call | flops 2415919104 | bytes 12582912 | tf_op jit(solution)/shard_map/unpack/pallas_call | solution.py:144
  134.2 4.4 fusion.10.gate_ref
  138.6 4.4 fusion.8.up_ref
  143.1 77.9 %all-gather.2.cloned.1.call-done.weight_ref = bf16[4096,512]{1,0:T(8,128)(2,1)} async-done(((bf16[256,512]{1,0:T(8,128)(2,1)}), bf16[4096,512]{1,0:T(8,128)(2,1)}) %all-gather.2.cloned.1.call-update) | async-done | bytes 4194320 | tf_op jit(solution)/shard_map/all_gather | solution.py:495
  220.9 28.0 %expert_back.1 = (bf16[6144,512]{1,0:T(8,128)(2,1)}, bf16[768,4096]{1,0:T(8,128)(2,1)}, bf16[768,384]{1,0:T(8,128)(2,1)}, bf16[768,384]{1,0:T(8,128)(2,1)}, bf16[768,384]{1,0:T(8,128)(2,1)}, /*index=5*/f32[768,1]{1,0:T(8,128)}) custom-call(bf16[6144,512]{1,0:T(8,128)(2,1)} %bitcast.4.raw_ref, f32[768,384]{1,0:T(8,128)} %fusion.10.gate_ref, ...), custom_call_target="tpu_custom_call" | custom-call | flops 12079595520 | bytes 33554432 | tf_op jit(solution)/shard_map/expert_back/pallas_call | solution.py:202
  249.0 1.2 convert_reduce_fusion
  250.3 18.0 %all_to_all.21 = bf16[128,1,6]{2,1,0:T(2,128)(2,1)S(1)} all-to-all(bf16[128,1,6]{2,1,0:T(2,128)(2,1)S(1)} %convert_element_type.62), channel_id=1, replica_groups=mesh['ctx'=16,'tp'=8] {'ctx','tp'}, dimensions={0} | all-to-all | bytes 3072 | tf_op jit(solution)/shard_map/all_to_all | solution.py:503
  268.3 6.2 %all-to-all-start.2 = ((bf16[128,48,512]{2,1,0:T(8,128)(2,1)}), bf16[128,48,512]{2,1,0:T(8,128)(2,1)}, u32[]{:S(2)}, u32[]{:S(2)}) async-start(bf16[128,48,512]{2,1,0:T(8,128)(2,1)} %bitcast.49), calls=%async_computation.2 | async-start | bytes 12582912 | tf_op jit(solution)/shard_map/all_to_all | solution.py:502
  275.9 7.3 %fusion.2 = bf16[1,384,4096]{2,1,0:T(8,128)(2,1)} fusion(bf16[768,384]{1,0:T(8,128)(2,1)S(1)} %copy-done.11, bf16[768,4096]{1,0:T(8,128)(2,1)} %get-tuple-element.30), kind=kOutput, calls=%fused_computation.5 | convolution fusion | flops 2417491968 | bytes 10027008 | tf_op jit(solution)/shard_map/dot_general | solution.py:24
  283.2 6.0 %fusion.1 = bf16[1,4096,384]{2,1,0:T(8,128)(2,1)} fusion(bf16[768,4096]{1,0:T(8,128)(2,1)S(1)} %bitcast.45, bf16[768,384]{1,0:T(8,128)(2,1)} %get-tuple-element.28), kind=kOutput, calls=%fused_computation.4 | convolution fusion | flops 2417491968 | bytes 10027008 | tf_op jit(solution)/shard_map/dot_general | solution.py:24
  289.2 4.9 fusion
  295.2 58.4 %all-to-all-done.2 = bf16[128,48,512]{2,1,0:T(8,128)(2,1)} async-done(((bf16[128,48,512]{2,1,0:T(8,128)(2,1)}), bf16[128,48,512]{2,1,0:T(8,128)(2,1)}, u32[]{:S(2)}, u32[]{:S(2)}) %all-to-all-start.2) | async-done | bytes 6291488 | tf_op jit(solution)/shard_map/all_to_all | solution.py:502
  353.6 1.2 copy-done.6
  354.9 12.7 %combine.1.resid_ref = bf16[128,4096]{1,0:T(8,128)(2,1)} custom-call(s32[128,2]{1,0:T(8,128)S(1)} %copy.23.ids_ref, bf16[6144,512]{1,0:T(8,128)(2,1)} %bitcast.11.back_ref, bf16[128,4096]{1,0:T(8,128)(2,1)S(1)} %copy-done.4, f32[1,4096]{1,0:T(1,128)S(1)} %bitcast.48, bf16[128,4096]{1,0:T(8,128)(2,1)S(1)} %copy-done.6), custom_call_target="tpu_custom_call" | custom-call | flops 6442450944 | bytes 12582912 | tf_op jit(solution)/shard_map/combine/pallas_call | solution.py:264
  367.5 1.2 copy-done.10
  368.8 115.4 %project.1 = (bf16[1024,512]{1,0:T(8,128)(2,1)S(1)}, bf16[256,512]{1,0:T(8,128)(2,1)S(1)}) custom-call(bf16[128,4096]{1,0:T(8,128)(2,1)S(1)} %copy-done.10, bf16[1024,512]{1,0:T(8,128)(2,1)S(1)} %copy-done.7, bf16[4096,512]{1,0:T(8,128)(2,1)} %all-gather.2.cloned.1.call-done.weight_ref), custom_call_target="tpu_custom_call" | custom-call | flops 8589934592 | bytes 8388608 | tf_op jit(solution)/shard_map/project/pallas_call | solution.py:442
  484.1 1.0 copy.33
  (53 shorter events, 5.5 us)
Async XLA Ops:
  7.8 0.7 copy-start.1
  8.5 1.2 copy-start.3
  9.8 1.2 copy-start.5
  11.0 0.7 copy-start.8
  21.1 92.7 %all-to-all-start.1 = ((bf16[128,48,512]{2,1,0:T(8,128)(2,1)}), bf16[128,48,512]{2,1,0:T(8,128)(2,1)}, u32[]{:S(2)}, u32[]{:S(2)}) async-start(bf16[128,48,512]{2,1,0:T(8,128)(2,1)} %bitcast.51), calls=%async_computation.1 | async-start | bytes 12582912 | tf_op jit(solution)/shard_map/all_to_all | solution.py:492
  32.7 188.2 %all-gather.2.cloned.1.call-start = ((), (), s32[]{:S(2)}) async-start(), calls=%async_computation.4 | async-start | bytes 4456448 | tf_op jit(solution)/shard_map/all_gather | solution.py:495
  113.8 107.1 %all-to-all-start = ((bf16[128,48,512]{2,1,0:T(8,128)(2,1)}), bf16[128,48,512]{2,1,0:T(8,128)(2,1)}, u32[]{:S(2)}, u32[]{:S(2)}) async-start(bf16[128,48,512]{2,1,0:T(8,128)(2,1)} %bitcast.50), calls=%async_computation | async-start | bytes 12582912 | tf_op jit(solution)/shard_map/all_to_all | solution.py:493
  126.2 8.0 %copy-start.13 = (bf16[1,4096,384]{2,1,0:T(8,128)(2,1)S(1)}, bf16[1,4096,384]{2,1,0:T(8,128)(2,1)}, u32[]{:S(2)}) copy-start(bf16[1,4096,384]{2,1,0:T(8,128)(2,1)} %param.16) | copy-start | bytes 9437188
  134.2 4.4 copy-start
  134.2 4.4 copy-start.14
  268.3 6.2 %copy-start.2 = (s32[128,2]{0,1:T(2,128)S(1)}, s32[128,2]{0,1:T(2,128)}, u32[]{:S(2)}) copy-start(s32[128,2]{0,1:T(2,128)} %param.14) | copy-start | bytes 3076
  268.3 7.6 %copy-start.11 = (bf16[768,384]{1,0:T(8,128)(2,1)S(1)}, bf16[768,384]{1,0:T(8,128)(2,1)}, u32[]{:S(2)}) copy-start(bf16[768,384]{1,0:T(8,128)(2,1)} %get-tuple-element.29) | copy-start | bytes 1769476
  268.3 85.3 %all-to-all-start.2 = ((bf16[128,48,512]{2,1,0:T(8,128)(2,1)}), bf16[128,48,512]{2,1,0:T(8,128)(2,1)}, u32[]{:S(2)}, u32[]{:S(2)}) async-start(bf16[128,48,512]{2,1,0:T(8,128)(2,1)} %bitcast.49), calls=%async_computation.2 | async-start | bytes 12582912 | tf_op jit(solution)/shard_map/all_to_all | solution.py:502
  274.9 8.2 %slice-start = ((s8[6291456]{0:T(1024)(128)(4,1)}), s8[2097152]{0:T(1024)(128)(4,1)S(1)}, s32[]{:S(2)}) async-start(s8[6291456]{0:T(1024)(128)(4,1)} %bitcast.44), calls=%async_computation.5 | async-start | bytes 4194304
  275.9 7.3 %slice-start.1 = ((s8[6291456]{0:T(1024)(128)(4,1)}), s8[4194304]{0:T(1024)(128)(4,1)S(1)}, s32[]{:S(2)}) async-start(s8[6291456]{0:T(1024)(128)(4,1)} %bitcast.44), calls=%async_computation.6 | async-start | bytes 8388608
  283.2 6.0 %copy-start.15 = (bf16[768,384]{1,0:T(8,128)(2,1)S(1)}, bf16[768,384]{1,0:T(8,128)(2,1)}, u32[]{:S(2)}) copy-start(bf16[768,384]{1,0:T(8,128)(2,1)} %get-tuple-element.27) | copy-start | bytes 1769476
  289.1 5.5 %copy-start.12 = (f32[128,2]{0,1:T(2,128)S(1)}, f32[128,2]{0,1:T(2,128)}, u32[]{:S(2)}) copy-start(f32[128,2]{0,1:T(2,128)} %param.15) | copy-start | bytes 3076
  289.1 64.5 %copy-start.4 = (bf16[128,4096]{1,0:T(8,128)(2,1)S(1)}, bf16[128,4096]{1,0:T(8,128)(2,1)}, u32[]{:S(2)}) copy-start(bf16[128,4096]{1,0:T(8,128)(2,1)} %hidden_ref.3) | copy-start | bytes 3145732
  289.1 64.5 %copy-start.9 = (f32[4096]{0:T(1024)S(1)}, f32[4096]{0:T(1024)}, u32[]{:S(2)}) copy-start(f32[4096]{0:T(1024)} %param.13) | copy-start | bytes 49156
  353.6 1.2 copy-start.6
  354.9 12.7 %copy-start.7 = (bf16[1024,512]{1,0:T(8,128)(2,1)S(1)}, bf16[1024,512]{1,0:T(8,128)(2,1)}, u32[]{:S(2)}) copy-start(bf16[1024,512]{1,0:T(8,128)(2,1)} %heads_ref.1) | copy-start | bytes 3145732
  367.5 1.2 copy-start.10
Sparse Core Ops, SparseCore 0:
  36.0 184.9 all-gather.1

commit v3 on v2

--- a/solution.py
+++ b/solution.py
@@ -25,10 +25,10 @@
 
 
 def dispatch_kernel(ids_ref, weight_ref, hidden_ref, gain_ref, cot_ref, rows_ref, cots_ref,
-                    slot, weight, stacked_rows, stacked_cots):
+                    flat_rows, flat_cots, unpack):
     tokens, features = hidden_ref.shape
     width = features // BLOCKS
-    experts = slot.shape[0]
+    experts = flat_rows.shape[0] // CAP
     group = rows_ref.shape[0]
     step = pl.program_id(0)
 
@@ -40,38 +40,42 @@
         named = jnp.where(first | second, 1.0, 0.0)
         earlier = jnp.where(iota((tokens, tokens), 0) < iota((tokens, tokens), 1), 1.0, 0.0)
         prior = mm(named.astype(jnp.bfloat16), earlier.astype(jnp.bfloat16))
-        slot[...] = jnp.where(named > 0.5, prior, -1.0)
-        weight[...] = jnp.where(
+        unpack[...] = unpack_matrix(group)
+        slots = jnp.where(named > 0.5, prior, -1.0).astype(jnp.bfloat16)
+        weights = jnp.where(
             first, weight_ref[0:1, :], jnp.where(second, weight_ref[1:2, :], 0.0)
-        )
+        ).astype(jnp.bfloat16)
+        row = iota((experts * CAP, experts), 0)
+        expert_of = row // CAP
+        spread = jnp.where(expert_of == iota((experts * CAP, experts), 1), 1.0, 0.0)
+        spread = spread.astype(jnp.bfloat16)
+        place = iota((experts * CAP, tokens), 0)
+        place = (place - place // CAP * CAP).astype(jnp.float32)
+        taken = mm(spread, slots) == place
+        pick_rows = jnp.where(taken, 1.0, 0.0).astype(jnp.bfloat16)
+        pick_cots = jnp.where(taken, mm(spread, weights), 0.0).astype(jnp.bfloat16)
         wide = hidden_ref[...].astype(jnp.float32)
         scale = lax.rsqrt(jnp.mean(wide * wide, axis=-1, keepdims=True) + EPSILON)
         for block in range(BLOCKS):
             columns = slice(block * width, (block + 1) * width)
-            rows = slice(block * tokens, (block + 1) * tokens)
-            stacked_rows[rows, :] = (
+            normed = (
                 hidden_ref[:, columns].astype(jnp.float32) * scale * gain_ref[:, columns]
             ).astype(jnp.bfloat16)
-            stacked_cots[rows, :] = cot_ref[:, columns]
-
-    here = pl.ds(pl.multiple_of(step * group, group), group)
-    shape = (group, CHUNK, tokens)
-    slots = jnp.broadcast_to(slot[here, :][:, None, :], shape)
-    weights = jnp.broadcast_to(weight[here, :][:, None, :], shape)
-    place = iota(shape, 1)
-    block_of = place // CAP
-    taken = slots == (place - block_of * CAP).astype(jnp.float32)
-    weights = jnp.where(taken, weights, 0.0).reshape(group * CHUNK, tokens)
-    taken = jnp.where(taken, 1.0, 0.0).reshape(group * CHUNK, tokens)
-    block_of = block_of.reshape(group * CHUNK, tokens)
-    pick_rows = jnp.concatenate(
-        [jnp.where(block_of == b, taken, 0.0).astype(jnp.bfloat16) for b in range(BLOCKS)], axis=1
-    )
-    pick_cots = jnp.concatenate(
-        [jnp.where(block_of == b, weights, 0.0).astype(jnp.bfloat16) for b in range(BLOCKS)], axis=1
-    )
-    rows = mm(pick_rows, stacked_rows[...]).astype(jnp.bfloat16).reshape(group, CHUNK, width)
-    cots = mm(pick_cots, stacked_cots[...]).astype(jnp.bfloat16).reshape(group, CHUNK, width)
+            flat_rows[:, columns] = mm(pick_rows, normed).astype(jnp.bfloat16)
+            flat_cots[:, columns] = mm(pick_cots, cot_ref[:, columns]).astype(jnp.bfloat16)
+
+    height = group * CAP
+    here = pl.ds(pl.multiple_of(step * height, height), height)
+    rows, cots = (
+        mm(
+            unpack[...],
+            jnp.concatenate(
+                [flat[here, b * width:(b + 1) * width] for b in range(BLOCKS)], axis=0
+            ),
+            CONTRACT_FIRST,
+        ).astype(jnp.bfloat16).reshape(group, CHUNK, width)
+        for flat in (flat_rows, flat_cots)
+    )
     for half in range(2):
         rows_ref[:, half] = rows
         cots_ref[:, half] = cots
@@ -92,10 +96,9 @@
         out_specs=[out_spec, out_spec],
         out_shape=[out, out],
         scratch_shapes=[
-            pltpu.VMEM((experts, tokens), jnp.float32),
-            pltpu.VMEM((experts, tokens), jnp.float32),
-            pltpu.VMEM((BLOCKS * tokens, width), jnp.bfloat16),
-            pltpu.VMEM((BLOCKS * tokens, width), jnp.bfloat16),
+            pltpu.VMEM((experts * CAP, features), jnp.bfloat16),
+            pltpu.VMEM((experts * CAP, features), jnp.bfloat16),
+            pltpu.VMEM((group * CHUNK, group * CHUNK), jnp.bfloat16),
         ],
         compiler_params=pltpu.CompilerParams(vmem_limit_bytes=48 * MIB),
         cost_estimate=pl.CostEstimate(
@@ -191,7 +194,7 @@
         ).astype(jnp.bfloat16)
 
 
-def expert_back(raw, gate_pre, up_value, w_gate, w_up, w_down, steps=4):
+def expert_back(raw, gate_pre, up_value, w_gate, w_up, w_down, steps=2):
     total, width = raw.shape
     features, hidden = w_gate.shape
     slots = gate_pre.shape[0]
@@ -241,20 +244,32 @@
     piece = lane // CAP
     taken = jnp.where(slots == (lane - piece * CAP).astype(jnp.float32), 1.0, 0.0)
     block_of = piece - piece // BLOCKS * BLOCKS
-    for b in range(BLOCKS):
-        columns = slice(b * width, (b + 1) * width)
-        pick = jnp.where(block_of == b, taken, 0.0).astype(jnp.bfloat16)
-        total[:, columns] += mm(pick, back_ref[...])
+    picks = jnp.concatenate(
+        [jnp.where(block_of == b, taken, 0.0).astype(jnp.bfloat16) for b in range(BLOCKS)], axis=0
+    )
+    total[...] += mm(picks, back_ref[...])
 
     @pl.when(step == pl.num_programs(0) - 1)
     def _():
         wide = hidden_ref[...].astype(jnp.float32)
         scale = lax.rsqrt(jnp.mean(wide * wide, axis=-1, keepdims=True) + EPSILON)
-        gained = total[...] * gain_ref[...]
-        inner = jnp.mean(gained * wide, axis=-1, keepdims=True)
-        resid_ref[...] = (
-            cot_ref[...].astype(jnp.float32) + scale * gained - wide * (scale * scale * scale * inner)
-        ).astype(jnp.bfloat16)
+        inner = jnp.zeros((tokens, 1), jnp.float32)
+        for b in range(BLOCKS):
+            columns = slice(b * width, (b + 1) * width)
+            rows = slice(b * tokens, (b + 1) * tokens)
+            gained = total[rows, :] * gain_ref[:, columns]
+            inner += jnp.sum(
+                gained * hidden_ref[:, columns].astype(jnp.float32), axis=-1, keepdims=True
+            )
+        inner = (scale * scale * scale) * (inner / features)
+        for b in range(BLOCKS):
+            columns = slice(b * width, (b + 1) * width)
+            rows = slice(b * tokens, (b + 1) * tokens)
+            gained = total[rows, :] * gain_ref[:, columns]
+            resid_ref[:, columns] = (
+                cot_ref[:, columns].astype(jnp.float32) + scale * gained
+                - hidden_ref[:, columns].astype(jnp.float32) * inner
+            ).astype(jnp.bfloat16)
 
 
 def combine(ids, back, hidden, gain, cots, experts, steps=8):
@@ -269,7 +284,7 @@
         out_specs=whole(hidden.shape),
         out_shape=jax.ShapeDtypeStruct(hidden.shape, jnp.bfloat16),
         scratch_shapes=[pltpu.VMEM((tokens, experts), jnp.bfloat16),
-                        pltpu.VMEM((tokens, features), jnp.float32)],
+                        pltpu.VMEM((BLOCKS * tokens, width), jnp.float32)],
         compiler_params=pltpu.CompilerParams(vmem_limit_bytes=40 * MIB),
         cost_estimate=pl.CostEstimate(
             flops=2 * BLOCKS * tokens * total * width, bytes_accessed=12 * MIB, transcendentals=0),
@@ -335,7 +350,7 @@
         send(i, tp, whole, TO_L, SAME_R, left)
         send(i, tp, whole, TO_Z, FAR_C, far)
 
-    def spread(i):
+    def first_hops(i):
         if i % 2 == 0:
             arrive(i, there + x, whole, FAR_C)
             send(i, there + x, whole, EXTRA_A, FAR_L, right)
@@ -348,20 +363,24 @@
         send(i, here + right_x, bottom, PASS_L, SAME_B, left)
         if i % 2 == 1:
             send(i, here + right_x, whole, EXTRA_B, FAR_R, far)
-        if i + 1 < STEPS:
-            start_own(i + 1)
+
+    def second_hops(i):
         if i % 2 == 0:
             arrive(i, there + left_x, whole, FAR_L)
             send(i, there + left_x, top, EXTRA_C, FAR_T, right)
             arrive(i, there + right_x, whole, FAR_R)
             send(i, there + right_x, bottom, EXTRA_D, FAR_B, left)
-            arrive(i, here + opposite_x, top, SAME_T)
-            arrive(i, here + opposite_x, bottom, SAME_B)
         else:
             arrive(i, here + opposite_x, top, SAME_T)
             send(i, here + opposite_x, top, EXTRA_C, FAR_T, far)
             arrive(i, here + opposite_x, bottom, SAME_B)
             send(i, here + opposite_x, bottom, EXTRA_D, FAR_B, far)
+
+    def arrivals(i):
+        if i % 2 == 0:
+            arrive(i, here + opposite_x, top, SAME_T)
+            arrive(i, here + opposite_x, bottom, SAME_B)
+        else:
             arrive(i, there + x, whole, FAR_C)
             arrive(i, there + left_x, whole, FAR_L)
             arrive(i, there + right_x, whole, FAR_R)
@@ -394,13 +413,13 @@
 
         lax.fori_loop(0, group // 2, one, 0)
 
-    start_own(0)
-    for i in range(STEPS):
-        spread(i)
+    def multiply(i, between=()):
         weight_partial(i, 1)
         to_core = remote(partial.at[i, 1], from_core.at[i], core_send.at[i], core_recv.at[i], sibling)
         to_core.start()
         weight_partial(i, 0)
+        for hops, other in between:
+            hops(other)
         heads_partial(i)
         to_core.wait()
         if i < STEPS - 1:
@@ -410,6 +429,25 @@
             copy = remote(summed.at[i], from_y.at[i], y_send.at[i], y_recv.at[i], plane(owner(i)))
             copy.start()
             sent.append(copy)
+
+    start_own(0)
+    start_own(1)
+    first_hops(0)
+    first_hops(1)
+    second_hops(0)
+    start_own(2)
+    second_hops(1)
+    start_own(3)
+    arrivals(0)
+    multiply(0)
+    arrivals(1)
+    multiply(1, ((first_hops, 2), (first_hops, 3)))
+    second_hops(2)
+    second_hops(3)
+    arrivals(2)
+    multiply(2)
+    arrivals(3)
+    multiply(3)
 
     last = STEPS - 1
     for i in range(last):
@@ -500,7 +538,13 @@
         raw_cots, gate_pre, up_value, w_gate[0], w_up[0], w_down[0]
     )
     back = exchange(grads.reshape(devices, CHUNK, width)).reshape(-1, width)
-    back_dots = exchange(dots.reshape(devices, CAP).astype(jnp.bfloat16)).astype(jnp.float32)
+    lanes = 128
+    sent_dots = jnp.pad(dots.reshape(-1, lanes), ((0, 2), (0, 0))).astype(jnp.bfloat16)
+    all_dots = lax.all_gather(sent_dots, axes, axis=0, tiled=True)
+    me = lax.axis_index(axes)
+    back_dots = lax.dynamic_slice(
+        all_dots.reshape(devices, -1), (0, me * CAP), (devices, CAP)
+    ).astype(jnp.float32)
     down_wgrad = mm(activated, slot_cots, CONTRACT_FIRST).astype(jnp.bfloat16)
     gate_wgrad = mm(slot_rows, gate_grad, CONTRACT_FIRST).astype(jnp.bfloat16)
     up_wgrad = mm(slot_rows, up_grad, CONTRACT_FIRST).astype(jnp.bfloat16)

time: 495 us -> 755 us (1.53)
  blocking collectives: 18 us -> 378 us
  waiting for transfers between devices: 217 us -> 159 us
  Pallas kernels: 173 us -> 123 us
    all_gather x0 -> x1, blocking collectives: none -> 378 us  [per_device(): all_dots = lax.all_gather(sent_dots, axes, axis=0, tiled=True)]
    all_to_all x1, waiting for transfers between devices: 58.4 us -> 0.01 us  [per_device(): back = exchange(grads.reshape(devices, CHUNK, width)).reshape(-1, width)]
    pallas_call x1, Pallas kernels: 115 us -> 69.6 us  [project(): pl.pallas_call(project_kernel, in_specs=[vmem] * 3, out_specs=[vmem] * 2,...]
    all_to_all x1 -> x0, blocking collectives: 18 us -> none  [per_device(): exchange(dots.reshape(devices, CAP).astype(jnp.bfloat16))]
  transfers between devices with their start and end apart: 4 -> 4, of which waited for: 3 -> 2; matrix products, arithmetic and copies ran while one was open for 6% -> 4% of each run, Pallas kernels for 2% -> 1%
where the time goes in v3:
time: 755 us; the launch traced here: 746 us
  blocking collectives  378 us (50%)
  waiting for transfers between devices  159 us (21%)
  Pallas kernels  123 us (16%)
  starting transfers between devices  33.3 us (4%)
  matrix products  26 us (3%)
  between operations  14.3 us (2%)
  local copies, waits for them, and re-layouts  9.03 us (1%)
    all_gather x1, blocking collectives, per_device(): all_dots = lax.all_gather(sent_dots, axes, axis=0, tiled=True)  378 us
    all_to_all x1, waiting for transfers between devices, per_device(): exchange(send_rows.reshape(devices, CHUNK, width)).reshape(-1, width)  80.4 us
    all_gather x1, waiting for transfers between devices, per_device(): full_weight = lax.all_gather(out_weight, 'ctx', axis=0, tiled=True)  77.9 us
    pallas_call x1, Pallas kernels, project(): pl.pallas_call(project_kernel, in_specs=[vmem] * 3, out_specs=[vmem] * 2,...  69.6 us
    dot_general x5, matrix products, mm(): return lax.dot_general(a, b, dims, preferred_element_type=jnp.float32)  25.8 us
    pallas_call x1, Pallas kernels, expert_back(): pl.pallas_call(back_kernel, grid=(steps,), in_specs=[tall((total // steps...  24.2 us
  transfers between devices with their start and end apart: 4, of which 2 were waited for; matrix products, arithmetic and copies ran while one was open for 4% of the time, Pallas kernels for 1%

profile of v3, /device:TPU:0, one launch (start us, length us, event | category | flops | bytes accessed | tf_op | source)
XLA Modules:
  0.0 745.8 jit_solution(7067140998210941969)
XLA Ops:
  7.2 0.7 convert_bitcast_fusion.weight_ref
  8.5 1.2 copy-done.3
  9.8 1.2 copy-done.5
  11.0 0.7 copy-done.8
  11.7 9.2 %dispatch.1 = (bf16[64,2,48,512]{3,2,1,0:T(8,128)(2,1)}, bf16[64,2,48,512]{3,2,1,0:T(8,128)(2,1)}) custom-call(s32[2,128]{1,0:T(2,128)S(1)} %bitcast.48, f32[2,128]{1,0:T(2,128)S(1)} %convert_bitcast_fusion.weight_ref, bf16[128,4096]{1,0:T(8,128)(2,1)S(1)} %copy-done.3, f32[1,4096]{1,0:T(1,128)S(1)} %bitcast.49, bf16[128,4096]{1,0:T(8,128)(2,1)S(1)} %copy-done.5), custom_call_target="tpu_custom_call" | custom-call | flops 6442450944 | bytes 16777216 | tf_op jit(solution)/shard_map/dispatch/pallas_call | solution.py:91
  20.9 11.6 %all-to-all-start.1 = ((bf16[128,48,512]{2,1,0:T(8,128)(2,1)}), bf16[128,48,512]{2,1,0:T(8,128)(2,1)}, u32[]{:S(2)}, u32[]{:S(2)}) async-start(bf16[128,48,512]{2,1,0:T(8,128)(2,1)} %bitcast.53), calls=%async_computation.1 | async-start | bytes 12582912 | tf_op jit(solution)/shard_map/all_to_all | solution.py:530
  33.3 80.4 %all-to-all-done.1 = bf16[128,48,512]{2,1,0:T(8,128)(2,1)} async-done(((bf16[128,48,512]{2,1,0:T(8,128)(2,1)}), bf16[128,48,512]{2,1,0:T(8,128)(2,1)}, u32[]{:S(2)}, u32[]{:S(2)}) %all-to-all-start.1) | async-done | bytes 6291488 | tf_op jit(solution)/shard_map/all_to_all | solution.py:530
  113.7 12.3 %all-to-all-start = ((bf16[128,48,512]{2,1,0:T(8,128)(2,1)}), bf16[128,48,512]{2,1,0:T(8,128)(2,1)}, u32[]{:S(2)}, u32[]{:S(2)}) async-start(bf16[128,48,512]{2,1,0:T(8,128)(2,1)} %bitcast.52), calls=%async_computation | async-start | bytes 12582912 | tf_op jit(solution)/shard_map/all_to_all | solution.py:531
  126.0 8.0 %unpack.1 = bf16[768,4096]{1,0:T(8,128)(2,1)S(1)} custom-call(bf16[6144,512]{1,0:T(8,128)(2,1)} %bitcast.6.raw_ref), custom_call_target="tpu_custom_call" | custom-call | flops 2415919104 | bytes 12582912 | tf_op jit(solution)/shard_map/unpack/pallas_call | solution.py:147
  134.0 4.4 fusion.10.gate_ref
  138.5 4.4 fusion.8.up_ref
  142.9 77.9 %all-gather.2.cloned.1.call-done.weight_ref = bf16[4096,512]{1,0:T(8,128)(2,1)} async-done(((bf16[256,512]{1,0:T(8,128)(2,1)}), bf16[4096,512]{1,0:T(8,128)(2,1)}) %all-gather.2.cloned.1.call-update) | async-done | bytes 4194320 | tf_op jit(solution)/shard_map/all_gather | solution.py:533
  220.8 24.2 %expert_back.1 = (bf16[6144,512]{1,0:T(8,128)(2,1)}, bf16[768,4096]{1,0:T(8,128)(2,1)}, bf16[768,384]{1,0:T(8,128)(2,1)}, bf16[768,384]{1,0:T(8,128)(2,1)}, bf16[768,384]{1,0:T(8,128)(2,1)}, /*index=5*/f32[768,1]{1,0:T(8,128)}) custom-call(bf16[6144,512]{1,0:T(8,128)(2,1)} %bitcast.4.raw_ref, f32[768,384]{1,0:T(8,128)} %fusion.10.gate_ref, ...), custom_call_target="tpu_custom_call" | custom-call | flops 12079595520 | bytes 33554432 | tf_op jit(solution)/shard_map/expert_back/pallas_call | solution.py:205
  245.0 9.4 %all-to-all-start.2 = ((bf16[128,48,512]{2,1,0:T(8,128)(2,1)}), bf16[128,48,512]{2,1,0:T(8,128)(2,1)}, u32[]{:S(2)}, u32[]{:S(2)}) async-start(bf16[128,48,512]{2,1,0:T(8,128)(2,1)} %bitcast.51), calls=%async_computation.2 | async-start | bytes 12582912 | tf_op jit(solution)/shard_map/all_to_all | solution.py:540
  256.0 378.4 %all_gather.7 = bf16[1024,128]{1,0:T(8,128)(2,1)S(1)} all-gather(bf16[8,128]{1,0:T(8,128)(2,1)S(1)} %pad.5), channel_id=1, replica_groups=mesh['ctx'=16,'tp'=8] {'ctx','tp'}, dimensions={0}, use_global_device_ids=true | all-gather | bytes 264192 | tf_op jit(solution)/shard_map/all_gather | solution.py:543
  635.8 7.2 fusion.2
  643.0 4.9 fusion.1
  647.9 4.9 fusion
  652.8 1.2 copy-done.6
  654.0 12.4 %combine.1.resid_ref = bf16[128,4096]{1,0:T(8,128)(2,1)} custom-call(s32[128,2]{1,0:T(8,128)S(1)} %copy.18.ids_ref, bf16[6144,512]{1,0:T(8,128)(2,1)} %bitcast.11.back_ref, bf16[128,4096]{1,0:T(8,128)(2,1)S(1)} %copy-done.4, f32[1,4096]{1,0:T(1,128)S(1)} %bitcast.50, bf16[128,4096]{1,0:T(8,128)(2,1)S(1)} %copy-done.6), custom_call_target="tpu_custom_call" | custom-call | flops 6442450944 | bytes 12582912 | tf_op jit(solution)/shard_map/combine/pallas_call | solution.py:279
  666.4 1.2 copy-done.10
  667.6 69.6 %project.1 = (bf16[1024,512]{1,0:T(8,128)(2,1)S(1)}, bf16[256,512]{1,0:T(8,128)(2,1)S(1)}) custom-call(bf16[128,4096]{1,0:T(8,128)(2,1)S(1)} %copy-done.10, bf16[1024,512]{1,0:T(8,128)(2,1)S(1)} %copy-done.7, bf16[4096,512]{1,0:T(8,128)(2,1)} %all-gather.2.cloned.1.call-done.weight_ref), custom_call_target="tpu_custom_call" | custom-call | flops 8589934592 | bytes 8388608 | tf_op jit(solution)/shard_map/project/pallas_call | solution.py:480
  737.2 1.0 copy.27
  738.2 0.7 copy.28
  (58 shorter events, 4.3 us)
Async XLA Ops:
  7.8 0.7 copy-start.1
  8.5 1.2 copy-start.3
  9.8 1.2 copy-start.5
  11.0 0.7 copy-start.8
  20.9 92.7 %all-to-all-start.1 = ((bf16[128,48,512]{2,1,0:T(8,128)(2,1)}), bf16[128,48,512]{2,1,0:T(8,128)(2,1)}, u32[]{:S(2)}, u32[]{:S(2)}) async-start(bf16[128,48,512]{2,1,0:T(8,128)(2,1)} %bitcast.53), calls=%async_computation.1 | async-start | bytes 12582912 | tf_op jit(solution)/shard_map/all_to_all | solution.py:530
  32.6 188.2 %all-gather.2.cloned.1.call-start = ((), (), s32[]{:S(2)}) async-start(), calls=%async_computation.3 | async-start | bytes 4456448 | tf_op jit(solution)/shard_map/all_gather | solution.py:533
  113.7 107.1 %all-to-all-start = ((bf16[128,48,512]{2,1,0:T(8,128)(2,1)}), bf16[128,48,512]{2,1,0:T(8,128)(2,1)}, u32[]{:S(2)}, u32[]{:S(2)}) async-start(bf16[128,48,512]{2,1,0:T(8,128)(2,1)} %bitcast.52), calls=%async_computation | async-start | bytes 12582912 | tf_op jit(solution)/shard_map/all_to_all | solution.py:531
  126.0 8.0 %copy-start.14 = (bf16[1,4096,384]{2,1,0:T(8,128)(2,1)S(1)}, bf16[1,4096,384]{2,1,0:T(8,128)(2,1)}, u32[]{:S(2)}) copy-start(bf16[1,4096,384]{2,1,0:T(8,128)(2,1)} %param.16) | copy-start | bytes 9437188
  134.0 4.4 copy-start
  134.0 4.4 copy-start.15
  245.0 9.4 %copy-start.2 = (s32[128,2]{0,1:T(2,128)S(1)}, s32[128,2]{0,1:T(2,128)}, u32[]{:S(2)}) copy-start(s32[128,2]{0,1:T(2,128)} %param.14) | copy-start | bytes 3076
  245.0 10.8 %copy-start.12 = (f32[768,1]{1,0:T(8,128)S(1)}, f32[768,1]{1,0:T(8,128)}, u32[]{:S(2)}) copy-start(f32[768,1]{1,0:T(8,128)} %get-tuple-element.26) | copy-start | bytes 9220
  245.0 390.1 %copy-start.13 = (f32[128,2]{0,1:T(2,128)S(1)}, f32[128,2]{0,1:T(2,128)}, u32[]{:S(2)}) copy-start(f32[128,2]{0,1:T(2,128)} %param.15) | copy-start | bytes 3076
  245.0 390.7 %copy-start.11 = (bf16[768,384]{1,0:T(8,128)(2,1)S(1)}, bf16[768,384]{1,0:T(8,128)(2,1)}, u32[]{:S(2)}) copy-start(bf16[768,384]{1,0:T(8,128)(2,1)} %get-tuple-element.29) | copy-start | bytes 1769476
  245.0 407.7 %all-to-all-start.2 = ((bf16[128,48,512]{2,1,0:T(8,128)(2,1)}), bf16[128,48,512]{2,1,0:T(8,128)(2,1)}, u32[]{:S(2)}, u32[]{:S(2)}) async-start(bf16[128,48,512]{2,1,0:T(8,128)(2,1)} %bitcast.51), calls=%async_computation.2 | async-start | bytes 12582912 | tf_op jit(solution)/shard_map/all_to_all | solution.py:540
  634.6 8.4 %slice-start = ((s8[6291456]{0:T(1024)(128)(4,1)}), s8[2097152]{0:T(1024)(128)(4,1)S(1)}, s32[]{:S(2)}) async-start(s8[6291456]{0:T(1024)(128)(4,1)} %bitcast.46), calls=%async_computation.4 | async-start | bytes 4194304
  634.6 8.4 %copy-start.17 = (bf16[768,384]{1,0:T(8,128)(2,1)S(1)}, bf16[768,384]{1,0:T(8,128)(2,1)}, u32[]{:S(2)}) copy-start(bf16[768,384]{1,0:T(8,128)(2,1)} %get-tuple-element.28) | copy-start | bytes 1769476
  635.8 7.3 slice-start.1
  643.0 4.9 copy-start.16
  647.9 4.9 copy-start.4
  647.9 4.9 copy-start.9
  652.8 1.2 copy-start.6
  654.0 12.4 %copy-start.7 = (bf16[1024,512]{1,0:T(8,128)(2,1)S(1)}, bf16[1024,512]{1,0:T(8,128)(2,1)}, u32[]{:S(2)}) copy-start(bf16[1024,512]{1,0:T(8,128)(2,1)} %heads_ref.1) | copy-start | bytes 3145732
  666.4 1.2 copy-start.10
Sparse Core Ops, SparseCore 0:
  35.8 184.9 all-gather.1

commit v4 on v3

--- a/solution.py
+++ b/solution.py
@@ -24,12 +24,11 @@
     return lax.dot_general(a, b, dims, preferred_element_type=jnp.float32)
 
 
-def dispatch_kernel(ids_ref, weight_ref, hidden_ref, gain_ref, cot_ref, rows_ref, cots_ref,
-                    flat_rows, flat_cots, unpack):
-    tokens, features = hidden_ref.shape
+def dispatch_kernel(normalize, ids_ref, weight_ref, value_ref, gain_ref, out_ref, flat, unpack):
+    tokens, features = value_ref.shape
     width = features // BLOCKS
-    experts = flat_rows.shape[0] // CAP
-    group = rows_ref.shape[0]
+    experts = flat.shape[0] // CAP
+    group = out_ref.shape[0]
     step = pl.program_id(0)
 
     @pl.when(step == 0)
@@ -52,60 +51,51 @@
         place = iota((experts * CAP, tokens), 0)
         place = (place - place // CAP * CAP).astype(jnp.float32)
         taken = mm(spread, slots) == place
-        pick_rows = jnp.where(taken, 1.0, 0.0).astype(jnp.bfloat16)
-        pick_cots = jnp.where(taken, mm(spread, weights), 0.0).astype(jnp.bfloat16)
-        wide = hidden_ref[...].astype(jnp.float32)
-        scale = lax.rsqrt(jnp.mean(wide * wide, axis=-1, keepdims=True) + EPSILON)
+        if normalize:
+            picks = jnp.where(taken, 1.0, 0.0).astype(jnp.bfloat16)
+            wide = value_ref[...].astype(jnp.float32)
+            scale = lax.rsqrt(jnp.mean(wide * wide, axis=-1, keepdims=True) + EPSILON)
+        else:
+            picks = jnp.where(taken, mm(spread, weights), 0.0).astype(jnp.bfloat16)
         for block in range(BLOCKS):
             columns = slice(block * width, (block + 1) * width)
-            normed = (
-                hidden_ref[:, columns].astype(jnp.float32) * scale * gain_ref[:, columns]
-            ).astype(jnp.bfloat16)
-            flat_rows[:, columns] = mm(pick_rows, normed).astype(jnp.bfloat16)
-            flat_cots[:, columns] = mm(pick_cots, cot_ref[:, columns]).astype(jnp.bfloat16)
+            values = value_ref[:, columns]
+            if normalize:
+                values = (values.astype(jnp.float32) * scale * gain_ref[:, columns]).astype(jnp.bfloat16)
+            flat[:, columns] = mm(picks, values).astype(jnp.bfloat16)
 
     height = group * CAP
     here = pl.ds(pl.multiple_of(step * height, height), height)
-    rows, cots = (
-        mm(
-            unpack[...],
-            jnp.concatenate(
-                [flat[here, b * width:(b + 1) * width] for b in range(BLOCKS)], axis=0
-            ),
-            CONTRACT_FIRST,
-        ).astype(jnp.bfloat16).reshape(group, CHUNK, width)
-        for flat in (flat_rows, flat_cots)
-    )
+    stacked = jnp.concatenate(
+        [flat[here, b * width:(b + 1) * width] for b in range(BLOCKS)], axis=0
+    )
+    chunks = mm(unpack[...], stacked, CONTRACT_FIRST).astype(jnp.bfloat16)
+    chunks = chunks.reshape(group, CHUNK, width)
     for half in range(2):
-        rows_ref[:, half] = rows
-        cots_ref[:, half] = cots
-
-
-def dispatch(ids_t, weights_t, hidden, gain, cots, experts):
-    tokens, features = hidden.shape
+        out_ref[:, half] = chunks
+
+
+def dispatch(normalize, ids_t, weights_t, values, gain, experts):
+    tokens, features = values.shape
     width = features // BLOCKS
     group = 8
     whole = lambda shape: pl.BlockSpec(shape, lambda i: (0, 0))
-    out = jax.ShapeDtypeStruct((experts, 2, CHUNK, width), jnp.bfloat16)
-    out_spec = pl.BlockSpec((group, 2, CHUNK, width), lambda i: (i, 0, 0, 0))
     return pl.pallas_call(
-        dispatch_kernel,
+        functools.partial(dispatch_kernel, normalize),
         grid=(experts // group,),
-        in_specs=[whole(ids_t.shape), whole(weights_t.shape), whole(hidden.shape),
-                  whole(gain.shape), whole(cots.shape)],
-        out_specs=[out_spec, out_spec],
-        out_shape=[out, out],
+        in_specs=[whole(ids_t.shape), whole(weights_t.shape), whole(values.shape), whole(gain.shape)],
+        out_specs=pl.BlockSpec((group, 2, CHUNK, width), lambda i: (i, 0, 0, 0)),
+        out_shape=jax.ShapeDtypeStruct((experts, 2, CHUNK, width), jnp.bfloat16),
         scratch_shapes=[
-            pltpu.VMEM((experts * CAP, features), jnp.bfloat16),
             pltpu.VMEM((experts * CAP, features), jnp.bfloat16),
             pltpu.VMEM((group * CHUNK, group * CHUNK), jnp.bfloat16),
         ],
-        compiler_params=pltpu.CompilerParams(vmem_limit_bytes=48 * MIB),
+        compiler_params=pltpu.CompilerParams(vmem_limit_bytes=32 * MIB),
         cost_estimate=pl.CostEstimate(
-            flops=4 * experts * CHUNK * tokens * features, bytes_accessed=16 * MIB,
+            flops=2 * experts * CHUNK * tokens * features, bytes_accessed=8 * MIB,
             transcendentals=0),
-        name="dispatch",
-    )(ids_t, weights_t, hidden, gain, cots)
+        name="dispatch_rows" if normalize else "dispatch_cots",
+    )(ids_t, weights_t, values, gain)
 
 
 def unpack_matrix(sources):
@@ -298,8 +288,9 @@
 
 
 def project_kernel(resid_ref, heads_ref, weight_ref, out_heads_ref, out_weight_ref,
-                   pieces, total, partial, from_core, summed, from_y, to_z, from_z,
-                   piece_send, piece_recv, core_send, core_recv, y_send, y_recv, z_send, z_recv):
+                   pieces, total, partial, from_core, summed, from_y, to_z, from_z, blocks,
+                   piece_send, piece_recv, core_send, core_recv, y_send, y_recv, z_send, z_recv,
+                   block_send, block_y_recv, block_core_recv, block_z_recv):
     ctx, tp = lax.axis_index("ctx"), lax.axis_index("tp")
     y, z_hi, core = ctx // 4, (ctx // 2) % 2, ctx % 2
     z_lo, x = tp // 4, tp % 4
@@ -350,6 +341,44 @@
         send(i, tp, whole, TO_L, SAME_R, left)
         send(i, tp, whole, TO_Z, FAR_C, far)
 
+    def send_block(p, zh, semaphore, lands, device):
+        ref = blocks.at[p, zh, core]
+        copy = remote(ref, ref, semaphore, lands, device)
+        copy.start()
+        sent.append(copy)
+
+    def block_arrives(p, zh, whose, lands):
+        ref = blocks.at[p, zh, whose]
+        remote(ref, ref, block_send.at[0], lands, sibling).wait_recv()
+
+    def start_blocks():
+        blocks[y, z_hi, core] = weight_ref[...]
+        send_block(y, z_hi, block_send.at[0], block_z_recv, across)
+        for i in range(STEPS - 1):
+            send_block(y, z_hi, block_send.at[1 + i], block_y_recv.at[0, i], plane((y + 3 - i) % 4))
+        send_block(y, z_hi, block_send.at[7], block_core_recv.at[0, STEPS - 1], sibling)
+
+    def pass_blocks():
+        block_arrives(y, 1 - z_hi, core, block_z_recv)
+        for i in range(STEPS - 1):
+            send_block(
+                y, 1 - z_hi, block_send.at[4 + i], block_y_recv.at[1, i], plane((y + 3 - i) % 4)
+            )
+        send_block(y, 1 - z_hi, block_send.at[8], block_core_recv.at[1, STEPS - 1], sibling)
+
+    def share_blocks(i):
+        for side in range(2):
+            zh = z_hi if side == 0 else 1 - z_hi
+            block_arrives(owner(i), zh, core, block_y_recv.at[side, i])
+            send_block(
+                owner(i), zh, block_send.at[9 + 2 * i + side], block_core_recv.at[side, i], sibling
+            )
+
+    def blocks_ready(i):
+        for side in range(2):
+            zh = z_hi if side == 0 else 1 - z_hi
+            block_arrives(owner(i), zh, 1 - core, block_core_recv.at[side, i])
+
     def first_hops(i):
         if i % 2 == 0:
             arrive(i, there + x, whole, FAR_C)
@@ -397,12 +426,10 @@
         lax.fori_loop(0, 2, one, 0)
 
     def heads_partial(i):
-        weight_rows = pl.ds(pl.multiple_of(owner(i) * chunk, chunk), chunk)
-
         def one(r, carry):
             tall = pl.ds(pl.multiple_of(r * 2 * tokens, 2 * tokens), 2 * tokens)
             left_side = pieces[i, pl.ds(2 * r, 2)].reshape(2 * tokens, chunk)
-            value = mm(left_side, weight_ref[weight_rows, :])
+            value = mm(left_side, blocks[owner(i)].reshape(chunk, blocks.shape[-1]))
             if i > 0:
                 value = value + total[tall, :]
             if i < STEPS - 1:
@@ -420,6 +447,7 @@
         weight_partial(i, 0)
         for hops, other in between:
             hops(other)
+        blocks_ready(i)
         heads_partial(i)
         to_core.wait()
         if i < STEPS - 1:
@@ -432,16 +460,19 @@
 
     start_own(0)
     start_own(1)
+    start_blocks()
     first_hops(0)
+    pass_blocks()
     first_hops(1)
     second_hops(0)
     start_own(2)
     second_hops(1)
     start_own(3)
+    share_blocks(0)
     arrivals(0)
-    multiply(0)
+    multiply(0, ((share_blocks, 1),))
     arrivals(1)
-    multiply(1, ((first_hops, 2), (first_hops, 3)))
+    multiply(1, ((first_hops, 2), (first_hops, 3), (share_blocks, 2)))
     second_hops(2)
     second_hops(3)
     arrivals(2)
@@ -491,8 +522,10 @@
             pltpu.VMEM((STEPS - 1, 2, rows, columns), bf16),
             pltpu.VMEM((rows, columns), bf16),
             pltpu.VMEM((rows, columns), bf16),
+            pltpu.VMEM((STEPS, 2, 2, rows, columns), bf16),
             dma((STEPS, 9)), dma((STEPS, 9)), dma((STEPS,)), dma((STEPS,)),
             dma((STEPS - 1,)), dma((STEPS - 1,)), dma, dma,
+            dma((15,)), dma((2, STEPS - 1)), dma((2, STEPS)), dma,
         ],
         compiler_params=pltpu.CompilerParams(
             collective_id=0, has_side_effects=True, vmem_limit_bytes=48 * MIB),
@@ -524,27 +557,20 @@
     width = features // BLOCKS
     gain = norm_gain.reshape(1, features)
     rounded_weights = route_weights.astype(jnp.bfloat16).astype(jnp.float32)
-    send_rows, send_cots = dispatch(
-        expert_ids.T, rounded_weights.T, hidden_in, gain, grad_out, experts
-    )
+    ids_t, weights_t = expert_ids.T, rounded_weights.T
+    send_rows = dispatch(True, ids_t, weights_t, hidden_in, gain, experts)
+    send_cots = dispatch(False, ids_t, weights_t, grad_out, gain, experts)
     raw_rows = exchange(send_rows.reshape(devices, CHUNK, width)).reshape(-1, width)
     raw_cots = exchange(send_cots.reshape(devices, CHUNK, width)).reshape(-1, width)
     slot_rows = unpack_chunks(raw_rows)
-    full_weight = lax.all_gather(out_weight, "ctx", axis=0, tiled=True)
     gate_pre = mm(slot_rows, w_gate[0])
     up_value = mm(slot_rows, w_up[0])
-    gate_pre, full_weight = lax.optimization_barrier((gate_pre, full_weight))
     grads, slot_cots, activated, gate_grad, up_grad, dots = expert_back(
         raw_cots, gate_pre, up_value, w_gate[0], w_up[0], w_down[0]
     )
     back = exchange(grads.reshape(devices, CHUNK, width)).reshape(-1, width)
-    lanes = 128
-    sent_dots = jnp.pad(dots.reshape(-1, lanes), ((0, 2), (0, 0))).astype(jnp.bfloat16)
-    all_dots = lax.all_gather(sent_dots, axes, axis=0, tiled=True)
-    me = lax.axis_index(axes)
-    back_dots = lax.dynamic_slice(
-        all_dots.reshape(devices, -1), (0, me * CAP), (devices, CAP)
-    ).astype(jnp.float32)
+    back, dots = lax.optimization_barrier((back, dots))
+    back_dots = exchange(dots.reshape(devices, CAP).astype(jnp.bfloat16)).astype(jnp.float32)
     down_wgrad = mm(activated, slot_cots, CONTRACT_FIRST).astype(jnp.bfloat16)
     gate_wgrad = mm(slot_rows, gate_grad, CONTRACT_FIRST).astype(jnp.bfloat16)
     up_wgrad = mm(slot_rows, up_grad, CONTRACT_FIRST).astype(jnp.bfloat16)
@@ -560,7 +586,7 @@
         jnp.sum(jnp.where(at_rank, picked, 0.0), axis=1).reshape(tokens, -1) / rounded_weights
     )
 
-    heads_grad, weight_grad = project(resid_grad, ctx_heads, full_weight, lax.axis_size("tp"))
+    heads_grad, weight_grad = project(resid_grad, ctx_heads, out_weight, lax.axis_size("tp"))
     return (
         heads_grad,
         weight_grad,

time: 755 us -> 426 us (0.56); the launches traced: 746 us -> 425 us
  blocking collectives: 378 us -> 0 us
  waiting for transfers between devices: 159 us -> 195 us
  Pallas kernels: 123 us -> 143 us
  between operations: 14.3 us -> 0.89 us
  starting transfers between devices: 33.3 us -> 42.8 us
    all_gather x1 -> x0, blocking collectives: 378 us -> none  [per_device(): all_dots = lax.all_gather(sent_dots, axes, axis=0, tiled=True)]
    all_gather x1 -> x0, waiting for transfers between devices: 77.9 us -> none  [per_device(): full_weight = lax.all_gather(out_weight, 'ctx', axis=0, tiled=True)]
    all_to_all x1, waiting for transfers between devices: 0.01 us -> 62.3 us  [per_device(): exchange(send_cots.reshape(devices, CHUNK, width)).reshape(-1, width)]
    all_to_all x1, waiting for transfers between devices: 0.01 us -> 60.6 us  [per_device(): back = exchange(grads.reshape(devices, CHUNK, width)).reshape(-1, width)]
    pallas_call x1, Pallas kernels: 69.6 us -> 89.1 us  [project(): pl.pallas_call(project_kernel, in_specs=[vmem] * 3, out_specs=[vmem] * 2,...]
    all_to_all x0 -> x1, starting transfers between devices: none -> 10.1 us  [per_device(): exchange(dots.reshape(devices, CAP).astype(jnp.bfloat16))]
    all_to_all x1, waiting for transfers between devices: 80.4 us -> 72.2 us  [per_device(): exchange(send_rows.reshape(devices, CHUNK, width)).reshape(-1, width)]
  transfers between devices with their start and end apart: 4 -> 4, of which waited for: 2 -> 3; matrix products, arithmetic and copies ran while one was open for 4% -> 6% of each run, Pallas kernels for 1% -> 27%
where the time goes in v4:
time: 426 us; the launch traced here: 425 us
  waiting for transfers between devices  195 us (46%)
  Pallas kernels  143 us (34%)
  starting transfers between devices  42.8 us (10%)
  matrix products  26.2 us (6%)
  local copies, waits for them, and re-layouts  13.6 us (3%)
    pallas_call x1, Pallas kernels, project(): pl.pallas_call(project_kernel, in_specs=[vmem] * 3, out_specs=[vmem] * 2,...  89.1 us
    all_to_all x1, waiting for transfers between devices, per_device(): exchange(send_rows.reshape(devices, CHUNK, width)).reshape(-1, width)  72.2 us
    all_to_all x1, waiting for transfers between devices, per_device(): exchange(send_cots.reshape(devices, CHUNK, width)).reshape(-1, width)  62.3 us
    all_to_all x1, waiting for transfers between devices, per_device(): back = exchange(grads.reshape(devices, CHUNK, width)).reshape(-1, width)  60.6 us
    dot_general x5, matrix products, mm(): return lax.dot_general(a, b, dims, preferred_element_type=jnp.float32)  26 us
    pallas_call x1, Pallas kernels, expert_back(): pl.pallas_call(back_kernel, grid=(steps,), in_specs=[tall((total // steps...  24.2 us
    pallas_call x1, Pallas kernels, combine(): pl.pallas_call(combine_kernel, grid=(steps,), in_specs=[whole(ids.shape),...  12.4 us
    unnamed x43, local copies, waits for them, and re-layouts  12.1 us
  transfers between devices with their start and end apart: 4, of which 3 were waited for; matrix products, arithmetic and copies ran while one was open for 6% of the time, Pallas kernels for 27%

profile of v4, /device:TPU:0, one launch (start us, length us, event | category | flops | bytes accessed | tf_op | source)
XLA Modules:
  0.0 424.9 jit_solution(16831168685869708178)
XLA Ops:
  2.0 1.2 copy-done.6
  3.9 4.7 %dispatch_rows.1 = bf16[64,2,48,512]{3,2,1,0:T(8,128)(2,1)S(1)} custom-call(s32[2,128]{1,0:T(2,128)S(1)} %bitcast.48, f32[2,128]{1,0:T(2,128)S(1)} %convert_bitcast_fusion.weight_ref, bf16[128,4096]{1,0:T(8,128)(2,1)S(1)} %copy-done.6, f32[1,4096]{1,0:T(1,128)S(1)} %bitcast.50), custom_call_target="tpu_custom_call" | custom-call | flops 3221225472 | bytes 8388608 | tf_op jit(solution)/shard_map/dispatch_rows/pallas_call | solution.py:83
  8.7 2.6 copy-done.2
  11.3 11.6 %all-to-all-start.1 = ((bf16[128,48,512]{2,1,0:T(8,128)(2,1)}), bf16[128,48,512]{2,1,0:T(8,128)(2,1)}, u32[]{:S(2)}, u32[]{:S(2)}) async-start(bf16[128,48,512]{2,1,0:T(8,128)(2,1)} %bitcast.47), calls=%async_computation.1 | async-start | bytes 12582912 | tf_op jit(solution)/shard_map/all_to_all | solution.py:563
  23.0 4.6 %dispatch_cots.1 = bf16[64,2,48,512]{3,2,1,0:T(8,128)(2,1)S(1)} custom-call(s32[2,128]{1,0:T(2,128)S(1)} %bitcast.49, f32[2,128]{1,0:T(2,128)S(1)} %convert_bitcast_fusion.weight_ref, bf16[128,4096]{1,0:T(8,128)(2,1)S(1)} %copy-done.5, f32[1,4096]{1,0:T(1,128)S(1)} %bitcast.51), custom_call_target="tpu_custom_call" | custom-call | flops 3221225472 | bytes 8388608 | tf_op jit(solution)/shard_map/dispatch_cots/pallas_call | solution.py:83
  27.6 2.6 copy-done.1
  30.2 72.2 %all-to-all-done.1 = bf16[128,48,512]{2,1,0:T(8,128)(2,1)} async-done(((bf16[128,48,512]{2,1,0:T(8,128)(2,1)}), bf16[128,48,512]{2,1,0:T(8,128)(2,1)}, u32[]{:S(2)}, u32[]{:S(2)}) %all-to-all-start.1) | async-done | bytes 6291488 | tf_op jit(solution)/shard_map/all_to_all | solution.py:563
  102.4 10.3 %all-to-all-start = ((bf16[128,48,512]{2,1,0:T(8,128)(2,1)}), bf16[128,48,512]{2,1,0:T(8,128)(2,1)}, u32[]{:S(2)}, u32[]{:S(2)}) async-start(bf16[128,48,512]{2,1,0:T(8,128)(2,1)} %bitcast.46), calls=%async_computation | async-start | bytes 12582912 | tf_op jit(solution)/shard_map/all_to_all | solution.py:564
  112.7 8.0 %unpack.1 = bf16[768,4096]{1,0:T(8,128)(2,1)S(1)} custom-call(bf16[6144,512]{1,0:T(8,128)(2,1)} %bitcast.6.raw_ref), custom_call_target="tpu_custom_call" | custom-call | flops 2415919104 | bytes 12582912 | tf_op jit(solution)/shard_map/unpack/pallas_call | solution.py:137
  120.7 4.4 %fusion.10.gate_ref = f32[768,384]{1,0:T(8,128)} fusion(bf16[768,4096]{1,0:T(8,128)(2,1)S(1)} %unpack.1, bf16[1,4096,384]{2,1,0:T(8,128)(2,1)S(1)} %copy-done.14), kind=kOutput, calls=%fused_computation.25 | convolution fusion | flops 2415919104 | bytes 10616832 | tf_op jit(solution)/shard_map/dot_general | solution.py:24
  125.2 4.4 %fusion.8.up_ref = f32[768,384]{1,0:T(8,128)} fusion(bf16[768,4096]{1,0:T(8,128)(2,1)S(1)} %unpack.1, bf16[1,4096,384]{2,1,0:T(8,128)(2,1)S(1)} %copy-done.15), kind=kOutput, calls=%fused_computation.23 | convolution fusion | flops 2415919104 | bytes 10616832 | tf_op jit(solution)/shard_map/dot_general | solution.py:24
  129.6 62.3 %all-to-all-done = bf16[128,48,512]{2,1,0:T(8,128)(2,1)} async-done(((bf16[128,48,512]{2,1,0:T(8,128)(2,1)}), bf16[128,48,512]{2,1,0:T(8,128)(2,1)}, u32[]{:S(2)}, u32[]{:S(2)}) %all-to-all-start) | async-done | bytes 6291488 | tf_op jit(solution)/shard_map/all_to_all | solution.py:564
  191.9 24.2 %expert_back.1 = (bf16[6144,512]{1,0:T(8,128)(2,1)}, bf16[768,4096]{1,0:T(8,128)(2,1)}, bf16[768,384]{1,0:T(8,128)(2,1)}, bf16[768,384]{1,0:T(8,128)(2,1)}, bf16[768,384]{1,0:T(8,128)(2,1)}, /*index=5*/f32[768,1]{1,0:T(8,128)}) custom-call(bf16[6144,512]{1,0:T(8,128)(2,1)} %bitcast.4.raw_ref, f32[768,384]{1,0:T(8,128)} %fusion.10.gate_ref, ...), custom_call_target="tpu_custom_call" | custom-call | flops 12079595520 | bytes 33554432 | tf_op jit(solution)/shard_map/expert_back/pallas_call | solution.py:195
  216.1 10.8 %all-to-all-start.2 = ((bf16[128,48,512]{2,1,0:T(8,128)(2,1)}), bf16[128,48,512]{2,1,0:T(8,128)(2,1)}, u32[]{:S(2)}, u32[]{:S(2)}) async-start(bf16[128,48,512]{2,1,0:T(8,128)(2,1)} %bitcast.53), calls=%async_computation.2 | async-start | bytes 12582912 | tf_op jit(solution)/shard_map/all_to_all | solution.py:571
  228.3 7.4 %fusion.2 = bf16[1,384,4096]{2,1,0:T(8,128)(2,1)} fusion(bf16[768,384]{1,0:T(8,128)(2,1)} %get-tuple-element.25, bf16[768,4096]{1,0:T(8,128)(2,1)} %get-tuple-element.26), kind=kOutput, calls=%fused_computation.5 | convolution fusion | flops 2417491968 | bytes 10027008 | tf_op jit(solution)/shard_map/dot_general | solution.py:24
  235.7 4.9 %fusion.1 = bf16[1,4096,384]{2,1,0:T(8,128)(2,1)} fusion(bf16[768,4096]{1,0:T(8,128)(2,1)S(1)} %bitcast.45, bf16[768,384]{1,0:T(8,128)(2,1)S(1)} %copy-done.17), kind=kOutput, calls=%fused_computation.4 | convolution fusion | flops 2417491968 | bytes 10027008 | tf_op jit(solution)/shard_map/dot_general | solution.py:24
  240.6 4.8 %fusion = bf16[1,4096,384]{2,1,0:T(8,128)(2,1)} fusion(bf16[768,4096]{1,0:T(8,128)(2,1)S(1)} %bitcast.45, bf16[768,384]{1,0:T(8,128)(2,1)S(1)} %copy-done.16), kind=kOutput, calls=%fused_computation.3 | convolution fusion | flops 2417491968 | bytes 10027008 | tf_op jit(solution)/shard_map/dot_general | solution.py:24
  245.4 60.6 %all-to-all-done.2 = bf16[128,48,512]{2,1,0:T(8,128)(2,1)} async-done(((bf16[128,48,512]{2,1,0:T(8,128)(2,1)}), bf16[128,48,512]{2,1,0:T(8,128)(2,1)}, u32[]{:S(2)}, u32[]{:S(2)}) %all-to-all-start.2) | async-done | bytes 6291488 | tf_op jit(solution)/shard_map/all_to_all | solution.py:571
  306.0 1.2 convert_reduce_fusion
  308.0 10.1 %all-to-all-start.3 = ((bf16[128,1,6]{2,1,0:T(2,128)(2,1)}), bf16[128,1,6]{2,1,0:T(2,128)(2,1)S(1)}, u32[]{:S(2)}, u32[]{:S(2)}) async-start(bf16[128,1,6]{2,1,0:T(2,128)(2,1)} %convert_element_type.62), calls=%async_computation.3 | async-start | bytes 131072 | tf_op jit(solution)/shard_map/all_to_all | solution.py:573
  318.1 1.2 copy-done.7
  319.3 12.4 %combine.1.resid_ref = bf16[128,4096]{1,0:T(8,128)(2,1)} custom-call(s32[128,2]{1,0:T(8,128)S(1)} %copy.23.ids_ref, bf16[6144,512]{1,0:T(8,128)(2,1)} %bitcast.11.back_ref, bf16[128,4096]{1,0:T(8,128)(2,1)S(1)} %copy-done.7, f32[1,4096]{1,0:T(1,128)S(1)} %bitcast.52, bf16[128,4096]{1,0:T(8,128)(2,1)S(1)} %copy-done.5), custom_call_target="tpu_custom_call" | custom-call | flops 6442450944 | bytes 12582912 | tf_op jit(solution)/shard_map/combine/pallas_call | solution.py:269
  331.7 1.2 copy-done.12
  333.0 89.1 %project.1 = (bf16[1024,512]{1,0:T(8,128)(2,1)S(1)}, bf16[256,512]{1,0:T(8,128)(2,1)S(1)}) custom-call(bf16[128,4096]{1,0:T(8,128)(2,1)S(1)} %copy-done.12, bf16[1024,512]{1,0:T(8,128)(2,1)S(1)} %copy-done.8, bf16[256,512]{1,0:T(8,128)(2,1)S(1)} %copy-done.9), custom_call_target="tpu_custom_call" | custom-call | flops 8589934592 | bytes 8388608 | tf_op jit(solution)/shard_map/project/pallas_call | solution.py:511
  (56 shorter events, 7.2 us)
Async XLA Ops:
  1.3 0.7 copy-start.3
  2.0 1.2 copy-start.6
  3.2 0.7 copy-start.10
  8.7 2.7 copy-start.2
  11.3 11.6 %copy-start.4 = (s32[128,2]{0,1:T(2,128)S(1)}, s32[128,2]{0,1:T(2,128)}, u32[]{:S(2)}) copy-start(s32[128,2]{0,1:T(2,128)} %param.14) | copy-start | bytes 3076
  11.3 11.6 %copy-start.5 = (bf16[128,4096]{1,0:T(8,128)(2,1)S(1)}, bf16[128,4096]{1,0:T(8,128)(2,1)}, u32[]{:S(2)}) copy-start(bf16[128,4096]{1,0:T(8,128)(2,1)} %cot_ref.1) | copy-start | bytes 3145732
  11.3 11.6 %copy-start.11 = (f32[4096]{0:T(1024)S(1)}, f32[4096]{0:T(1024)}, u32[]{:S(2)}) copy-start(f32[4096]{0:T(1024)} %param.13) | copy-start | bytes 49156
  11.3 91.0 %all-to-all-start.1 = ((bf16[128,48,512]{2,1,0:T(8,128)(2,1)}), bf16[128,48,512]{2,1,0:T(8,128)(2,1)}, u32[]{:S(2)}, u32[]{:S(2)}) async-start(bf16[128,48,512]{2,1,0:T(8,128)(2,1)} %bitcast.47), calls=%async_computation.1 | async-start | bytes 12582912 | tf_op jit(solution)/shard_map/all_to_all | solution.py:563
  27.6 2.6 copy-start.1
  102.4 89.5 %all-to-all-start = ((bf16[128,48,512]{2,1,0:T(8,128)(2,1)}), bf16[128,48,512]{2,1,0:T(8,128)(2,1)}, u32[]{:S(2)}, u32[]{:S(2)}) async-start(bf16[128,48,512]{2,1,0:T(8,128)(2,1)} %bitcast.46), calls=%async_computation | async-start | bytes 12582912 | tf_op jit(solution)/shard_map/all_to_all | solution.py:564
  112.7 8.0 %copy-start.14 = (bf16[1,4096,384]{2,1,0:T(8,128)(2,1)S(1)}, bf16[1,4096,384]{2,1,0:T(8,128)(2,1)}, u32[]{:S(2)}) copy-start(bf16[1,4096,384]{2,1,0:T(8,128)(2,1)} %param.16) | copy-start | bytes 9437188
  120.7 4.4 %copy-start = (bf16[768,4096]{1,0:T(8,128)(2,1)}, bf16[768,4096]{1,0:T(8,128)(2,1)S(1)}, u32[]{:S(2)}) copy-start(bf16[768,4096]{1,0:T(8,128)(2,1)S(1)} %unpack.1) | copy-start | bytes 18874372
  120.7 4.4 %copy-start.15 = (bf16[1,4096,384]{2,1,0:T(8,128)(2,1)S(1)}, bf16[1,4096,384]{2,1,0:T(8,128)(2,1)}, u32[]{:S(2)}) copy-start(bf16[1,4096,384]{2,1,0:T(8,128)(2,1)} %param.17) | copy-start | bytes 9437188
  216.1 89.9 %all-to-all-start.2 = ((bf16[128,48,512]{2,1,0:T(8,128)(2,1)}), bf16[128,48,512]{2,1,0:T(8,128)(2,1)}, u32[]{:S(2)}, u32[]{:S(2)}) async-start(bf16[128,48,512]{2,1,0:T(8,128)(2,1)} %bitcast.53), calls=%async_computation.2 | async-start | bytes 12582912 | tf_op jit(solution)/shard_map/all_to_all | solution.py:571
  227.3 8.4 %slice-start = ((s8[6291456]{0:T(1024)(128)(4,1)}), s8[2097152]{0:T(1024)(128)(4,1)S(1)}, s32[]{:S(2)}) async-start(s8[6291456]{0:T(1024)(128)(4,1)} %bitcast.44), calls=%async_computation.4 | async-start | bytes 4194304
  228.1 7.6 %copy-start.17 = (bf16[768,384]{1,0:T(8,128)(2,1)S(1)}, bf16[768,384]{1,0:T(8,128)(2,1)}, u32[]{:S(2)}) copy-start(bf16[768,384]{1,0:T(8,128)(2,1)} %get-tuple-element.24) | copy-start | bytes 1769476
  228.2 7.4 %slice-start.1 = ((s8[6291456]{0:T(1024)(128)(4,1)}), s8[4194304]{0:T(1024)(128)(4,1)S(1)}, s32[]{:S(2)}) async-start(s8[6291456]{0:T(1024)(128)(4,1)} %bitcast.44), calls=%async_computation.5 | async-start | bytes 8388608
  235.7 4.9 %copy-start.16 = (bf16[768,384]{1,0:T(8,128)(2,1)S(1)}, bf16[768,384]{1,0:T(8,128)(2,1)}, u32[]{:S(2)}) copy-start(bf16[768,384]{1,0:T(8,128)(2,1)} %get-tuple-element.23) | copy-start | bytes 1769476
  308.0 114.0 %all-to-all-start.3 = ((bf16[128,1,6]{2,1,0:T(2,128)(2,1)}), bf16[128,1,6]{2,1,0:T(2,128)(2,1)S(1)}, u32[]{:S(2)}, u32[]{:S(2)}) async-start(bf16[128,1,6]{2,1,0:T(2,128)(2,1)} %convert_element_type.62), calls=%async_computation.3 | async-start | bytes 131072 | tf_op jit(solution)/shard_map/all_to_all | solution.py:573
  318.1 1.2 copy-start.7
  319.3 12.4 %copy-start.8 = (bf16[1024,512]{1,0:T(8,128)(2,1)S(1)}, bf16[1024,512]{1,0:T(8,128)(2,1)}, u32[]{:S(2)}) copy-start(bf16[1024,512]{1,0:T(8,128)(2,1)} %heads_ref.1) | copy-start | bytes 3145732
  319.3 12.4 %copy-start.9 = (bf16[256,512]{1,0:T(8,128)(2,1)S(1)}, bf16[256,512]{1,0:T(8,128)(2,1)}, u32[]{:S(2)}) copy-start(bf16[256,512]{1,0:T(8,128)(2,1)} %weight_ref.1) | copy-start | bytes 786436
  331.7 1.2 copy-start.12
  333.0 89.7 %copy-start.13 = (f32[128,2]{0,1:T(2,128)S(1)}, f32[128,2]{0,1:T(2,128)}, u32[]{:S(2)}) copy-start(f32[128,2]{0,1:T(2,128)} %param.15) | copy-start | bytes 3076

commit v5 on v4

--- a/solution.py
+++ b/solution.py
@@ -9,7 +9,7 @@
 
 EPSILON = 1e-06
 CAP = 6
-BLOCKS = 8
+BLOCKS = 4
 CHUNK = CAP * BLOCKS
 CONTRACT_FIRST = (((0,), (0,)), ((), ()))
 CONTRACT_LAST = (((1,), (1,)), ((), ()))
@@ -69,8 +69,8 @@
     stacked = jnp.concatenate(
         [flat[here, b * width:(b + 1) * width] for b in range(BLOCKS)], axis=0
     )
-    chunks = mm(unpack[...], stacked, CONTRACT_FIRST).astype(jnp.bfloat16)
-    chunks = chunks.reshape(group, CHUNK, width)
+    chunks = mm(unpack[...], stacked, CONTRACT_FIRST).reshape(group, CHUNK, width)
+    chunks = chunks.astype(jnp.bfloat16)
     for half in range(2):
         out_ref[:, half] = chunks
 
@@ -90,7 +90,7 @@
             pltpu.VMEM((experts * CAP, features), jnp.bfloat16),
             pltpu.VMEM((group * CHUNK, group * CHUNK), jnp.bfloat16),
         ],
-        compiler_params=pltpu.CompilerParams(vmem_limit_bytes=32 * MIB),
+        compiler_params=pltpu.CompilerParams(vmem_limit_bytes=60 * MIB),
         cost_estimate=pl.CostEstimate(
             flops=2 * experts * CHUNK * tokens * features, bytes_accessed=8 * MIB,
             transcendentals=0),
@@ -262,7 +262,7 @@
             ).astype(jnp.bfloat16)
 
 
-def combine(ids, back, hidden, gain, cots, experts, steps=8):
+def combine(ids, back, hidden, gain, cots, experts, steps=4):
     tokens, features = hidden.shape
     total, width = back.shape
     whole = lambda shape: pl.BlockSpec(shape, lambda i: (0, 0))
@@ -447,42 +447,41 @@
         weight_partial(i, 0)
         for hops, other in between:
             hops(other)
+        if i == STEPS - 1:
+            return to_core
         blocks_ready(i)
         heads_partial(i)
         to_core.wait()
-        if i < STEPS - 1:
-            summed[i] = (
-                partial[i, 0].astype(jnp.float32) + from_core[i].astype(jnp.float32)
-            ).astype(jnp.bfloat16)
-            copy = remote(summed.at[i], from_y.at[i], y_send.at[i], y_recv.at[i], plane(owner(i)))
-            copy.start()
-            sent.append(copy)
+        summed[i] = (
+            partial[i, 0].astype(jnp.float32) + from_core[i].astype(jnp.float32)
+        ).astype(jnp.bfloat16)
+        copy = remote(summed.at[i], from_y.at[i], y_send.at[i], y_recv.at[i], plane(owner(i)))
+        copy.start()
+        sent.append(copy)
 
     start_own(0)
     start_own(1)
     start_blocks()
     first_hops(0)
+    first_hops(1)
     pass_blocks()
-    first_hops(1)
+    start_own(2)
     second_hops(0)
-    start_own(2)
     second_hops(1)
     start_own(3)
-    share_blocks(0)
+    first_hops(2)
     arrivals(0)
-    multiply(0, ((share_blocks, 1),))
+    multiply(0, ((first_hops, 3), (share_blocks, 0)))
+    second_hops(2)
     arrivals(1)
-    multiply(1, ((first_hops, 2), (first_hops, 3), (share_blocks, 2)))
-    second_hops(2)
-    second_hops(3)
+    multiply(1, ((second_hops, 3), (share_blocks, 1)))
+    share_blocks(2)
     arrivals(2)
     multiply(2)
     arrivals(3)
-    multiply(3)
+    to_core = multiply(3)
 
     last = STEPS - 1
-    for i in range(last):
-        remote(summed.at[i], from_y.at[i], y_send.at[i], y_recv.at[i], across).wait_recv()
 
     def reduced(zh):
         value = partial[last, 0, zh].astype(jnp.float32) + from_core[last, zh].astype(jnp.float32)
@@ -490,9 +489,14 @@
             value = value + from_y[i, zh].astype(jnp.float32)
         return value
 
+    to_core.wait()
+    for i in range(last):
+        remote(summed.at[i], from_y.at[i], y_send.at[i], y_recv.at[i], across).wait_recv()
     to_z[...] = reduced(1 - z_hi).astype(jnp.bfloat16)
     copy = remote(to_z, from_z, z_send, z_recv, across)
     copy.start()
+    blocks_ready(last)
+    heads_partial(last)
     own = reduced(z_hi)
     copy.wait()
     out_weight_ref[...] = (own + from_z[...].astype(jnp.float32)).astype(jnp.bfloat16)

time: 426 us -> 421 us (0.988)
  local copies, waits for them, and re-layouts: 13.6 us -> 6.98 us
    unnamed x43 -> x33, local copies, waits for them, and re-layouts: 12.1 us -> 5.51 us
    pallas_call x2, Pallas kernels: 9.32 us -> 15.4 us  [dispatch(): pl.pallas_call(functools.partial(dispatch_kernel, normalize), grid=(exper...]
  transfers between devices with their start and end apart: 4 -> 4, of which waited for: 3 -> 3; matrix products, arithmetic and copies ran while one was open for 6% -> 7% of each run, Pallas kernels for 27% -> 27%
where the time goes in v5:
time: 421 us; the launch traced here: 420 us
  waiting for transfers between devices  195 us (46%)
  Pallas kernels  143 us (34%)
  starting transfers between devices  42.8 us (10%)
  matrix products  27.1 us (6%)
  local copies, waits for them, and re-layouts  6.98 us (2%)
    pallas_call x1, Pallas kernels, project(): pl.pallas_call(project_kernel, in_specs=[vmem] * 3, out_specs=[vmem] * 2,...  91.5 us
    all_to_all x1, waiting for transfers between devices, per_device(): exchange(send_rows.reshape(devices, CHUNK, width)).reshape(-1, width)  71.8 us
    all_to_all x1, waiting for transfers between devices, per_device(): exchange(send_cots.reshape(devices, CHUNK, width)).reshape(-1, width)  63.4 us
    all_to_all x1, waiting for transfers between devices, per_device(): back = exchange(grads.reshape(devices, CHUNK, width)).reshape(-1, width)  59.6 us
    dot_general x5, matrix products, mm(): return lax.dot_general(a, b, dims, preferred_element_type=jnp.float32)  26.9 us
    pallas_call x1, Pallas kernels, expert_back(): pl.pallas_call(back_kernel, grid=(steps,), in_specs=[tall((total // steps...  20.9 us
    pallas_call x2, Pallas kernels, dispatch(): pl.pallas_call(functools.partial(dispatch_kernel, normalize), grid=(exper...  15.4 us
    all_to_all x1, starting transfers between devices, per_device(): exchange(send_rows.reshape(devices, CHUNK, width)).reshape(-1, width)  11.6 us
  transfers between devices with their start and end apart: 4, of which 3 were waited for; matrix products, arithmetic and copies ran while one was open for 7% of the time, Pallas kernels for 27%

profile of v5, /device:TPU:0, one launch (start us, length us, event | category | flops | bytes accessed | tf_op | source)
XLA Modules:
  0.0 419.6 jit_solution(1473973220387229719)
XLA Ops:
  0.6 1.2 convert_bitcast_fusion.weight_ref
  1.9 7.8 %dispatch_rows.1 = bf16[64,2,24,1024]{3,2,1,0:T(8,128)(2,1)} custom-call(s32[2,128]{1,0:T(2,128)} %bitcast.53, f32[2,128]{1,0:T(2,128)} %convert_bitcast_fusion.weight_ref, bf16[128,4096]{1,0:T(8,128)(2,1)} %hidden_ref.1, f32[1,4096]{1,0:T(1,128)} %bitcast.46), custom_call_target="tpu_custom_call" | custom-call | flops 1610612736 | bytes 8388608 | tf_op jit(solution)/shard_map/dispatch_rows/pallas_call | solution.py:83
  9.7 11.6 %all-to-all-start.1 = ((bf16[128,24,1024]{2,1,0:T(8,128)(2,1)}), bf16[128,24,1024]{2,1,0:T(8,128)(2,1)}, u32[]{:S(2)}, u32[]{:S(2)}) async-start(bf16[128,24,1024]{2,1,0:T(8,128)(2,1)} %bitcast.50), calls=%async_computation.1 | async-start | bytes 12582912 | tf_op jit(solution)/shard_map/all_to_all | solution.py:567
  21.3 7.6 %dispatch_cots.1 = bf16[64,2,24,1024]{3,2,1,0:T(8,128)(2,1)} custom-call(s32[2,128]{1,0:T(2,128)} %bitcast.54, f32[2,128]{1,0:T(2,128)} %convert_bitcast_fusion.weight_ref, bf16[128,4096]{1,0:T(8,128)(2,1)} %cot_ref.1, f32[1,4096]{1,0:T(1,128)} %bitcast.47), custom_call_target="tpu_custom_call" | custom-call | flops 1610612736 | bytes 8388608 | tf_op jit(solution)/shard_map/dispatch_cots/pallas_call | solution.py:83
  28.9 71.8 %all-to-all-done.1 = bf16[128,24,1024]{2,1,0:T(8,128)(2,1)} async-done(((bf16[128,24,1024]{2,1,0:T(8,128)(2,1)}), bf16[128,24,1024]{2,1,0:T(8,128)(2,1)}, u32[]{:S(2)}, u32[]{:S(2)}) %all-to-all-start.1) | async-done | bytes 6291488 | tf_op jit(solution)/shard_map/all_to_all | solution.py:567
  100.7 10.3 %all-to-all-start = ((bf16[128,24,1024]{2,1,0:T(8,128)(2,1)}), bf16[128,24,1024]{2,1,0:T(8,128)(2,1)}, u32[]{:S(2)}, u32[]{:S(2)}) async-start(bf16[128,24,1024]{2,1,0:T(8,128)(2,1)} %bitcast.49), calls=%async_computation | async-start | bytes 12582912 | tf_op jit(solution)/shard_map/all_to_all | solution.py:568
  111.0 6.8 %unpack.1 = bf16[768,4096]{1,0:T(8,128)(2,1)S(1)} custom-call(bf16[3072,1024]{1,0:T(8,128)(2,1)} %bitcast.6.raw_ref), custom_call_target="tpu_custom_call" | custom-call | flops 1207959552 | bytes 12582912 | tf_op jit(solution)/shard_map/unpack/pallas_call | solution.py:137
  117.9 4.4 %fusion.10.gate_ref = f32[768,384]{1,0:T(8,128)} fusion(bf16[768,4096]{1,0:T(8,128)(2,1)S(1)} %unpack.1, bf16[1,4096,384]{2,1,0:T(8,128)(2,1)S(1)} %copy-done.10), kind=kOutput, calls=%fused_computation.25 | convolution fusion | flops 2415919104 | bytes 10616832 | tf_op jit(solution)/shard_map/dot_general | solution.py:24
  122.3 4.4 %fusion.8.up_ref = f32[768,384]{1,0:T(8,128)} fusion(bf16[768,4096]{1,0:T(8,128)(2,1)S(1)} %unpack.1, bf16[1,4096,384]{2,1,0:T(8,128)(2,1)S(1)} %copy-done.11), kind=kOutput, calls=%fused_computation.23 | convolution fusion | flops 2415919104 | bytes 10616832 | tf_op jit(solution)/shard_map/dot_general | solution.py:24
  126.7 63.4 %all-to-all-done = bf16[128,24,1024]{2,1,0:T(8,128)(2,1)} async-done(((bf16[128,24,1024]{2,1,0:T(8,128)(2,1)}), bf16[128,24,1024]{2,1,0:T(8,128)(2,1)}, u32[]{:S(2)}, u32[]{:S(2)}) %all-to-all-start) | async-done | bytes 6291488 | tf_op jit(solution)/shard_map/all_to_all | solution.py:568
  190.2 20.9 %expert_back.1 = (bf16[3072,1024]{1,0:T(8,128)(2,1)}, bf16[768,4096]{1,0:T(8,128)(2,1)}, bf16[768,384]{1,0:T(8,128)(2,1)}, bf16[768,384]{1,0:T(8,128)(2,1)}, bf16[768,384]{1,0:T(8,128)(2,1)}, /*index=5*/f32[768,1]{1,0:T(8,128)}) custom-call(bf16[3072,1024]{1,0:T(8,128)(2,1)} %bitcast.4.raw_ref, f32[768,384]{1,0:T(8,128)} %fusion.10.gate_ref, ...), custom_call_target="tpu_custom_call" | custom-call | flops 9663676416 | bytes 33554432 | tf_op jit(solution)/shard_map/expert_back/pallas_call | solution.py:195
  211.1 10.8 %all-to-all-start.2 = ((bf16[128,24,1024]{2,1,0:T(8,128)(2,1)}), bf16[128,24,1024]{2,1,0:T(8,128)(2,1)}, u32[]{:S(2)}, u32[]{:S(2)}) async-start(bf16[128,24,1024]{2,1,0:T(8,128)(2,1)} %bitcast.51), calls=%async_computation.2 | async-start | bytes 12582912 | tf_op jit(solution)/shard_map/all_to_all | solution.py:575
  223.3 7.3 %fusion.2 = bf16[1,384,4096]{2,1,0:T(8,128)(2,1)} fusion(bf16[768,384]{1,0:T(8,128)(2,1)S(1)} %copy-done.7, bf16[768,4096]{1,0:T(8,128)(2,1)} %get-tuple-element.26), kind=kOutput, calls=%fused_computation.5 | convolution fusion | flops 2417491968 | bytes 10027008 | tf_op jit(solution)/shard_map/dot_general | solution.py:24
  230.6 6.0 %fusion.1 = bf16[1,4096,384]{2,1,0:T(8,128)(2,1)} fusion(bf16[768,4096]{1,0:T(8,128)(2,1)S(1)} %bitcast.45, bf16[768,384]{1,0:T(8,128)(2,1)} %get-tuple-element.24), kind=kOutput, calls=%fused_computation.4 | convolution fusion | flops 2417491968 | bytes 10027008 | tf_op jit(solution)/shard_map/dot_general | solution.py:24
  236.6 4.8 %fusion = bf16[1,4096,384]{2,1,0:T(8,128)(2,1)} fusion(bf16[768,4096]{1,0:T(8,128)(2,1)S(1)} %bitcast.45, bf16[768,384]{1,0:T(8,128)(2,1)S(1)} %copy-done.12), kind=kOutput, calls=%fused_computation.3 | convolution fusion | flops 2417491968 | bytes 10027008 | tf_op jit(solution)/shard_map/dot_general | solution.py:24
  241.4 59.6 %all-to-all-done.2 = bf16[128,24,1024]{2,1,0:T(8,128)(2,1)} async-done(((bf16[128,24,1024]{2,1,0:T(8,128)(2,1)}), bf16[128,24,1024]{2,1,0:T(8,128)(2,1)}, u32[]{:S(2)}, u32[]{:S(2)}) %all-to-all-start.2) | async-done | bytes 6291488 | tf_op jit(solution)/shard_map/all_to_all | solution.py:575
  301.0 1.2 convert_reduce_fusion
  303.0 10.1 %all-to-all-start.3 = ((bf16[128,1,6]{2,1,0:T(2,128)(2,1)}), bf16[128,1,6]{2,1,0:T(2,128)(2,1)S(1)}, u32[]{:S(2)}, u32[]{:S(2)}) async-start(bf16[128,1,6]{2,1,0:T(2,128)(2,1)} %convert_element_type.62), calls=%async_computation.3 | async-start | bytes 131072 | tf_op jit(solution)/shard_map/all_to_all | solution.py:577
  313.1 1.2 copy-done.2
  314.4 8.4 %combine.1.resid_ref = bf16[128,4096]{1,0:T(8,128)(2,1)} custom-call(s32[128,2]{1,0:T(8,128)S(1)} %copy.23.ids_ref, bf16[3072,1024]{1,0:T(8,128)(2,1)} %bitcast.11.back_ref, bf16[128,4096]{1,0:T(8,128)(2,1)S(1)} %copy-done.2, f32[1,4096]{1,0:T(1,128)S(1)} %bitcast.48, bf16[128,4096]{1,0:T(8,128)(2,1)S(1)} %copy-done.1), custom_call_target="tpu_custom_call" | custom-call | flops 3221225472 | bytes 12582912 | tf_op jit(solution)/shard_map/combine/pallas_call | solution.py:269
  322.8 1.2 copy-done.4
  324.0 1.2 copy-done.6
  325.2 91.5 %project.1 = (bf16[1024,512]{1,0:T(8,128)(2,1)S(1)}, bf16[256,512]{1,0:T(8,128)(2,1)S(1)}) custom-call(bf16[128,4096]{1,0:T(8,128)(2,1)S(1)} %copy-done.6, bf16[1024,512]{1,0:T(8,128)(2,1)S(1)} %copy-done.4, bf16[256,512]{1,0:T(8,128)(2,1)S(1)} %copy-done.5), custom_call_target="tpu_custom_call" | custom-call | flops 8589934592 | bytes 8388608 | tf_op jit(solution)/shard_map/project/pallas_call | solution.py:515
  418.0 1.0 copy.33
  (46 shorter events, 4.1 us)
Async XLA Ops:
  9.7 91.0 %all-to-all-start.1 = ((bf16[128,24,1024]{2,1,0:T(8,128)(2,1)}), bf16[128,24,1024]{2,1,0:T(8,128)(2,1)}, u32[]{:S(2)}, u32[]{:S(2)}) async-start(bf16[128,24,1024]{2,1,0:T(8,128)(2,1)} %bitcast.50), calls=%async_computation.1 | async-start | bytes 12582912 | tf_op jit(solution)/shard_map/all_to_all | solution.py:567
  100.7 89.5 %all-to-all-start = ((bf16[128,24,1024]{2,1,0:T(8,128)(2,1)}), bf16[128,24,1024]{2,1,0:T(8,128)(2,1)}, u32[]{:S(2)}, u32[]{:S(2)}) async-start(bf16[128,24,1024]{2,1,0:T(8,128)(2,1)} %bitcast.49), calls=%async_computation | async-start | bytes 12582912 | tf_op jit(solution)/shard_map/all_to_all | solution.py:568
  111.0 6.9 %copy-start.10 = (bf16[1,4096,384]{2,1,0:T(8,128)(2,1)S(1)}, bf16[1,4096,384]{2,1,0:T(8,128)(2,1)}, u32[]{:S(2)}) copy-start(bf16[1,4096,384]{2,1,0:T(8,128)(2,1)} %param.16) | copy-start | bytes 9437188
  117.9 4.4 %copy-start = (bf16[768,4096]{1,0:T(8,128)(2,1)}, bf16[768,4096]{1,0:T(8,128)(2,1)S(1)}, u32[]{:S(2)}) copy-start(bf16[768,4096]{1,0:T(8,128)(2,1)S(1)} %unpack.1) | copy-start | bytes 18874372
  117.9 4.4 %copy-start.11 = (bf16[1,4096,384]{2,1,0:T(8,128)(2,1)S(1)}, bf16[1,4096,384]{2,1,0:T(8,128)(2,1)}, u32[]{:S(2)}) copy-start(bf16[1,4096,384]{2,1,0:T(8,128)(2,1)} %param.17) | copy-start | bytes 9437188
  211.1 10.8 %copy-start.8 = (s32[128,2]{0,1:T(2,128)S(1)}, s32[128,2]{0,1:T(2,128)}, u32[]{:S(2)}) copy-start(s32[128,2]{0,1:T(2,128)} %param.14) | copy-start | bytes 3076
  211.1 12.2 %copy-start.7 = (bf16[768,384]{1,0:T(8,128)(2,1)S(1)}, bf16[768,384]{1,0:T(8,128)(2,1)}, u32[]{:S(2)}) copy-start(bf16[768,384]{1,0:T(8,128)(2,1)} %get-tuple-element.25) | copy-start | bytes 1769476
  211.1 89.9 %all-to-all-start.2 = ((bf16[128,24,1024]{2,1,0:T(8,128)(2,1)}), bf16[128,24,1024]{2,1,0:T(8,128)(2,1)}, u32[]{:S(2)}, u32[]{:S(2)}) async-start(bf16[128,24,1024]{2,1,0:T(8,128)(2,1)} %bitcast.51), calls=%async_computation.2 | async-start | bytes 12582912 | tf_op jit(solution)/shard_map/all_to_all | solution.py:575
  222.3 8.2 %slice-start = ((s8[6291456]{0:T(1024)(128)(4,1)}), s8[2097152]{0:T(1024)(128)(4,1)S(1)}, s32[]{:S(2)}) async-start(s8[6291456]{0:T(1024)(128)(4,1)} %bitcast.44), calls=%async_computation.4 | async-start | bytes 4194304
  223.3 7.3 %slice-start.1 = ((s8[6291456]{0:T(1024)(128)(4,1)}), s8[4194304]{0:T(1024)(128)(4,1)S(1)}, s32[]{:S(2)}) async-start(s8[6291456]{0:T(1024)(128)(4,1)} %bitcast.44), calls=%async_computation.5 | async-start | bytes 8388608
  230.6 6.0 %copy-start.12 = (bf16[768,384]{1,0:T(8,128)(2,1)S(1)}, bf16[768,384]{1,0:T(8,128)(2,1)}, u32[]{:S(2)}) copy-start(bf16[768,384]{1,0:T(8,128)(2,1)} %get-tuple-element.23) | copy-start | bytes 1769476
  236.5 76.6 %copy-start.1 = (bf16[128,4096]{1,0:T(8,128)(2,1)S(1)}, bf16[128,4096]{1,0:T(8,128)(2,1)}, u32[]{:S(2)}) copy-start(bf16[128,4096]{1,0:T(8,128)(2,1)} %cot_ref.1) | copy-start | bytes 3145732
  236.5 76.6 %copy-start.3 = (f32[4096]{0:T(1024)S(1)}, f32[4096]{0:T(1024)}, u32[]{:S(2)}) copy-start(f32[4096]{0:T(1024)} %param.13) | copy-start | bytes 49156
  241.4 81.4 %copy-start.5 = (bf16[256,512]{1,0:T(8,128)(2,1)S(1)}, bf16[256,512]{1,0:T(8,128)(2,1)}, u32[]{:S(2)}) copy-start(bf16[256,512]{1,0:T(8,128)(2,1)} %weight_ref.1) | copy-start | bytes 786436
  303.0 113.7 %all-to-all-start.3 = ((bf16[128,1,6]{2,1,0:T(2,128)(2,1)}), bf16[128,1,6]{2,1,0:T(2,128)(2,1)S(1)}, u32[]{:S(2)}, u32[]{:S(2)}) async-start(bf16[128,1,6]{2,1,0:T(2,128)(2,1)} %convert_element_type.62), calls=%async_computation.3 | async-start | bytes 131072 | tf_op jit(solution)/shard_map/all_to_all | solution.py:577
  313.1 1.2 copy-start.2
  322.8 1.2 copy-start.4
  324.0 1.2 copy-start.6
  325.2 92.1 %copy-start.9 = (f32[128,2]{0,1:T(2,128)S(1)}, f32[128,2]{0,1:T(2,128)}, u32[]{:S(2)}) copy-start(f32[128,2]{0,1:T(2,128)} %param.15) | copy-start | bytes 3076

commit v6 on v5

--- a/solution.py
+++ b/solution.py
@@ -275,7 +275,7 @@
         out_shape=jax.ShapeDtypeStruct(hidden.shape, jnp.bfloat16),
         scratch_shapes=[pltpu.VMEM((tokens, experts), jnp.bfloat16),
                         pltpu.VMEM((BLOCKS * tokens, width), jnp.float32)],
-        compiler_params=pltpu.CompilerParams(vmem_limit_bytes=40 * MIB),
+        compiler_params=pltpu.CompilerParams(vmem_limit_bytes=61 * MIB),
         cost_estimate=pl.CostEstimate(
             flops=2 * BLOCKS * tokens * total * width, bytes_accessed=12 * MIB, transcendentals=0),
         name="combine",
@@ -287,10 +287,15 @@
 TO_Z, TO_R, TO_L, PASS_R, PASS_L, EXTRA_A, EXTRA_B, EXTRA_C, EXTRA_D = range(9)
 
 
-def project_kernel(resid_ref, heads_ref, weight_ref, out_heads_ref, out_weight_ref,
-                   pieces, total, partial, from_core, summed, from_y, to_z, from_z, blocks,
+EXTRA = 16
+
+
+def project_kernel(resid_ref, heads_ref, weight_ref, dots_ref,
+                   out_heads_ref, out_weight_ref, out_dots_ref,
+                   heads, heads_t, dots_all, dots_rows, pieces, total, partial, from_core, summed, from_y, to_z, from_z, blocks,
                    piece_send, piece_recv, core_send, core_recv, y_send, y_recv, z_send, z_recv,
-                   block_send, block_y_recv, block_core_recv, block_z_recv):
+                   block_send, block_y_recv, block_core_recv, block_z_recv,
+                   local, dots_send, dots_recv):
     ctx, tp = lax.axis_index("ctx"), lax.axis_index("tp")
     y, z_hi, core = ctx // 4, (ctx // 2) % 2, ctx % 2
     z_lo, x = tp // 4, tp % 4
@@ -306,8 +311,23 @@
     half = tokens // 2
     group = pieces.shape[1]
 
+    columns = heads.shape[1]
+
+    def owner(i):
+        return (y + 1 + i) % 4
+
+    def fetch(i):
+        lanes = pl.ds(pl.multiple_of(owner(i) * chunk, chunk), chunk)
+        return pltpu.make_async_copy(resid_ref.at[:, lanes], pieces.at[i, tp], local.at[i])
+
+    fetch_heads = pltpu.make_async_copy(heads_ref, heads, local.at[STEPS])
+    for i in range(STEPS):
+        fetch(i).start()
+    fetch_heads.start()
+
     barrier = pltpu.get_barrier_semaphore()
-    peers = [right, left, far, sibling, across] + [plane((y + d) % 4) for d in (1, 2, 3)]
+    peers = [(ctx, (tp + d) % group) for d in range(1, group)]
+    peers += [sibling, across] + [plane((y + d) % 4) for d in (1, 2, 3)]
     for peer in peers:
         pl.semaphore_signal(barrier, inc=1, device_id=peer, device_id_type=pl.DeviceIdType.MESH)
     pl.semaphore_wait(barrier, len(peers))
@@ -331,12 +351,8 @@
         ref = pieces.at[i, piece, part]
         remote(ref, ref, piece_send.at[i, 0], piece_recv.at[i, lands], far).wait_recv()
 
-    def owner(i):
-        return (y + 1 + i) % 4
-
     def start_own(i):
-        columns = pl.ds(pl.multiple_of(owner(i) * chunk, chunk), chunk)
-        pieces[i, tp] = resid_ref[:, columns]
+        fetch(i).wait()
         send(i, tp, whole, TO_R, SAME_L, right)
         send(i, tp, whole, TO_L, SAME_R, left)
         send(i, tp, whole, TO_Z, FAR_C, far)
@@ -416,11 +432,51 @@
         arrive(i, there + opposite_x, top, FAR_T)
         arrive(i, there + opposite_x, bottom, FAR_B)
 
+    def start_dots():
+        dots_all[tp] = dots_ref[...]
+        for d in range(1, group):
+            ref = dots_all.at[tp]
+            copy = remote(
+                ref, ref, dots_send.at[d - 1], dots_recv.at[d - 1], (ctx, (tp + d) % group)
+            )
+            copy.start()
+            sent.append(copy)
+
+    def gather_dots():
+        for d in range(1, group):
+            ref = dots_all.at[(tp + group - d) % group]
+            remote(ref, ref, dots_send.at[0], dots_recv.at[d - 1], far).wait_recv()
+        sources = dots_all.shape[2]
+        count = group * EXTRA
+        table = dots_all[...].reshape(count, sources)
+        mine = iota((16, sources), 1) == iota((16, sources), 0) * group + tp
+        mine = jnp.where(mine, 1.0, 0.0).astype(jnp.bfloat16)
+        held = mm(mine, table, CONTRACT_LAST).astype(jnp.bfloat16)
+        row, lane = iota((count, 2 * rows), 0), iota((count, 2 * rows), 1)
+        device = row // EXTRA
+        slot = row - device * EXTRA
+        place = jnp.where(slot < CAP, (ctx * 4 + device // 2) * CAP + slot, -1)
+        spread = jnp.where(lane == place, 1.0, 0.0).astype(jnp.bfloat16)
+        dots_rows[...] = mm(held, spread)
+
+    def turn_heads():
+        fetch_heads.wait()
+        for r in range(4):
+            part = heads.shape[0] // 4
+            heads_t[:, r * part:(r + 1) * part] = heads[r * part:(r + 1) * part, :].T
+
     def weight_partial(i, whose):
         def one(zh, carry):
-            first = pl.multiple_of((2 * zh + (core if whose == 0 else 1 - core)) * rows, rows)
-            left_side = pieces[i, :, :, pl.ds(first, rows)].reshape(group * tokens, rows)
-            partial[i, whose, zh] = mm(left_side, heads_ref[...], CONTRACT_FIRST).astype(jnp.bfloat16)
+            local_owner = 2 * zh + (core if whose == 0 else 1 - core)
+            first = pl.multiple_of(local_owner * rows, rows)
+            right_side = pieces[i, :, :, pl.ds(first, rows)].reshape(group * tokens, rows)
+            value = mm(heads_t[...], right_side)
+            partial[i, whose, zh, 0:columns] = value.astype(jnp.bfloat16)
+            at = iota((16, 2 * rows), 0) == owner(i) * 4 + local_owner
+            line = jnp.sum(jnp.where(at, dots_rows[...], 0.0), axis=0, keepdims=True)
+            row = iota((EXTRA, rows), 0)
+            tail = jnp.where(row == 0, line[:, :rows], jnp.where(row == 1, line[:, rows:], 0.0))
+            partial[i, whose, zh, columns:columns + EXTRA] = tail.astype(jnp.bfloat16)
             return carry
 
         lax.fori_loop(0, 2, one, 0)
@@ -461,7 +517,9 @@
 
     start_own(0)
     start_own(1)
+    start_dots()
     start_blocks()
+    turn_heads()
     first_hops(0)
     first_hops(1)
     pass_blocks()
@@ -469,6 +527,7 @@
     second_hops(0)
     second_hops(1)
     start_own(3)
+    gather_dots()
     first_hops(2)
     arrivals(0)
     multiply(0, ((first_hops, 3), (share_blocks, 0)))
@@ -499,44 +558,54 @@
     heads_partial(last)
     own = reduced(z_hi)
     copy.wait()
-    out_weight_ref[...] = (own + from_z[...].astype(jnp.float32)).astype(jnp.bfloat16)
+    own = own + from_z[...].astype(jnp.float32)
+    out_weight_ref[...] = own[:columns].T.astype(jnp.bfloat16)
+    out_dots_ref[...] = own[columns:]
     for copy in sent:
         copy.wait_send()
 
 
-def project(resid, heads, weight, group):
+def project(resid, heads, weight, dots, group):
     tokens, features = resid.shape
     columns = heads.shape[1]
     chunk = features // STEPS
     rows = chunk // 4
+    tall = columns + EXTRA
     bf16 = jnp.bfloat16
     dma = pltpu.SemaphoreType.DMA
     vmem = pl.BlockSpec(memory_space=pltpu.VMEM)
+    anywhere = pl.BlockSpec(memory_space=pltpu.HBM)
     return pl.pallas_call(
         project_kernel,
-        in_specs=[vmem] * 3,
-        out_specs=[vmem] * 2,
-        out_shape=[jax.ShapeDtypeStruct(heads.shape, bf16), jax.ShapeDtypeStruct((rows, columns), bf16)],
+        in_specs=[anywhere, anywhere, vmem, vmem],
+        out_specs=[vmem] * 3,
+        out_shape=[jax.ShapeDtypeStruct(heads.shape, bf16), jax.ShapeDtypeStruct((rows, columns), bf16),
+                   jax.ShapeDtypeStruct((EXTRA, rows), jnp.float32)],
         scratch_shapes=[
+            pltpu.VMEM(heads.shape, bf16),
+            pltpu.VMEM(heads.shape[::-1], bf16),
+            pltpu.VMEM((group,) + dots.shape, bf16),
+            pltpu.VMEM((16, 2 * rows), jnp.float32),
             pltpu.VMEM((STEPS, group, tokens, chunk), bf16),
             pltpu.VMEM(heads.shape, jnp.float32),
-            pltpu.VMEM((STEPS, 2, 2, rows, columns), bf16),
-            pltpu.VMEM((STEPS, 2, rows, columns), bf16),
-            pltpu.VMEM((STEPS - 1, 2, rows, columns), bf16),
-            pltpu.VMEM((STEPS - 1, 2, rows, columns), bf16),
-            pltpu.VMEM((rows, columns), bf16),
-            pltpu.VMEM((rows, columns), bf16),
+            pltpu.VMEM((STEPS, 2, 2, tall, rows), bf16),
+            pltpu.VMEM((STEPS, 2, tall, rows), bf16),
+            pltpu.VMEM((STEPS - 1, 2, tall, rows), bf16),
+            pltpu.VMEM((STEPS - 1, 2, tall, rows), bf16),
+            pltpu.VMEM((tall, rows), bf16),
+            pltpu.VMEM((tall, rows), bf16),
             pltpu.VMEM((STEPS, 2, 2, rows, columns), bf16),
             dma((STEPS, 9)), dma((STEPS, 9)), dma((STEPS,)), dma((STEPS,)),
             dma((STEPS - 1,)), dma((STEPS - 1,)), dma, dma,
             dma((15,)), dma((2, STEPS - 1)), dma((2, STEPS)), dma,
+            dma((STEPS + 1,)), dma((group - 1,)), dma((group - 1,)),
         ],
         compiler_params=pltpu.CompilerParams(
-            collective_id=0, has_side_effects=True, vmem_limit_bytes=48 * MIB),
+            collective_id=0, has_side_effects=True, vmem_limit_bytes=61 * MIB + MIB // 2),
         cost_estimate=pl.CostEstimate(
             flops=4 * group * tokens * features * columns, bytes_accessed=8 * MIB, transcendentals=0),
         name="project",
-    )(resid, heads, weight)
+    )(resid, heads, weight, dots)
 
 
 def per_device(
@@ -573,24 +642,24 @@
         raw_cots, gate_pre, up_value, w_gate[0], w_up[0], w_down[0]
     )
     back = exchange(grads.reshape(devices, CHUNK, width)).reshape(-1, width)
-    back, dots = lax.optimization_barrier((back, dots))
-    back_dots = exchange(dots.reshape(devices, CAP).astype(jnp.bfloat16)).astype(jnp.float32)
+    sent_dots = jnp.pad(dots.reshape(devices, CAP).T, ((0, EXTRA - CAP), (0, 0)))
     down_wgrad = mm(activated, slot_cots, CONTRACT_FIRST).astype(jnp.bfloat16)
     gate_wgrad = mm(slot_rows, gate_grad, CONTRACT_FIRST).astype(jnp.bfloat16)
     up_wgrad = mm(slot_rows, up_grad, CONTRACT_FIRST).astype(jnp.bfloat16)
     resid_grad = combine(expert_ids, back, hidden_in, gain, grad_out, experts)
 
+    heads_grad, weight_grad, summed_dots = project(
+        resid_grad, ctx_heads, out_weight, sent_dots.astype(jnp.bfloat16), lax.axis_size("tp")
+    )
+    summed_dots = summed_dots[:2].reshape(-1)[:experts * CAP].reshape(experts, CAP)
     flat_ids = expert_ids.reshape(-1)
     onehot = (flat_ids[:, None] == jnp.arange(experts, dtype=jnp.int32)[None, :]).astype(jnp.int32)
     slot_rank = jnp.sum((jnp.cumsum(onehot, axis=0) - onehot) * onehot, axis=1)
-    summed_dots = back_dots.reshape(experts, 2, CAP).sum(axis=1)
     picked = jnp.dot(onehot.astype(jnp.float32), summed_dots, precision=lax.Precision.HIGHEST)
     at_rank = slot_rank[:, None] == jnp.arange(CAP, dtype=jnp.int32)[None, :]
     route_grads = (
         jnp.sum(jnp.where(at_rank, picked, 0.0), axis=1).reshape(tokens, -1) / rounded_weights
     )
-
-    heads_grad, weight_grad = project(resid_grad, ctx_heads, out_weight, lax.axis_size("tp"))
     return (
         heads_grad,
         weight_grad,

time: 421 us -> 413 us (0.981)
  starting transfers between devices: 42.8 us -> 32.7 us
  Pallas kernels: 143 us -> 148 us
    all_to_all x1 -> x0, starting transfers between devices: 10.1 us -> none  [per_device(): exchange(dots.reshape(devices, CAP).astype(jnp.bfloat16))]
    pallas_call x1, Pallas kernels: 91.5 us -> 95.9 us  [project(): pl.pallas_call(project_kernel, in_specs=[anywhere, anywhere, vmem, vmem],...]
  transfers between devices with their start and end apart: 4 -> 3, of which waited for: 3 -> 3; matrix products, arithmetic and copies ran while one was open for 7% -> 7% of each run, Pallas kernels for 27% -> 4%
where the time goes in v6:
time: 413 us; the launch traced here: 412 us
  waiting for transfers between devices  195 us (47%)
  Pallas kernels  148 us (36%)
  starting transfers between devices  32.7 us (8%)
  matrix products  26 us (6%)
  local copies, waits for them, and re-layouts  6.45 us (2%)
    pallas_call x1, Pallas kernels, project(): pl.pallas_call(project_kernel, in_specs=[anywhere, anywhere, vmem, vmem],...  95.9 us
    all_to_all x1, waiting for transfers between devices, per_device(): exchange(send_rows.reshape(devices, CHUNK, width)).reshape(-1, width)  71.8 us
    all_to_all x1, waiting for transfers between devices, per_device(): exchange(send_cots.reshape(devices, CHUNK, width)).reshape(-1, width)  63.5 us
    all_to_all x1, waiting for transfers between devices, per_device(): back = exchange(grads.reshape(devices, CHUNK, width)).reshape(-1, width)  59.7 us
    dot_general x5, matrix products, mm(): return lax.dot_general(a, b, dims, preferred_element_type=jnp.float32)  25.8 us
    pallas_call x1, Pallas kernels, expert_back(): pl.pallas_call(back_kernel, grid=(steps,), in_specs=[tall((total // steps...  20.9 us
    pallas_call x2, Pallas kernels, dispatch(): pl.pallas_call(functools.partial(dispatch_kernel, normalize), grid=(exper...  15.4 us
    all_to_all x1, starting transfers between devices, per_device(): exchange(send_rows.reshape(devices, CHUNK, width)).reshape(-1, width)  11.6 us
  transfers between devices with their start and end apart: 3, of which 3 were waited for; matrix products, arithmetic and copies ran while one was open for 7% of the time, Pallas kernels for 4%

profile of v6, /device:TPU:0, one launch (start us, length us, event | category | flops | bytes accessed | tf_op | source)
XLA Modules:
  0.0 411.7 jit_solution(12936673084697574785)
XLA Ops:
  0.6 1.2 convert_bitcast_fusion.weight_ref
  1.9 7.7 %dispatch_rows.1 = bf16[64,2,24,1024]{3,2,1,0:T(8,128)(2,1)} custom-call(s32[2,128]{1,0:T(2,128)} %bitcast.56, f32[2,128]{1,0:T(2,128)} %convert_bitcast_fusion.weight_ref, bf16[128,4096]{1,0:T(8,128)(2,1)} %hidden_ref.1, f32[1,4096]{1,0:T(1,128)} %bitcast.53), custom_call_target="tpu_custom_call" | custom-call | flops 1610612736 | bytes 8388608 | tf_op jit(solution)/shard_map/dispatch_rows/pallas_call | solution.py:83
  9.6 11.6 %all-to-all-start.1 = ((bf16[128,24,1024]{2,1,0:T(8,128)(2,1)}), bf16[128,24,1024]{2,1,0:T(8,128)(2,1)}, u32[]{:S(2)}, u32[]{:S(2)}) async-start(bf16[128,24,1024]{2,1,0:T(8,128)(2,1)} %bitcast.51), calls=%async_computation.1 | async-start | bytes 12582912 | tf_op jit(solution)/shard_map/all_to_all | solution.py:636
  21.2 7.6 %dispatch_cots.1 = bf16[64,2,24,1024]{3,2,1,0:T(8,128)(2,1)} custom-call(s32[2,128]{1,0:T(2,128)} %bitcast.57, f32[2,128]{1,0:T(2,128)} %convert_bitcast_fusion.weight_ref, bf16[128,4096]{1,0:T(8,128)(2,1)} %cot_ref.1, f32[1,4096]{1,0:T(1,128)} %bitcast.54), custom_call_target="tpu_custom_call" | custom-call | flops 1610612736 | bytes 8388608 | tf_op jit(solution)/shard_map/dispatch_cots/pallas_call | solution.py:83
  28.9 71.8 %all-to-all-done.1 = bf16[128,24,1024]{2,1,0:T(8,128)(2,1)} async-done(((bf16[128,24,1024]{2,1,0:T(8,128)(2,1)}), bf16[128,24,1024]{2,1,0:T(8,128)(2,1)}, u32[]{:S(2)}, u32[]{:S(2)}) %all-to-all-start.1) | async-done | bytes 6291488 | tf_op jit(solution)/shard_map/all_to_all | solution.py:636
  100.6 10.3 %all-to-all-start = ((bf16[128,24,1024]{2,1,0:T(8,128)(2,1)}), bf16[128,24,1024]{2,1,0:T(8,128)(2,1)}, u32[]{:S(2)}, u32[]{:S(2)}) async-start(bf16[128,24,1024]{2,1,0:T(8,128)(2,1)} %bitcast.50), calls=%async_computation | async-start | bytes 12582912 | tf_op jit(solution)/shard_map/all_to_all | solution.py:637
  111.0 6.8 %unpack.1 = bf16[768,4096]{1,0:T(8,128)(2,1)S(1)} custom-call(bf16[3072,1024]{1,0:T(8,128)(2,1)} %bitcast.6.raw_ref), custom_call_target="tpu_custom_call" | custom-call | flops 1207959552 | bytes 12582912 | tf_op jit(solution)/shard_map/unpack/pallas_call | solution.py:137
  117.8 4.4 %fusion.10.gate_ref = f32[768,384]{1,0:T(8,128)} fusion(bf16[768,4096]{1,0:T(8,128)(2,1)S(1)} %unpack.1, bf16[1,4096,384]{2,1,0:T(8,128)(2,1)S(1)} %copy-done.6), kind=kOutput, calls=%fused_computation.26 | convolution fusion | flops 2415919104 | bytes 10616832 | tf_op jit(solution)/shard_map/dot_general | solution.py:24
  122.3 4.4 %fusion.8.up_ref = f32[768,384]{1,0:T(8,128)} fusion(bf16[768,4096]{1,0:T(8,128)(2,1)S(1)} %unpack.1, bf16[1,4096,384]{2,1,0:T(8,128)(2,1)S(1)} %copy-done.7), kind=kOutput, calls=%fused_computation.24 | convolution fusion | flops 2415919104 | bytes 10616832 | tf_op jit(solution)/shard_map/dot_general | solution.py:24
  126.7 63.5 %all-to-all-done = bf16[128,24,1024]{2,1,0:T(8,128)(2,1)} async-done(((bf16[128,24,1024]{2,1,0:T(8,128)(2,1)}), bf16[128,24,1024]{2,1,0:T(8,128)(2,1)}, u32[]{:S(2)}, u32[]{:S(2)}) %all-to-all-start) | async-done | bytes 6291488 | tf_op jit(solution)/shard_map/all_to_all | solution.py:637
  190.1 20.9 %expert_back.1 = (bf16[3072,1024]{1,0:T(8,128)(2,1)}, bf16[768,4096]{1,0:T(8,128)(2,1)}, bf16[768,384]{1,0:T(8,128)(2,1)}, bf16[768,384]{1,0:T(8,128)(2,1)}, bf16[768,384]{1,0:T(8,128)(2,1)}, /*index=5*/f32[768,1]{1,0:T(8,128)}) custom-call(bf16[3072,1024]{1,0:T(8,128)(2,1)} %bitcast.4.raw_ref, f32[768,384]{1,0:T(8,128)} %fusion.10.gate_ref, ...), custom_call_target="tpu_custom_call" | custom-call | flops 9663676416 | bytes 33554432 | tf_op jit(solution)/shard_map/expert_back/pallas_call | solution.py:195
  211.1 10.8 %all-to-all-start.2 = ((bf16[128,24,1024]{2,1,0:T(8,128)(2,1)}), bf16[128,24,1024]{2,1,0:T(8,128)(2,1)}, u32[]{:S(2)}, u32[]{:S(2)}) async-start(bf16[128,24,1024]{2,1,0:T(8,128)(2,1)} %bitcast.52), calls=%async_computation.2 | async-start | bytes 12582912 | tf_op jit(solution)/shard_map/all_to_all | solution.py:644
  222.3 0.6 reduce-window.6
  223.6 0.6 pad.5.dots_ref
  224.3 7.3 %fusion.2 = bf16[1,384,4096]{2,1,0:T(8,128)(2,1)} fusion(bf16[768,384]{1,0:T(8,128)(2,1)S(1)} %copy-done.1, bf16[768,4096]{1,0:T(8,128)(2,1)} %get-tuple-element.24), kind=kOutput, calls=%fused_computation.5 | convolution fusion | flops 2417491968 | bytes 10027008 | tf_op jit(solution)/shard_map/dot_general | solution.py:24
  231.6 4.9 %fusion.1 = bf16[1,4096,384]{2,1,0:T(8,128)(2,1)} fusion(bf16[768,4096]{1,0:T(8,128)(2,1)S(1)} %bitcast.49, bf16[768,384]{1,0:T(8,128)(2,1)S(1)} %copy-done.9), kind=kOutput, calls=%fused_computation.4 | convolution fusion | flops 2417491968 | bytes 10027008 | tf_op jit(solution)/shard_map/dot_general | solution.py:24
  236.4 4.8 %fusion = bf16[1,4096,384]{2,1,0:T(8,128)(2,1)} fusion(bf16[768,4096]{1,0:T(8,128)(2,1)S(1)} %bitcast.49, bf16[768,384]{1,0:T(8,128)(2,1)S(1)} %copy-done.8), kind=kOutput, calls=%fused_computation.3 | convolution fusion | flops 2417491968 | bytes 10027008 | tf_op jit(solution)/shard_map/dot_general | solution.py:24
  241.3 59.7 %all-to-all-done.2 = bf16[128,24,1024]{2,1,0:T(8,128)(2,1)} async-done(((bf16[128,24,1024]{2,1,0:T(8,128)(2,1)}), bf16[128,24,1024]{2,1,0:T(8,128)(2,1)}, u32[]{:S(2)}, u32[]{:S(2)}) %all-to-all-start.2) | async-done | bytes 6291488 | tf_op jit(solution)/shard_map/all_to_all | solution.py:644
  301.0 9.1 %combine.1.resid_ref = bf16[128,4096]{1,0:T(8,128)(2,1)} custom-call(s32[128,2]{1,0:T(8,128)} %copy-done.2, bf16[3072,1024]{1,0:T(8,128)(2,1)} %bitcast.11.back_ref, bf16[128,4096]{1,0:T(8,128)(2,1)} %hidden_ref.1, f32[1,4096]{1,0:T(1,128)} %bitcast.55, bf16[128,4096]{1,0:T(8,128)(2,1)} %cot_ref.1), custom_call_target="tpu_custom_call" | custom-call | flops 3221225472 | bytes 12582912 | tf_op jit(solution)/shard_map/combine/pallas_call | solution.py:269
  310.1 95.9 %project.1 = (bf16[1024,512]{1,0:T(8,128)(2,1)}, bf16[256,512]{1,0:T(8,128)(2,1)}, f32[16,256]{1,0:T(8,128)}) custom-call(bf16[128,4096]{1,0:T(8,128)(2,1)} %combine.1.resid_ref, bf16[1024,512]{1,0:T(8,128)(2,1)} %heads_ref.1, bf16[256,512]{1,0:T(8,128)(2,1)} %weight_ref.1, bf16[16,128]{1,0:T(8,128)(2,1)} %pad.5.dots_ref), custom_call_target="tpu_custom_call" | custom-call | flops 8589934592 | bytes 8388608 | tf_op jit(solution)/shard_map/project/pallas_call | solution.py:578
  405.9 0.7 slice_bitcast_fusion
  407.2 0.6 convert_divide_fusion
  407.8 2.3 copy.29
  410.1 1.7 copy.30
  (41 shorter events, 1.8 us)
Async XLA Ops:
  9.6 91.0 %all-to-all-start.1 = ((bf16[128,24,1024]{2,1,0:T(8,128)(2,1)}), bf16[128,24,1024]{2,1,0:T(8,128)(2,1)}, u32[]{:S(2)}, u32[]{:S(2)}) async-start(bf16[128,24,1024]{2,1,0:T(8,128)(2,1)} %bitcast.51), calls=%async_computation.1 | async-start | bytes 12582912 | tf_op jit(solution)/shard_map/all_to_all | solution.py:636
  100.6 89.5 %all-to-all-start = ((bf16[128,24,1024]{2,1,0:T(8,128)(2,1)}), bf16[128,24,1024]{2,1,0:T(8,128)(2,1)}, u32[]{:S(2)}, u32[]{:S(2)}) async-start(bf16[128,24,1024]{2,1,0:T(8,128)(2,1)} %bitcast.50), calls=%async_computation | async-start | bytes 12582912 | tf_op jit(solution)/shard_map/all_to_all | solution.py:637
  111.0 6.9 %copy-start.6 = (bf16[1,4096,384]{2,1,0:T(8,128)(2,1)S(1)}, bf16[1,4096,384]{2,1,0:T(8,128)(2,1)}, u32[]{:S(2)}) copy-start(bf16[1,4096,384]{2,1,0:T(8,128)(2,1)} %param.16) | copy-start | bytes 9437188
  117.8 4.4 %copy-start = (bf16[768,4096]{1,0:T(8,128)(2,1)}, bf16[768,4096]{1,0:T(8,128)(2,1)S(1)}, u32[]{:S(2)}) copy-start(bf16[768,4096]{1,0:T(8,128)(2,1)S(1)} %unpack.1) | copy-start | bytes 18874372
  117.8 4.4 %copy-start.7 = (bf16[1,4096,384]{2,1,0:T(8,128)(2,1)S(1)}, bf16[1,4096,384]{2,1,0:T(8,128)(2,1)}, u32[]{:S(2)}) copy-start(bf16[1,4096,384]{2,1,0:T(8,128)(2,1)} %param.17) | copy-start | bytes 9437188
  211.0 10.8 %copy-start.4 = (s32[128,2]{0,1:T(2,128)S(1)}, s32[128,2]{0,1:T(2,128)}, u32[]{:S(2)}) copy-start(s32[128,2]{0,1:T(2,128)} %param.14) | copy-start | bytes 3076
  211.0 12.2 %copy-start.3 = (f32[768,1]{1,0:T(8,128)S(1)}, f32[768,1]{1,0:T(8,128)}, u32[]{:S(2)}) copy-start(f32[768,1]{1,0:T(8,128)} %get-tuple-element.17) | copy-start | bytes 9220
  211.0 13.2 %copy-start.1 = (bf16[768,384]{1,0:T(8,128)(2,1)S(1)}, bf16[768,384]{1,0:T(8,128)(2,1)}, u32[]{:S(2)}) copy-start(bf16[768,384]{1,0:T(8,128)(2,1)} %get-tuple-element.23) | copy-start | bytes 1769476
  211.1 89.9 %all-to-all-start.2 = ((bf16[128,24,1024]{2,1,0:T(8,128)(2,1)}), bf16[128,24,1024]{2,1,0:T(8,128)(2,1)}, u32[]{:S(2)}, u32[]{:S(2)}) async-start(bf16[128,24,1024]{2,1,0:T(8,128)(2,1)} %bitcast.52), calls=%async_computation.2 | async-start | bytes 12582912 | tf_op jit(solution)/shard_map/all_to_all | solution.py:644
  222.0 9.6 %copy-start.2 = (s32[128,2]{1,0:T(8,128)}, s32[128,2]{1,0:T(8,128)S(1)}, u32[]{:S(2)}) copy-start(s32[128,2]{1,0:T(8,128)S(1)} %copy.18.ids_ref) | copy-start | bytes 3076
  223.4 8.1 %slice-start = ((s8[6291456]{0:T(1024)(128)(4,1)}), s8[2097152]{0:T(1024)(128)(4,1)S(1)}, s32[]{:S(2)}) async-start(s8[6291456]{0:T(1024)(128)(4,1)} %bitcast.48), calls=%async_computation.3 | async-start | bytes 4194304
  223.4 8.1 %copy-start.9 = (bf16[768,384]{1,0:T(8,128)(2,1)S(1)}, bf16[768,384]{1,0:T(8,128)(2,1)}, u32[]{:S(2)}) copy-start(bf16[768,384]{1,0:T(8,128)(2,1)} %get-tuple-element.22) | copy-start | bytes 1769476
  224.3 7.3 %slice-start.1 = ((s8[6291456]{0:T(1024)(128)(4,1)}), s8[4194304]{0:T(1024)(128)(4,1)S(1)}, s32[]{:S(2)}) async-start(s8[6291456]{0:T(1024)(128)(4,1)} %bitcast.48), calls=%async_computation.4 | async-start | bytes 8388608
  231.6 4.9 %copy-start.8 = (bf16[768,384]{1,0:T(8,128)(2,1)S(1)}, bf16[768,384]{1,0:T(8,128)(2,1)}, u32[]{:S(2)}) copy-start(bf16[768,384]{1,0:T(8,128)(2,1)} %get-tuple-element.21) | copy-start | bytes 1769476
  310.1 97.2 %copy-start.5 = (f32[128,2]{0,1:T(2,128)S(1)}, f32[128,2]{0,1:T(2,128)}, u32[]{:S(2)}) copy-start(f32[128,2]{0,1:T(2,128)} %param.15) | copy-start | bytes 3076

commit v7 on v6

--- a/solution.py
+++ b/solution.py
@@ -41,9 +41,6 @@
         prior = mm(named.astype(jnp.bfloat16), earlier.astype(jnp.bfloat16))
         unpack[...] = unpack_matrix(group)
         slots = jnp.where(named > 0.5, prior, -1.0).astype(jnp.bfloat16)
-        weights = jnp.where(
-            first, weight_ref[0:1, :], jnp.where(second, weight_ref[1:2, :], 0.0)
-        ).astype(jnp.bfloat16)
         row = iota((experts * CAP, experts), 0)
         expert_of = row // CAP
         spread = jnp.where(expert_of == iota((experts * CAP, experts), 1), 1.0, 0.0)
@@ -56,6 +53,9 @@
             wide = value_ref[...].astype(jnp.float32)
             scale = lax.rsqrt(jnp.mean(wide * wide, axis=-1, keepdims=True) + EPSILON)
         else:
+            weights = jnp.where(
+                first, weight_ref[0:1, :], jnp.where(second, weight_ref[1:2, :], 0.0)
+            ).astype(jnp.bfloat16)
             picks = jnp.where(taken, mm(spread, weights), 0.0).astype(jnp.bfloat16)
         for block in range(BLOCKS):
             columns = slice(block * width, (block + 1) * width)
@@ -521,20 +521,20 @@
     start_blocks()
     turn_heads()
     first_hops(0)
+    pass_blocks()
     first_hops(1)
-    pass_blocks()
+    second_hops(0)
     start_own(2)
-    second_hops(0)
     second_hops(1)
     start_own(3)
     gather_dots()
-    first_hops(2)
+    share_blocks(0)
     arrivals(0)
-    multiply(0, ((first_hops, 3), (share_blocks, 0)))
+    multiply(0, ((share_blocks, 1),))
+    arrivals(1)
+    multiply(1, ((first_hops, 2), (first_hops, 3), (share_blocks, 2)))
     second_hops(2)
-    arrivals(1)
-    multiply(1, ((second_hops, 3), (share_blocks, 1)))
-    share_blocks(2)
+    second_hops(3)
     arrivals(2)
     multiply(2)
     arrivals(3)
@@ -601,7 +601,7 @@
             dma((STEPS + 1,)), dma((group - 1,)), dma((group - 1,)),
         ],
         compiler_params=pltpu.CompilerParams(
-            collective_id=0, has_side_effects=True, vmem_limit_bytes=61 * MIB + MIB // 2),
+            collective_id=0, has_side_effects=True, vmem_limit_bytes=61 * MIB),
         cost_estimate=pl.CostEstimate(
             flops=4 * group * tokens * features * columns, bytes_accessed=8 * MIB, transcendentals=0),
         name="project",
@@ -631,7 +631,7 @@
     gain = norm_gain.reshape(1, features)
     rounded_weights = route_weights.astype(jnp.bfloat16).astype(jnp.float32)
     ids_t, weights_t = expert_ids.T, rounded_weights.T
-    send_rows = dispatch(True, ids_t, weights_t, hidden_in, gain, experts)
+    send_rows = dispatch(True, ids_t, ids_t, hidden_in, gain, experts)
     send_cots = dispatch(False, ids_t, weights_t, grad_out, gain, experts)
     raw_rows = exchange(send_rows.reshape(devices, CHUNK, width)).reshape(-1, width)
     raw_cots = exchange(send_cots.reshape(devices, CHUNK, width)).reshape(-1, width)

time: 413 us -> 408 us (0.988)
  no operation moved by 1% of the time
where the time goes in v7:
time: 408 us
  waiting for transfers between devices  194 us (48%)
  Pallas kernels  145 us (36%)
  starting transfers between devices  32.7 us (8%)
  matrix products  26 us (6%)
  local copies, waits for them, and re-layouts  6.45 us (2%)
    pallas_call x1, Pallas kernels, project(): pl.pallas_call(project_kernel, in_specs=[anywhere, anywhere, vmem, vmem],...  92.9 us
    all_to_all x1, waiting for transfers between devices, per_device(): exchange(send_rows.reshape(devices, CHUNK, width)).reshape(-1, width)  71.2 us
    all_to_all x1, waiting for transfers between devices, per_device(): exchange(send_cots.reshape(devices, CHUNK, width)).reshape(-1, width)  63.4 us
    all_to_all x1, waiting for transfers between devices, per_device(): back = exchange(grads.reshape(devices, CHUNK, width)).reshape(-1, width)  59.7 us
    dot_general x5, matrix products, mm(): return lax.dot_general(a, b, dims, preferred_element_type=jnp.float32)  25.8 us
    pallas_call x1, Pallas kernels, expert_back(): pl.pallas_call(back_kernel, grid=(steps,), in_specs=[tall((total // steps...  20.9 us
    pallas_call x2, Pallas kernels, dispatch(): pl.pallas_call(functools.partial(dispatch_kernel, normalize), grid=(exper...  15.4 us
    all_to_all x1, starting transfers between devices, per_device(): exchange(send_rows.reshape(devices, CHUNK, width)).reshape(-1, width)  11.6 us
  transfers between devices with their start and end apart: 3, of which 3 were waited for; matrix products, arithmetic and copies ran while one was open for 7% of the time, Pallas kernels for 4%

profile of v7, /device:TPU:0, one launch (start us, length us, event | category | flops | bytes accessed | tf_op | source)
XLA Modules:
  0.0 407.6 jit_solution(7263133180872708041)
XLA Ops:
  0.6 7.8 %dispatch_rows.1 = bf16[64,2,24,1024]{3,2,1,0:T(8,128)(2,1)} custom-call(s32[2,128]{1,0:T(2,128)} %bitcast.56, s32[2,128]{1,0:T(2,128)} %bitcast.57, bf16[128,4096]{1,0:T(8,128)(2,1)} %hidden_ref.1, f32[1,4096]{1,0:T(1,128)} %bitcast.53), custom_call_target="tpu_custom_call" | custom-call | flops 1610612736 | bytes 8388608 | tf_op jit(solution)/shard_map/dispatch_rows/pallas_call | solution.py:83
  8.4 11.6 %all-to-all-start.1 = ((bf16[128,24,1024]{2,1,0:T(8,128)(2,1)}), bf16[128,24,1024]{2,1,0:T(8,128)(2,1)}, u32[]{:S(2)}, u32[]{:S(2)}) async-start(bf16[128,24,1024]{2,1,0:T(8,128)(2,1)} %bitcast.51), calls=%async_computation.1 | async-start | bytes 12582912 | tf_op jit(solution)/shard_map/all_to_all | solution.py:636
  20.0 0.6 convert_bitcast_fusion.weight_ref
  20.6 7.6 %dispatch_cots.1 = bf16[64,2,24,1024]{3,2,1,0:T(8,128)(2,1)} custom-call(s32[2,128]{1,0:T(2,128)} %bitcast.58, f32[2,128]{1,0:T(2,128)} %convert_bitcast_fusion.weight_ref, bf16[128,4096]{1,0:T(8,128)(2,1)} %cot_ref.1, f32[1,4096]{1,0:T(1,128)} %bitcast.54), custom_call_target="tpu_custom_call" | custom-call | flops 1610612736 | bytes 8388608 | tf_op jit(solution)/shard_map/dispatch_cots/pallas_call | solution.py:83
  28.2 71.2 %all-to-all-done.1 = bf16[128,24,1024]{2,1,0:T(8,128)(2,1)} async-done(((bf16[128,24,1024]{2,1,0:T(8,128)(2,1)}), bf16[128,24,1024]{2,1,0:T(8,128)(2,1)}, u32[]{:S(2)}, u32[]{:S(2)}) %all-to-all-start.1) | async-done | bytes 6291488 | tf_op jit(solution)/shard_map/all_to_all | solution.py:636
  99.4 10.3 %all-to-all-start = ((bf16[128,24,1024]{2,1,0:T(8,128)(2,1)}), bf16[128,24,1024]{2,1,0:T(8,128)(2,1)}, u32[]{:S(2)}, u32[]{:S(2)}) async-start(bf16[128,24,1024]{2,1,0:T(8,128)(2,1)} %bitcast.50), calls=%async_computation | async-start | bytes 12582912 | tf_op jit(solution)/shard_map/all_to_all | solution.py:637
  109.8 6.8 %unpack.1 = bf16[768,4096]{1,0:T(8,128)(2,1)S(1)} custom-call(bf16[3072,1024]{1,0:T(8,128)(2,1)} %bitcast.6.raw_ref), custom_call_target="tpu_custom_call" | custom-call | flops 1207959552 | bytes 12582912 | tf_op jit(solution)/shard_map/unpack/pallas_call | solution.py:137
  116.6 4.4 %fusion.10.gate_ref = f32[768,384]{1,0:T(8,128)} fusion(bf16[768,4096]{1,0:T(8,128)(2,1)S(1)} %unpack.1, bf16[1,4096,384]{2,1,0:T(8,128)(2,1)S(1)} %copy-done.6), kind=kOutput, calls=%fused_computation.26 | convolution fusion | flops 2415919104 | bytes 10616832 | tf_op jit(solution)/shard_map/dot_general | solution.py:24
  121.1 4.4 %fusion.8.up_ref = f32[768,384]{1,0:T(8,128)} fusion(bf16[768,4096]{1,0:T(8,128)(2,1)S(1)} %unpack.1, bf16[1,4096,384]{2,1,0:T(8,128)(2,1)S(1)} %copy-done.7), kind=kOutput, calls=%fused_computation.24 | convolution fusion | flops 2415919104 | bytes 10616832 | tf_op jit(solution)/shard_map/dot_general | solution.py:24
  125.5 63.4 %all-to-all-done = bf16[128,24,1024]{2,1,0:T(8,128)(2,1)} async-done(((bf16[128,24,1024]{2,1,0:T(8,128)(2,1)}), bf16[128,24,1024]{2,1,0:T(8,128)(2,1)}, u32[]{:S(2)}, u32[]{:S(2)}) %all-to-all-start) | async-done | bytes 6291488 | tf_op jit(solution)/shard_map/all_to_all | solution.py:637
  188.9 20.9 %expert_back.1 = (bf16[3072,1024]{1,0:T(8,128)(2,1)}, bf16[768,4096]{1,0:T(8,128)(2,1)}, bf16[768,384]{1,0:T(8,128)(2,1)}, bf16[768,384]{1,0:T(8,128)(2,1)}, bf16[768,384]{1,0:T(8,128)(2,1)}, /*index=5*/f32[768,1]{1,0:T(8,128)}) custom-call(bf16[3072,1024]{1,0:T(8,128)(2,1)} %bitcast.4.raw_ref, f32[768,384]{1,0:T(8,128)} %fusion.10.gate_ref, ...), custom_call_target="tpu_custom_call" | custom-call | flops 9663676416 | bytes 33554432 | tf_op jit(solution)/shard_map/expert_back/pallas_call | solution.py:195
  209.8 10.8 %all-to-all-start.2 = ((bf16[128,24,1024]{2,1,0:T(8,128)(2,1)}), bf16[128,24,1024]{2,1,0:T(8,128)(2,1)}, u32[]{:S(2)}, u32[]{:S(2)}) async-start(bf16[128,24,1024]{2,1,0:T(8,128)(2,1)} %bitcast.52), calls=%async_computation.2 | async-start | bytes 12582912 | tf_op jit(solution)/shard_map/all_to_all | solution.py:644
  221.0 0.6 reduce-window.6
  222.4 0.6 pad.5.dots_ref
  223.1 7.3 %fusion.2 = bf16[1,384,4096]{2,1,0:T(8,128)(2,1)} fusion(bf16[768,384]{1,0:T(8,128)(2,1)S(1)} %copy-done.1, bf16[768,4096]{1,0:T(8,128)(2,1)} %get-tuple-element.24), kind=kOutput, calls=%fused_computation.5 | convolution fusion | flops 2417491968 | bytes 10027008 | tf_op jit(solution)/shard_map/dot_general | solution.py:24
  230.4 4.9 %fusion.1 = bf16[1,4096,384]{2,1,0:T(8,128)(2,1)} fusion(bf16[768,4096]{1,0:T(8,128)(2,1)S(1)} %bitcast.49, bf16[768,384]{1,0:T(8,128)(2,1)S(1)} %copy-done.9), kind=kOutput, calls=%fused_computation.4 | convolution fusion | flops 2417491968 | bytes 10027008 | tf_op jit(solution)/shard_map/dot_general | solution.py:24
  235.2 4.8 %fusion = bf16[1,4096,384]{2,1,0:T(8,128)(2,1)} fusion(bf16[768,4096]{1,0:T(8,128)(2,1)S(1)} %bitcast.49, bf16[768,384]{1,0:T(8,128)(2,1)S(1)} %copy-done.8), kind=kOutput, calls=%fused_computation.3 | convolution fusion | flops 2417491968 | bytes 10027008 | tf_op jit(solution)/shard_map/dot_general | solution.py:24
  240.0 59.7 %all-to-all-done.2 = bf16[128,24,1024]{2,1,0:T(8,128)(2,1)} async-done(((bf16[128,24,1024]{2,1,0:T(8,128)(2,1)}), bf16[128,24,1024]{2,1,0:T(8,128)(2,1)}, u32[]{:S(2)}, u32[]{:S(2)}) %all-to-all-start.2) | async-done | bytes 6291488 | tf_op jit(solution)/shard_map/all_to_all | solution.py:644
  299.8 9.1 %combine.1.resid_ref = bf16[128,4096]{1,0:T(8,128)(2,1)} custom-call(s32[128,2]{1,0:T(8,128)} %copy-done.2, bf16[3072,1024]{1,0:T(8,128)(2,1)} %bitcast.11.back_ref, bf16[128,4096]{1,0:T(8,128)(2,1)} %hidden_ref.1, f32[1,4096]{1,0:T(1,128)} %bitcast.55, bf16[128,4096]{1,0:T(8,128)(2,1)} %cot_ref.1), custom_call_target="tpu_custom_call" | custom-call | flops 3221225472 | bytes 12582912 | tf_op jit(solution)/shard_map/combine/pallas_call | solution.py:269
  308.8 92.9 %project.1 = (bf16[1024,512]{1,0:T(8,128)(2,1)}, bf16[256,512]{1,0:T(8,128)(2,1)}, f32[16,256]{1,0:T(8,128)}) custom-call(bf16[128,4096]{1,0:T(8,128)(2,1)} %combine.1.resid_ref, bf16[1024,512]{1,0:T(8,128)(2,1)} %heads_ref.1, bf16[256,512]{1,0:T(8,128)(2,1)} %weight_ref.1, bf16[16,128]{1,0:T(8,128)(2,1)} %pad.5.dots_ref), custom_call_target="tpu_custom_call" | custom-call | flops 8589934592 | bytes 8388608 | tf_op jit(solution)/shard_map/project/pallas_call | solution.py:578
  401.7 0.7 slice_bitcast_fusion
  403.0 0.6 convert_divide_fusion
  403.6 2.3 copy.29
  405.9 1.7 copy.30
  (41 shorter events, 1.8 us)
Async XLA Ops:
  8.4 11.6 %copy-start.5 = (f32[128,2]{0,1:T(2,128)S(1)}, f32[128,2]{0,1:T(2,128)}, u32[]{:S(2)}) copy-start(f32[128,2]{0,1:T(2,128)} %param.15) | copy-start | bytes 3076
  8.4 91.0 %all-to-all-start.1 = ((bf16[128,24,1024]{2,1,0:T(8,128)(2,1)}), bf16[128,24,1024]{2,1,0:T(8,128)(2,1)}, u32[]{:S(2)}, u32[]{:S(2)}) async-start(bf16[128,24,1024]{2,1,0:T(8,128)(2,1)} %bitcast.51), calls=%async_computation.1 | async-start | bytes 12582912 | tf_op jit(solution)/shard_map/all_to_all | solution.py:636
  99.4 89.5 %all-to-all-start = ((bf16[128,24,1024]{2,1,0:T(8,128)(2,1)}), bf16[128,24,1024]{2,1,0:T(8,128)(2,1)}, u32[]{:S(2)}, u32[]{:S(2)}) async-start(bf16[128,24,1024]{2,1,0:T(8,128)(2,1)} %bitcast.50), calls=%async_computation | async-start | bytes 12582912 | tf_op jit(solution)/shard_map/all_to_all | solution.py:637
  109.7 6.9 %copy-start.6 = (bf16[1,4096,384]{2,1,0:T(8,128)(2,1)S(1)}, bf16[1,4096,384]{2,1,0:T(8,128)(2,1)}, u32[]{:S(2)}) copy-start(bf16[1,4096,384]{2,1,0:T(8,128)(2,1)} %param.16) | copy-start | bytes 9437188
  116.6 4.4 %copy-start = (bf16[768,4096]{1,0:T(8,128)(2,1)}, bf16[768,4096]{1,0:T(8,128)(2,1)S(1)}, u32[]{:S(2)}) copy-start(bf16[768,4096]{1,0:T(8,128)(2,1)S(1)} %unpack.1) | copy-start | bytes 18874372
  116.6 4.4 %copy-start.7 = (bf16[1,4096,384]{2,1,0:T(8,128)(2,1)S(1)}, bf16[1,4096,384]{2,1,0:T(8,128)(2,1)}, u32[]{:S(2)}) copy-start(bf16[1,4096,384]{2,1,0:T(8,128)(2,1)} %param.17) | copy-start | bytes 9437188
  209.8 10.8 %copy-start.4 = (s32[128,2]{0,1:T(2,128)S(1)}, s32[128,2]{0,1:T(2,128)}, u32[]{:S(2)}) copy-start(s32[128,2]{0,1:T(2,128)} %param.14) | copy-start | bytes 3076
  209.8 12.2 %copy-start.3 = (f32[768,1]{1,0:T(8,128)S(1)}, f32[768,1]{1,0:T(8,128)}, u32[]{:S(2)}) copy-start(f32[768,1]{1,0:T(8,128)} %get-tuple-element.17) | copy-start | bytes 9220
  209.8 13.2 %copy-start.1 = (bf16[768,384]{1,0:T(8,128)(2,1)S(1)}, bf16[768,384]{1,0:T(8,128)(2,1)}, u32[]{:S(2)}) copy-start(bf16[768,384]{1,0:T(8,128)(2,1)} %get-tuple-element.23) | copy-start | bytes 1769476
  209.8 89.9 %all-to-all-start.2 = ((bf16[128,24,1024]{2,1,0:T(8,128)(2,1)}), bf16[128,24,1024]{2,1,0:T(8,128)(2,1)}, u32[]{:S(2)}, u32[]{:S(2)}) async-start(bf16[128,24,1024]{2,1,0:T(8,128)(2,1)} %bitcast.52), calls=%async_computation.2 | async-start | bytes 12582912 | tf_op jit(solution)/shard_map/all_to_all | solution.py:644
  220.7 9.6 %copy-start.2 = (s32[128,2]{1,0:T(8,128)}, s32[128,2]{1,0:T(8,128)S(1)}, u32[]{:S(2)}) copy-start(s32[128,2]{1,0:T(8,128)S(1)} %copy.18.ids_ref) | copy-start | bytes 3076
  222.2 8.1 %slice-start = ((s8[6291456]{0:T(1024)(128)(4,1)}), s8[2097152]{0:T(1024)(128)(4,1)S(1)}, s32[]{:S(2)}) async-start(s8[6291456]{0:T(1024)(128)(4,1)} %bitcast.48), calls=%async_computation.3 | async-start | bytes 4194304
  222.2 8.1 %copy-start.9 = (bf16[768,384]{1,0:T(8,128)(2,1)S(1)}, bf16[768,384]{1,0:T(8,128)(2,1)}, u32[]{:S(2)}) copy-start(bf16[768,384]{1,0:T(8,128)(2,1)} %get-tuple-element.22) | copy-start | bytes 1769476
  223.1 7.3 %slice-start.1 = ((s8[6291456]{0:T(1024)(128)(4,1)}), s8[4194304]{0:T(1024)(128)(4,1)S(1)}, s32[]{:S(2)}) async-start(s8[6291456]{0:T(1024)(128)(4,1)} %bitcast.48), calls=%async_computation.4 | async-start | bytes 8388608
  230.3 4.9 %copy-start.8 = (bf16[768,384]{1,0:T(8,128)(2,1)S(1)}, bf16[768,384]{1,0:T(8,128)(2,1)}, u32[]{:S(2)}) copy-start(bf16[768,384]{1,0:T(8,128)(2,1)} %get-tuple-element.21) | copy-start | bytes 1769476

commit v8 on v7

--- a/solution.py
+++ b/solution.py
@@ -353,9 +353,12 @@
 
     def start_own(i):
         fetch(i).wait()
+        if i % 2 == 0:
+            send(i, tp, whole, TO_Z, FAR_C, far)
         send(i, tp, whole, TO_R, SAME_L, right)
         send(i, tp, whole, TO_L, SAME_R, left)
-        send(i, tp, whole, TO_Z, FAR_C, far)
+        if i % 2 == 1:
+            send(i, tp, whole, TO_Z, FAR_C, far)
 
     def send_block(p, zh, semaphore, lands, device):
         ref = blocks.at[p, zh, core]
@@ -530,9 +533,9 @@
     gather_dots()
     share_blocks(0)
     arrivals(0)
-    multiply(0, ((share_blocks, 1),))
+    multiply(0, ((first_hops, 2), (share_blocks, 1)))
     arrivals(1)
-    multiply(1, ((first_hops, 2), (first_hops, 3), (share_blocks, 2)))
+    multiply(1, ((first_hops, 3), (share_blocks, 2)))
     second_hops(2)
     second_hops(3)
     arrivals(2)

time: 408 us -> 405 us (level)
    pallas_call x1, Pallas kernels: 92.9 us -> 88.6 us  [project(): pl.pallas_call(project_kernel, in_specs=[anywhere, anywhere, vmem, vmem],...]
where the time goes in v8:
time: 405 us; the launch traced here: 403 us
  waiting for transfers between devices  194 us (48%)
  Pallas kernels  141 us (35%)
  starting transfers between devices  32.7 us (8%)
  matrix products  26 us (6%)
  local copies, waits for them, and re-layouts  6.45 us (2%)
    pallas_call x1, Pallas kernels, project(): pl.pallas_call(project_kernel, in_specs=[anywhere, anywhere, vmem, vmem],...  88.6 us
    all_to_all x1, waiting for transfers between devices, per_device(): exchange(send_rows.reshape(devices, CHUNK, width)).reshape(-1, width)  71.2 us
    all_to_all x1, waiting for transfers between devices, per_device(): exchange(send_cots.reshape(devices, CHUNK, width)).reshape(-1, width)  63.4 us
    all_to_all x1, waiting for transfers between devices, per_device(): back = exchange(grads.reshape(devices, CHUNK, width)).reshape(-1, width)  59.7 us
    dot_general x5, matrix products, mm(): return lax.dot_general(a, b, dims, preferred_element_type=jnp.float32)  25.8 us
    pallas_call x1, Pallas kernels, expert_back(): pl.pallas_call(back_kernel, grid=(steps,), in_specs=[tall((total // steps...  20.9 us
    pallas_call x2, Pallas kernels, dispatch(): pl.pallas_call(functools.partial(dispatch_kernel, normalize), grid=(exper...  15.4 us
    all_to_all x1, starting transfers between devices, per_device(): exchange(send_rows.reshape(devices, CHUNK, width)).reshape(-1, width)  11.6 us
  transfers between devices with their start and end apart: 3, of which 3 were waited for; matrix products, arithmetic and copies ran while one was open for 7% of the time, Pallas kernels for 4%

profile of v8, /device:TPU:0, one launch (start us, length us, event | category | flops | bytes accessed | tf_op | source)
XLA Modules:
  0.0 403.3 jit_solution(14026902296000356872)
XLA Ops:
  0.6 7.8 %dispatch_rows.1 = bf16[64,2,24,1024]{3,2,1,0:T(8,128)(2,1)} custom-call(s32[2,128]{1,0:T(2,128)} %bitcast.56, s32[2,128]{1,0:T(2,128)} %bitcast.57, bf16[128,4096]{1,0:T(8,128)(2,1)} %hidden_ref.1, f32[1,4096]{1,0:T(1,128)} %bitcast.53), custom_call_target="tpu_custom_call" | custom-call | flops 1610612736 | bytes 8388608 | tf_op jit(solution)/shard_map/dispatch_rows/pallas_call | solution.py:83
  8.4 11.6 %all-to-all-start.1 = ((bf16[128,24,1024]{2,1,0:T(8,128)(2,1)}), bf16[128,24,1024]{2,1,0:T(8,128)(2,1)}, u32[]{:S(2)}, u32[]{:S(2)}) async-start(bf16[128,24,1024]{2,1,0:T(8,128)(2,1)} %bitcast.51), calls=%async_computation.1 | async-start | bytes 12582912 | tf_op jit(solution)/shard_map/all_to_all | solution.py:639
  20.0 0.6 convert_bitcast_fusion.weight_ref
  20.6 7.6 %dispatch_cots.1 = bf16[64,2,24,1024]{3,2,1,0:T(8,128)(2,1)} custom-call(s32[2,128]{1,0:T(2,128)} %bitcast.58, f32[2,128]{1,0:T(2,128)} %convert_bitcast_fusion.weight_ref, bf16[128,4096]{1,0:T(8,128)(2,1)} %cot_ref.1, f32[1,4096]{1,0:T(1,128)} %bitcast.54), custom_call_target="tpu_custom_call" | custom-call | flops 1610612736 | bytes 8388608 | tf_op jit(solution)/shard_map/dispatch_cots/pallas_call | solution.py:83
  28.2 71.2 %all-to-all-done.1 = bf16[128,24,1024]{2,1,0:T(8,128)(2,1)} async-done(((bf16[128,24,1024]{2,1,0:T(8,128)(2,1)}), bf16[128,24,1024]{2,1,0:T(8,128)(2,1)}, u32[]{:S(2)}, u32[]{:S(2)}) %all-to-all-start.1) | async-done | bytes 6291488 | tf_op jit(solution)/shard_map/all_to_all | solution.py:639
  99.4 10.3 %all-to-all-start = ((bf16[128,24,1024]{2,1,0:T(8,128)(2,1)}), bf16[128,24,1024]{2,1,0:T(8,128)(2,1)}, u32[]{:S(2)}, u32[]{:S(2)}) async-start(bf16[128,24,1024]{2,1,0:T(8,128)(2,1)} %bitcast.50), calls=%async_computation | async-start | bytes 12582912 | tf_op jit(solution)/shard_map/all_to_all | solution.py:640
  109.8 6.8 %unpack.1 = bf16[768,4096]{1,0:T(8,128)(2,1)S(1)} custom-call(bf16[3072,1024]{1,0:T(8,128)(2,1)} %bitcast.6.raw_ref), custom_call_target="tpu_custom_call" | custom-call | flops 1207959552 | bytes 12582912 | tf_op jit(solution)/shard_map/unpack/pallas_call | solution.py:137
  116.6 4.4 %fusion.10.gate_ref = f32[768,384]{1,0:T(8,128)} fusion(bf16[768,4096]{1,0:T(8,128)(2,1)S(1)} %unpack.1, bf16[1,4096,384]{2,1,0:T(8,128)(2,1)S(1)} %copy-done.6), kind=kOutput, calls=%fused_computation.26 | convolution fusion | flops 2415919104 | bytes 10616832 | tf_op jit(solution)/shard_map/dot_general | solution.py:24
  121.1 4.4 %fusion.8.up_ref = f32[768,384]{1,0:T(8,128)} fusion(bf16[768,4096]{1,0:T(8,128)(2,1)S(1)} %unpack.1, bf16[1,4096,384]{2,1,0:T(8,128)(2,1)S(1)} %copy-done.7), kind=kOutput, calls=%fused_computation.24 | convolution fusion | flops 2415919104 | bytes 10616832 | tf_op jit(solution)/shard_map/dot_general | solution.py:24
  125.5 63.4 %all-to-all-done = bf16[128,24,1024]{2,1,0:T(8,128)(2,1)} async-done(((bf16[128,24,1024]{2,1,0:T(8,128)(2,1)}), bf16[128,24,1024]{2,1,0:T(8,128)(2,1)}, u32[]{:S(2)}, u32[]{:S(2)}) %all-to-all-start) | async-done | bytes 6291488 | tf_op jit(solution)/shard_map/all_to_all | solution.py:640
  188.9 20.9 %expert_back.1 = (bf16[3072,1024]{1,0:T(8,128)(2,1)}, bf16[768,4096]{1,0:T(8,128)(2,1)}, bf16[768,384]{1,0:T(8,128)(2,1)}, bf16[768,384]{1,0:T(8,128)(2,1)}, bf16[768,384]{1,0:T(8,128)(2,1)}, /*index=5*/f32[768,1]{1,0:T(8,128)}) custom-call(bf16[3072,1024]{1,0:T(8,128)(2,1)} %bitcast.4.raw_ref, f32[768,384]{1,0:T(8,128)} %fusion.10.gate_ref, ...), custom_call_target="tpu_custom_call" | custom-call | flops 9663676416 | bytes 33554432 | tf_op jit(solution)/shard_map/expert_back/pallas_call | solution.py:195
  209.8 10.8 %all-to-all-start.2 = ((bf16[128,24,1024]{2,1,0:T(8,128)(2,1)}), bf16[128,24,1024]{2,1,0:T(8,128)(2,1)}, u32[]{:S(2)}, u32[]{:S(2)}) async-start(bf16[128,24,1024]{2,1,0:T(8,128)(2,1)} %bitcast.52), calls=%async_computation.2 | async-start | bytes 12582912 | tf_op jit(solution)/shard_map/all_to_all | solution.py:647
  221.0 0.6 reduce-window.6
  222.4 0.6 pad.5.dots_ref
  223.1 7.3 %fusion.2 = bf16[1,384,4096]{2,1,0:T(8,128)(2,1)} fusion(bf16[768,384]{1,0:T(8,128)(2,1)S(1)} %copy-done.1, bf16[768,4096]{1,0:T(8,128)(2,1)} %get-tuple-element.24), kind=kOutput, calls=%fused_computation.5 | convolution fusion | flops 2417491968 | bytes 10027008 | tf_op jit(solution)/shard_map/dot_general | solution.py:24
  230.4 4.9 %fusion.1 = bf16[1,4096,384]{2,1,0:T(8,128)(2,1)} fusion(bf16[768,4096]{1,0:T(8,128)(2,1)S(1)} %bitcast.49, bf16[768,384]{1,0:T(8,128)(2,1)S(1)} %copy-done.9), kind=kOutput, calls=%fused_computation.4 | convolution fusion | flops 2417491968 | bytes 10027008 | tf_op jit(solution)/shard_map/dot_general | solution.py:24
  235.2 4.8 %fusion = bf16[1,4096,384]{2,1,0:T(8,128)(2,1)} fusion(bf16[768,4096]{1,0:T(8,128)(2,1)S(1)} %bitcast.49, bf16[768,384]{1,0:T(8,128)(2,1)S(1)} %copy-done.8), kind=kOutput, calls=%fused_computation.3 | convolution fusion | flops 2417491968 | bytes 10027008 | tf_op jit(solution)/shard_map/dot_general | solution.py:24
  240.0 59.7 %all-to-all-done.2 = bf16[128,24,1024]{2,1,0:T(8,128)(2,1)} async-done(((bf16[128,24,1024]{2,1,0:T(8,128)(2,1)}), bf16[128,24,1024]{2,1,0:T(8,128)(2,1)}, u32[]{:S(2)}, u32[]{:S(2)}) %all-to-all-start.2) | async-done | bytes 6291488 | tf_op jit(solution)/shard_map/all_to_all | solution.py:647
  299.8 9.1 %combine.1.resid_ref = bf16[128,4096]{1,0:T(8,128)(2,1)} custom-call(s32[128,2]{1,0:T(8,128)} %copy-done.2, bf16[3072,1024]{1,0:T(8,128)(2,1)} %bitcast.11.back_ref, bf16[128,4096]{1,0:T(8,128)(2,1)} %hidden_ref.1, f32[1,4096]{1,0:T(1,128)} %bitcast.55, bf16[128,4096]{1,0:T(8,128)(2,1)} %cot_ref.1), custom_call_target="tpu_custom_call" | custom-call | flops 3221225472 | bytes 12582912 | tf_op jit(solution)/shard_map/combine/pallas_call | solution.py:269
  308.8 88.6 %project.1 = (bf16[1024,512]{1,0:T(8,128)(2,1)}, bf16[256,512]{1,0:T(8,128)(2,1)}, f32[16,256]{1,0:T(8,128)}) custom-call(bf16[128,4096]{1,0:T(8,128)(2,1)} %combine.1.resid_ref, bf16[1024,512]{1,0:T(8,128)(2,1)} %heads_ref.1, bf16[256,512]{1,0:T(8,128)(2,1)} %weight_ref.1, bf16[16,128]{1,0:T(8,128)(2,1)} %pad.5.dots_ref), custom_call_target="tpu_custom_call" | custom-call | flops 8589934592 | bytes 8388608 | tf_op jit(solution)/shard_map/project/pallas_call | solution.py:581
  397.4 0.7 slice_bitcast_fusion
  398.7 0.6 convert_divide_fusion
  399.3 2.3 copy.29
  401.6 1.7 copy.30
  (41 shorter events, 1.8 us)
Async XLA Ops:
  8.4 11.6 %copy-start.5 = (f32[128,2]{0,1:T(2,128)S(1)}, f32[128,2]{0,1:T(2,128)}, u32[]{:S(2)}) copy-start(f32[128,2]{0,1:T(2,128)} %param.15) | copy-start | bytes 3076
  8.4 91.0 %all-to-all-start.1 = ((bf16[128,24,1024]{2,1,0:T(8,128)(2,1)}), bf16[128,24,1024]{2,1,0:T(8,128)(2,1)}, u32[]{:S(2)}, u32[]{:S(2)}) async-start(bf16[128,24,1024]{2,1,0:T(8,128)(2,1)} %bitcast.51), calls=%async_computation.1 | async-start | bytes 12582912 | tf_op jit(solution)/shard_map/all_to_all | solution.py:639
  99.4 89.5 %all-to-all-start = ((bf16[128,24,1024]{2,1,0:T(8,128)(2,1)}), bf16[128,24,1024]{2,1,0:T(8,128)(2,1)}, u32[]{:S(2)}, u32[]{:S(2)}) async-start(bf16[128,24,1024]{2,1,0:T(8,128)(2,1)} %bitcast.50), calls=%async_computation | async-start | bytes 12582912 | tf_op jit(solution)/shard_map/all_to_all | solution.py:640
  109.7 6.9 %copy-start.6 = (bf16[1,4096,384]{2,1,0:T(8,128)(2,1)S(1)}, bf16[1,4096,384]{2,1,0:T(8,128)(2,1)}, u32[]{:S(2)}) copy-start(bf16[1,4096,384]{2,1,0:T(8,128)(2,1)} %param.16) | copy-start | bytes 9437188
  116.6 4.4 %copy-start = (bf16[768,4096]{1,0:T(8,128)(2,1)}, bf16[768,4096]{1,0:T(8,128)(2,1)S(1)}, u32[]{:S(2)}) copy-start(bf16[768,4096]{1,0:T(8,128)(2,1)S(1)} %unpack.1) | copy-start | bytes 18874372
  116.6 4.4 %copy-start.7 = (bf16[1,4096,384]{2,1,0:T(8,128)(2,1)S(1)}, bf16[1,4096,384]{2,1,0:T(8,128)(2,1)}, u32[]{:S(2)}) copy-start(bf16[1,4096,384]{2,1,0:T(8,128)(2,1)} %param.17) | copy-start | bytes 9437188
  209.8 10.8 %copy-start.4 = (s32[128,2]{0,1:T(2,128)S(1)}, s32[128,2]{0,1:T(2,128)}, u32[]{:S(2)}) copy-start(s32[128,2]{0,1:T(2,128)} %param.14) | copy-start | bytes 3076
  209.8 12.2 %copy-start.3 = (f32[768,1]{1,0:T(8,128)S(1)}, f32[768,1]{1,0:T(8,128)}, u32[]{:S(2)}) copy-start(f32[768,1]{1,0:T(8,128)} %get-tuple-element.17) | copy-start | bytes 9220
  209.8 13.2 %copy-start.1 = (bf16[768,384]{1,0:T(8,128)(2,1)S(1)}, bf16[768,384]{1,0:T(8,128)(2,1)}, u32[]{:S(2)}) copy-start(bf16[768,384]{1,0:T(8,128)(2,1)} %get-tuple-element.23) | copy-start | bytes 1769476
  209.8 89.9 %all-to-all-start.2 = ((bf16[128,24,1024]{2,1,0:T(8,128)(2,1)}), bf16[128,24,1024]{2,1,0:T(8,128)(2,1)}, u32[]{:S(2)}, u32[]{:S(2)}) async-start(bf16[128,24,1024]{2,1,0:T(8,128)(2,1)} %bitcast.52), calls=%async_computation.2 | async-start | bytes 12582912 | tf_op jit(solution)/shard_map/all_to_all | solution.py:647
  220.7 9.6 %copy-start.2 = (s32[128,2]{1,0:T(8,128)}, s32[128,2]{1,0:T(8,128)S(1)}, u32[]{:S(2)}) copy-start(s32[128,2]{1,0:T(8,128)S(1)} %copy.18.ids_ref) | copy-start | bytes 3076
  222.2 8.1 %slice-start = ((s8[6291456]{0:T(1024)(128)(4,1)}), s8[2097152]{0:T(1024)(128)(4,1)S(1)}, s32[]{:S(2)}) async-start(s8[6291456]{0:T(1024)(128)(4,1)} %bitcast.48), calls=%async_computation.3 | async-start | bytes 4194304
  222.2 8.1 %copy-start.9 = (bf16[768,384]{1,0:T(8,128)(2,1)S(1)}, bf16[768,384]{1,0:T(8,128)(2,1)}, u32[]{:S(2)}) copy-start(bf16[768,384]{1,0:T(8,128)(2,1)} %get-tuple-element.22) | copy-start | bytes 1769476
  223.1 7.3 %slice-start.1 = ((s8[6291456]{0:T(1024)(128)(4,1)}), s8[4194304]{0:T(1024)(128)(4,1)S(1)}, s32[]{:S(2)}) async-start(s8[6291456]{0:T(1024)(128)(4,1)} %bitcast.48), calls=%async_computation.4 | async-start | bytes 8388608
  230.3 4.9 %copy-start.8 = (bf16[768,384]{1,0:T(8,128)(2,1)S(1)}, bf16[768,384]{1,0:T(8,128)(2,1)}, u32[]{:S(2)}) copy-start(bf16[768,384]{1,0:T(8,128)(2,1)} %get-tuple-element.21) | copy-start | bytes 1769476
